TPU v7x, 32 devices: a whole 2x2x4 slice. The times are simulated.
32 devices in a mesh: blk: 4 (over x, core), dom: 8 (over z, y).
Axes of the slice: x: 2, y: 2, z: 4, core: 2. Of those that a mesh axis runs over, the one named last changes fastest.
Arguments:
- nodes: bfloat16 [4096, 512], P(('blk', 'dom')), may hold values from -6 to 6
- experts_list: int32 [32, 1], P(('blk', 'dom')), may hold values from 0 to 3
- w_query: bfloat16 [512, 512], replicated
- w_key: bfloat16 [512, 512], replicated
- w_value: bfloat16 [512, 512], replicated, may hold values from -0.25 to 0.25
- w_out: bfloat16 [512, 512], replicated, may hold values from -0.25 to 0.25
- w_up: bfloat16 [512, 1024], replicated, may hold values from -0.25 to 0.25
- w_down: bfloat16 [1024, 512], replicated, may hold values from -0.1875 to 0.1875
- cotangent: bfloat16 [4096, 512], P(('blk', 'dom')), may hold values from -6 to 6
Outputs:
- layer_out: bfloat16 [4096, 512], P(('blk', 'dom'))
- grad_nodes: bfloat16 [4096, 512], P(('blk', 'dom'))
Inputs may be any that keep to these rules, and one draw needn't show every extreme that they name: `experts_list`: row g names 1 different values; value c stands for the block held at blk index c and the same dom index as block g. Every value is named by some row.
All inputs are finite; a program needn't handle non-finite values.
Results may differ from a plain program's by a relative error of at most 0.0057.
Values may be sent and summed in bfloat16 or wider, within the bound.
No kernel may reach another device: no remote copies, remote signals or barrier semaphores. Data moves between devices by JAX's collectives and lax.ppermute only.
A program may use at most 128 MiB of HBM per device.

v0:
```python
import jax
import jax.numpy as jnp
from jax import lax
from jax.sharding import PartitionSpec as P

H = 8
HEAD = 64


EPS = 1e-05
NEG = -1e30


def with_halo(array, sides, width):
    for axis, dim in sides:
        devices, length = (lax.axis_size(axis), array.shape[dim])
        up = [(i, (i + 1) % devices) for i in range(devices)]
        down = [(j, i) for i, j in up]
        last = lax.slice_in_dim(array, length - width, length, axis=dim)
        leading = lax.slice_in_dim(array, 0, width, axis=dim)
        before = lax.ppermute(last, axis, up)
        after = lax.ppermute(leading, axis, down)
        array = jnp.concatenate([before, array, after], axis=dim)
    return array


def shifted(array, axis, by):
    devices = lax.axis_size(axis)
    return lax.ppermute(array, axis, [(i, (i + by) % devices) for i in range(devices)])


def normalize(values):
    mean_v = jnp.mean(values, axis=-1, keepdims=True)
    centered = values - mean_v
    inv_std = lax.rsqrt(jnp.mean(centered * centered, axis=-1, keepdims=True) + EPS)
    return (centered * inv_std, inv_std)


def normalize_back(values, upstream):
    unit, inv_std = normalize(values)
    return inv_std * (
        upstream
        - jnp.mean(upstream, axis=-1, keepdims=True)
        - unit * jnp.mean(upstream * unit, axis=-1, keepdims=True)
    )


def heads_of(rows):
    return rows.reshape(rows.shape[0], H, HEAD)


def attend(queries, keyvals):
    width = queries.shape[1]
    scale = HEAD ** (-0.5)
    qh = heads_of(queries)
    kh = heads_of(keyvals[:, :width])
    vh = heads_of(keyvals[:, width:])
    scores = jnp.einsum("qhd,khd->hqk", qh, kh, preferred_element_type=jnp.float32) * scale
    top = jnp.max(scores, axis=-1, keepdims=True)
    weights = jnp.exp(scores - top)
    total = jnp.sum(weights, axis=-1, keepdims=True)
    mixed = jnp.einsum(
        "hqk,khd->qhd", weights.astype(jnp.bfloat16), vh, preferred_element_type=jnp.float32
    )
    mixed = mixed / jnp.transpose(total, (1, 0, 2))
    lse = (top + jnp.log(total))[..., 0]
    return (mixed.reshape(queries.shape[0], width).astype(jnp.bfloat16), lse)


def attend_back(queries, keyvals, grad_out, lse, delta, qmult):
    width = queries.shape[1]
    scale = HEAD ** (-0.5)
    qh = heads_of(queries)
    kh = heads_of(keyvals[:, :width])
    vh = heads_of(keyvals[:, width:])
    gh = heads_of(grad_out)
    scores = jnp.einsum("qhd,khd->hqk", qh, kh, preferred_element_type=jnp.float32) * scale
    valid = qmult[None, :, None] > 0
    scores = jnp.where(valid, scores, NEG)
    probs = jnp.exp(scores - lse[..., None]) * qmult[None, :, None]
    grad_v = jnp.einsum(
        "hqk,qhd->khd", probs.astype(jnp.bfloat16), gh, preferred_element_type=jnp.float32
    )
    dprob = jnp.einsum("qhd,khd->hqk", gh, vh, preferred_element_type=jnp.float32)
    dscore = (probs * (dprob - delta[..., None]) * scale).astype(jnp.bfloat16)
    grad_q = jnp.einsum("hqk,khd->qhd", dscore, kh, preferred_element_type=jnp.float32)
    grad_k = jnp.einsum("hqk,qhd->khd", dscore, qh, preferred_element_type=jnp.float32)
    count = keyvals.shape[0]
    return (
        grad_q.reshape(queries.shape[0], width),
        jnp.concatenate([grad_k.reshape(count, width), grad_v.reshape(count, width)], 1),
    )


def on_device(nodes, experts_list, w_query, w_key, w_value, w_out, w_up, w_down, cotangent):
    f32 = jnp.float32
    bf16 = jnp.bfloat16
    rows, width = nodes.shape
    groups = lax.axis_size("blk")
    place = lax.axis_index("blk")
    x_full = nodes.astype(f32)
    unit, _ = normalize(x_full)
    normed = unit.astype(bf16)
    queries = jnp.dot(normed, w_query, preferred_element_type=f32).astype(bf16)
    keys = jnp.dot(normed, w_key, preferred_element_type=f32).astype(bf16)
    values = jnp.dot(normed, w_value, preferred_element_type=f32).astype(bf16)
    keyvals = jnp.concatenate([keys, values], 1)
    window = with_halo(keyvals, (("dom", 0),), rows)
    panels = lax.all_gather(keyvals, "blk", axis=0, tiled=True)
    listed = experts_list[0]
    listed_count = listed.shape[0]
    chosen = jnp.take(panels.reshape(groups, rows, 2 * width), listed, axis=0)
    all_keys = jnp.concatenate([window, chosen.reshape(listed_count * rows, 2 * width)], 0)
    mixed, lse = attend(queries, all_keys)
    resid = x_full + jnp.dot(mixed, w_out, preferred_element_type=f32)
    unit2, _ = normalize(resid)
    normed2 = unit2.astype(bf16)
    pre = jnp.dot(normed2, w_up, preferred_element_type=f32)
    act, gelu_back = jax.vjp(jax.nn.gelu, pre)
    layer_out = (resid + jnp.dot(act.astype(bf16), w_down, preferred_element_type=f32)).astype(bf16)
    grad_act = jnp.dot(cotangent, w_down.T, preferred_element_type=f32)
    grad_pre = gelu_back(grad_act)[0].astype(bf16)
    grad_norm2 = jnp.dot(grad_pre, w_up.T, preferred_element_type=f32)
    grad_resid = cotangent.astype(f32) + normalize_back(resid, grad_norm2)
    grad_mixed = jnp.dot(grad_resid.astype(bf16), w_out.T, preferred_element_type=f32).astype(bf16)
    delta = jnp.sum(heads_of(grad_mixed).astype(f32) * heads_of(mixed).astype(f32), axis=-1).T
    ones_rows = jnp.ones((rows,), f32)
    grad_q, grad_kv = attend_back(queries, all_keys, grad_mixed, lse, delta, ones_rows)
    from_upper = shifted(grad_kv[:rows].astype(jnp.bfloat16), "dom", -1).astype(jnp.float32)
    from_lower = shifted(grad_kv[2 * rows : 3 * rows].astype(jnp.bfloat16), "dom", 1).astype(
        jnp.float32
    )
    own_grad = grad_kv[rows : 2 * rows] + from_upper + from_lower
    listed_parts = grad_kv[3 * rows :].reshape(listed_count, rows, 2 * width)
    onehot = (listed[:, None] == jnp.arange(groups, dtype=jnp.int32)[None, :]).astype(f32)
    far_parts = jnp.einsum("eg,erc->grc", onehot, listed_parts).reshape(groups * rows, 2 * width)

    def carry_step(step, running):
        running = shifted(running.astype(jnp.bfloat16), "blk", 1).astype(running.dtype)
        target = (place - step - 1) % groups
        return running + lax.dynamic_slice_in_dim(far_parts, target * rows, rows, 0)

    first = lax.dynamic_slice_in_dim(far_parts, (place - 1) % groups * rows, rows, 0)
    far_grad = lax.fori_loop(1, groups, carry_step, first)
    key_grad = own_grad + far_grad
    grad_in = (
        jnp.dot(grad_q.astype(bf16), w_query.T, preferred_element_type=f32)
        + jnp.dot(key_grad[:, :width].astype(bf16), w_key.T, preferred_element_type=f32)
        + jnp.dot(key_grad[:, width:].astype(bf16), w_value.T, preferred_element_type=f32)
    )
    grad_nodes = (grad_resid + normalize_back(x_full, grad_in)).astype(bf16)
    return (layer_out, grad_nodes)


def solution(mesh):
    return jax.shard_map(
        on_device,
        mesh=mesh,
        in_specs=(
            P(("blk", "dom"), None),
            P(("blk", "dom"), None),
            P(),
            P(),
            P(),
            P(),
            P(),
            P(),
            P(("blk", "dom"), None),
        ),
        out_specs=(P(("blk", "dom"), None), P(("blk", "dom"), None)),
        check_vma=False,
    )
```

profile of v0, /device:TPU:0, one launch (start us, length us, event | category | flops | bytes accessed | tf_op | source)
XLA Modules:
  0.0 102.1 jit_solution(2044202443709433844)
XLA Ops:
  7.2 1.1 %convert_reduce_fusion = f32[128]{0:T(128)S(1)} fusion(bf16[128,512]{1,0:T(8,128)(2,1)} %param.11), kind=kLoop, calls=%fused_computation.49 | loop fusion | flops 130944 | bytes 131584 | tf_op jit(solution)/shard_map/reduce_sum | solution.py:33
  9.5 1.4 %convolution_convert_fusion.2 = bf16[128,512]{1,0:T(8,128)(2,1)S(1)} fusion(bf16[512,512]{1,0:T(8,128)(2,1)} %param.15, bf16[128,512]{1,0:T(8,128)(2,1)} %param.11, f32[128]{0:T(128)S(1)} %add_rsqrt_fusion.1, f32[128]{0:T(128)S(1)} %broadcast_multiply_fusion.6), kind=kOutput, calls=%fused_computation.22 | convolution fusion | flops 67436544 | bytes 787456 | tf_op jit(solution)/shard_map/dot_general | solution.py:106
  10.9 1.4 %convolution_convert_fusion.3 = bf16[128,512]{1,0:T(8,128)(2,1)S(1)} fusion(bf16[512,512]{1,0:T(8,128)(2,1)} %param.14, bf16[128,512]{1,0:T(8,128)(2,1)} %param.11, f32[128]{0:T(128)S(1)} %add_rsqrt_fusion.1, f32[128]{0:T(128)S(1)} %broadcast_multiply_fusion.6), kind=kOutput, calls=%fused_computation.23 | convolution fusion | flops 67436544 | bytes 787456 | tf_op jit(solution)/shard_map/dot_general | solution.py:105
  13.0 6.1 %collective-permute-start.2 = (bf16[128,1024]{1,0:T(8,128)(2,1)}, bf16[128,1024]{1,0:T(8,128)(2,1)S(1)}, u32[]{:S(2)}, u32[]{:S(2)}) collective-permute-start(bf16[128,1024]{1,0:T(8,128)(2,1)} %pad_maximum_fusion.2), channel_id=1, source_target_pairs={{1,0},{2,1},{3,2},{4,3},{5,4},{6,5},{7,6},{0,7},{9,8},{10,9},{11,1... | collective-permute-start | bytes 786440 | tf_op jit(solution)/shard_map/ppermute | solution.py:22
  21.3 11.3 %all-gather.2.cloned.1.call-done = bf16[512,1024]{1,0:T(8,128)(2,1)} async-done(((bf16[128,1024]{1,0:T(8,128)(2,1)}), bf16[512,1024]{1,0:T(8,128)(2,1)}) %all-gather.2.cloned.1.call-update) | async-done | bytes 1048592 | tf_op jit(solution)/shard_map/all_gather | solution.py:109
  35.8 1.7 %fusion.68 = (f32[8,128]{1,0:T(8,128)S(1)}, f32[8,128,512]{2,1,0:T(8,128)S(1)}) fusion(bf16[128,8,64]{0,2,1:T(8,128)(2,1)} %bitcast.74, bf16[512,8,64]{0,2,1:T(8,128)(2,1)} %bitcast.66), kind=kOutput, calls=%fused_computation.106 | convolution fusion | flops 68156416 | bytes 2756608 | tf_op jit(solution)/shard_map/qhd,khd->hqk/dot_general | solution.py:58
  42.5 3.7 %fusion.65 = (f32[128]{0:T(128)}, f32[128]{0:T(128)}, f32[128,512]{1,0:T(8,128)}) fusion(f32[128]{0:T(128)} %copy-done.19, f32[128,512]{1,0:T(8,128)S(1)} %get-tuple-element.145, f32[128]{0:T(128)S(1)} %broadcast_multiply_fusion.5, bf16[512,1024]{1,0:T(8,128)(2,1)S(1)} %copy-done, f32[128,1024]{1,0:T(8,128)} %copy-done.16, bf16[128,512]{1,0:T(8,128)(2,1)} %param.19, ...), kind=kOutput, calls=%fused_computation.103 | convolution fusion | flops 271384320 | bytes 3278848 | tf_op jit(solution)/shard_map/dot_general | solution.py:123
  47.4 2.2 %convolution_convert_fusion = bf16[128,512]{1,0:T(8,128)(2,1)} fusion(bf16[512,512]{1,0:T(8,128)(2,1)} %param.16, f32[128,512]{1,0:T(8,128)} %get-tuple-element.146, bf16[128,512]{1,0:T(8,128)(2,1)} %param.19, f32[128,512]{1,0:T(8,128)S(1)} %get-tuple-element.145, f32[128]{0:T(128)S(1)} %get-tuple-element.148, f32[128]{0:T(128)S(1)} %get-tuple-element.149, ...), kind=kOutput, calls=%fused_computation.20 | convolution fusion | flops 67764224 | bytes 1312768 | tf_op jit(solution)/shard_map/dot_general | solution.py:125
  49.5 1.7 %copy.23 = bf16[128,512]{0,1:T(8,128)(2,1)} copy(bf16[128,512]{1,0:T(8,128)(2,1)} %convolution_convert_fusion) | data formatting | bytes 262144 | tf_op jit(solution)/shard_map/convert_element_type | solution.py:125
  52.3 1.8 %multiply_convert_fusion = bf16[8,128,512]{2,1,0:T(8,128)(2,1)S(1)} fusion(f32[8,128,512]{2,1,0:T(8,128)S(1)} %get-tuple-element.143, bf16[128,8,64]{0,2,1:T(8,128)(2,1)} %bitcast.72, bf16[512,8,64]{0,2,1:T(8,128)(2,1)} %bitcast.68, f32[8,128]{1,0:T(8,128)S(1)} %bitcast.80, f32[8,128]{1,0:T(8,128)S(1)} %log_add_fusion), kind=kOutput, calls=%fused_computation.7 | convolution fusion | flops 69730304 | bytes 3809280 | tf_op jit(solution)/shard_map/qhd,khd->hqk/dot_general | solution.py:84
  54.1 1.1 %convolution_convert_fusion.4 = bf16[8,64,128]{2,1,0:T(8,128)(2,1)} fusion(bf16[512,8,64]{0,2,1:T(8,128)(2,1)S(1)} %bitcast.67, bf16[8,128,512]{2,1,0:T(8,128)(2,1)S(1)} %multiply_convert_fusion), kind=kOutput, calls=%fused_computation.26 | convolution fusion | flops 67174400 | bytes 1703936 | tf_op jit(solution)/shard_map/hqk,khd->qhd/dot_general | solution.py:86
  55.3 1.3 %fusion.73 = f32[8,64,512]{2,1,0:T(8,128)} fusion(bf16[128,8,64]{0,2,1:T(8,128)(2,1)S(1)} %bitcast.75, bf16[8,128,512]{2,1,0:T(8,128)(2,1)S(1)} %multiply_convert_fusion), kind=kOutput, calls=%fused_computation.110 | convolution fusion | flops 67108864 | bytes 2228224 | tf_op jit(solution)/shard_map/hqk,qhd->khd/dot_general | solution.py:87
  56.5 1.6 %fusion.7 = f32[8,64,512]{2,1,0:T(8,128)} fusion(bf16[128,8,64]{0,2,1:T(8,128)(2,1)S(1)} %bitcast.73, f32[8,128,512]{2,1,0:T(8,128)S(1)} %get-tuple-element.143, f32[8,128]{1,0:T(8,128)S(1)} %log_add_fusion), kind=kOutput, calls=%fused_computation.27 | convolution fusion | flops 68157440 | bytes 3280896 | tf_op jit(solution)/shard_map/hqk,qhd->khd/dot_general | solution.py:81
  58.1 1.6 %copy.24 = f32[512,512]{1,0:T(8,128)S(1)} copy(f32[512,512]{0,1:T(8,128)} %bitcast.70) | data formatting | bytes 2097152 | tf_op jit(solution)/shard_map/reshape | solution.py:91
  59.7 1.6 %copy.25 = f32[512,512]{1,0:T(8,128)S(1)} copy(f32[512,512]{0,1:T(8,128)} %bitcast.71) | data formatting | bytes 2097152 | tf_op jit(solution)/shard_map/reshape | solution.py:91
  64.6 1.5 %collective-permute-start.4 = (bf16[128,1024]{1,0:T(8,128)(2,1)}, bf16[128,1024]{1,0:T(8,128)(2,1)}, u32[]{:S(2)}, u32[]{:S(2)}) collective-permute-start(bf16[128,1024]{1,0:T(8,128)(2,1)} %get-tuple-element.139), channel_id=1, source_target_pairs={{0,1},{1,2},{2,3},{3,4},{4,5},{5,6},{6,7},{7,0},{8,9},{9,10},{10,1... | collective-permute-start | bytes 786440 | tf_op jit(solution)/shard_map/ppermute | solution.py:29
  66.0 3.3 %collective-permute-start.3 = (bf16[128,1024]{1,0:T(8,128)(2,1)}, bf16[128,1024]{1,0:T(8,128)(2,1)}, u32[]{:S(2)}, u32[]{:S(2)}) collective-permute-start(bf16[128,1024]{1,0:T(8,128)(2,1)} %get-tuple-element.138), channel_id=1, source_target_pairs={{0,7},{1,0},{2,1},{3,2},{4,3},{5,4},{6,5},{7,6},{8,15},{9,8},{10,9... | collective-permute-start | bytes 786440 | tf_op jit(solution)/shard_map/ppermute | solution.py:29
  69.7 1.3 %copy-done.2 = f32[4,128,1024]{2,1,0:T(8,128)} copy-done((f32[4,128,1024]{2,1,0:T(8,128)}, f32[4,128,1024]{2,1,0:T(8,128)S(1)}, u32[]{:S(2)}) %copy-start.2) | copy-done | bytes 2097176
  70.9 21.0 %while.16 = (s32[]{:T(128)}, f32[128,1024]{1,0:T(8,128)S(1)}, s32[]{:T(128)}, f32[512,1024]{1,0:T(8,128)}, s32[]{:T(128)}, /*index=5*/s32[]{:T(128)}, s32[]{:T(1...) while((s32[]{:T(128)}, f32[128,1024]{1,0:T(8,128)S(1)}, s32[]{:T(128)}, f32[512,1024]{1,0:T(8,128)}, ...), condition=%wide.region_10.11_spmd, body=%wide.region_9.10_spmd.sunk | while | flops 393235 | bytes 3146060 | solution.py:144
  71.1 5.8 %collective-permute-done = bf16[128,1024]{1,0:T(8,128)(2,1)S(1)} collective-permute-done((bf16[128,1024]{1,0:T(8,128)(2,1)S(1)}, bf16[128,1024]{1,0:T(8,128)(2,1)S(1)}, u32[]{:S(2)}, u32[]{:S(2)}) %collective-permute-start) | collective-permute-done | bytes 262176 | tf_op jit(solution)/shard_map/while/body/eval_jaxpr/ppermute | solution.py:29
  76.8 1.1 %dynamic-slice_add_fusion.2 = f32[128,1024]{1,0:T(8,128)S(1)} fusion(f32[512,1024]{1,0:T(8,128)} %get-tuple-element.200, s32[]{:T(128)S(6)} %select_n.65, bf16[128,1024]{1,0:T(8,128)(2,1)S(1)} %collective-permute-done), kind=kLoop, calls=%fused_computation.clone.1 | loop fusion | flops 262144 | bytes 1310724 | tf_op jit(solution)/shard_map/while/body/eval_jaxpr/add | solution.py:141
  78.1 5.8 %collective-permute-done = bf16[128,1024]{1,0:T(8,128)(2,1)S(1)} collective-permute-done((bf16[128,1024]{1,0:T(8,128)(2,1)S(1)}, bf16[128,1024]{1,0:T(8,128)(2,1)S(1)}, u32[]{:S(2)}, u32[]{:S(2)}) %collective-permute-start) | collective-permute-done | bytes 262176 | tf_op jit(solution)/shard_map/while/body/eval_jaxpr/ppermute | solution.py:29
  85.1 5.8 %collective-permute-done = bf16[128,1024]{1,0:T(8,128)(2,1)S(1)} collective-permute-done((bf16[128,1024]{1,0:T(8,128)(2,1)S(1)}, bf16[128,1024]{1,0:T(8,128)(2,1)S(1)}, u32[]{:S(2)}, u32[]{:S(2)}) %collective-permute-start) | collective-permute-done | bytes 262176 | tf_op jit(solution)/shard_map/while/body/eval_jaxpr/ppermute | solution.py:29
  92.0 1.3 %fusion.23 = bf16[128,1024]{1,0:T(8,128)(2,1)S(1)} fusion(f32[128,1024]{1,0:T(8,128)S(1)} %get-tuple-element.114, f32[512,512]{1,0:T(8,128)S(1)} %copy.24, f32[512,512]{1,0:T(8,128)} %copy-done.1, bf16[128,1024]{1,0:T(8,128)(2,1)} %collective-permute-done.4, bf16[128,1024]{1,0:T(8,128)(2,1)} %collective-permute-done.3), kind=kLoop, calls=%fused_computation.45 | loop fusion | flops 917504 | bytes 3407872 | tf_op jit(solution)/shard_map/convert.2
  (102 shorter events, 21.7 us)
Async XLA Ops:
  7.2 33.1 %copy-start = (bf16[512,1024]{1,0:T(8,128)(2,1)S(1)}, bf16[512,1024]{1,0:T(8,128)(2,1)}, u32[]{:S(2)}) copy-start(bf16[512,1024]{1,0:T(8,128)(2,1)} %param.17) | copy-start | bytes 3145732
  7.2 11.9 %copy-start.3 = (bf16[128,512]{1,0:T(8,128)(2,1)S(1)}, bf16[128,512]{1,0:T(8,128)(2,1)}, u32[]{:S(2)}) copy-start(bf16[128,512]{1,0:T(8,128)(2,1)} %param.11) | copy-start | bytes 393220
  7.2 11.9 %copy-start.6 = (bf16[512,512]{1,0:T(8,128)(2,1)S(1)}, bf16[512,512]{1,0:T(8,128)(2,1)}, u32[]{:S(2)}) copy-start(bf16[512,512]{1,0:T(8,128)(2,1)} %param.13) | copy-start | bytes 1572868
  7.2 25.4 %all-gather.2.cloned.1.call-start = ((), (), s32[]{:S(2)}) async-start(), calls=%async_computation | async-start | bytes 1310720 | tf_op jit(solution)/shard_map/all_gather | solution.py:109
  13.0 20.6 %collective-permute-start.2 = (bf16[128,1024]{1,0:T(8,128)(2,1)}, bf16[128,1024]{1,0:T(8,128)(2,1)S(1)}, u32[]{:S(2)}, u32[]{:S(2)}) collective-permute-start(bf16[128,1024]{1,0:T(8,128)(2,1)} %pad_maximum_fusion.2), channel_id=1, source_target_pairs={{1,0},{2,1},{3,2},{4,3},{5,4},{6,5},{7,6},{0,7},{9,8},{10,9},{11,1... | collective-permute-start | bytes 786440 | tf_op jit(solution)/shard_map/ppermute | solution.py:22
  19.1 14.5 %collective-permute-start.1 = (bf16[128,1024]{1,0:T(8,128)(2,1)}, bf16[128,1024]{1,0:T(8,128)(2,1)S(1)}, u32[]{:S(2)}, u32[]{:S(2)}) collective-permute-start(bf16[128,1024]{1,0:T(8,128)(2,1)} %pad_maximum_fusion.2), channel_id=1, source_target_pairs={{0,1},{1,2},{2,3},{3,4},{4,5},{5,6},{6,7},{7,0},{8,9},{9,10},{10,1... | collective-permute-start | bytes 786440 | tf_op jit(solution)/shard_map/ppermute | solution.py:21
  35.8 2.4 %copy-start.5 = (bf16[512,512]{0,1:T(8,128)(2,1)S(1)}, bf16[512,512]{0,1:T(8,128)(2,1)}, u32[]{:S(2)}) copy-start(bf16[512,512]{0,1:T(8,128)(2,1)} %copy.20) | copy-start | bytes 1572868
  37.5 1.3 %copy-start.9 = (bf16[512,512]{1,0:T(8,128)(2,1)S(1)}, bf16[512,512]{1,0:T(8,128)(2,1)}, u32[]{:S(2)}) copy-start(bf16[512,512]{1,0:T(8,128)(2,1)} %param.16) | copy-start | bytes 1572868
  38.8 2.6 %copy-start.26 = (bf16[1024,512]{1,0:T(8,128)(2,1)S(1)}, bf16[1024,512]{1,0:T(8,128)(2,1)}, u32[]{:S(2)}) copy-start(bf16[1024,512]{1,0:T(8,128)(2,1)} %param.18) | copy-start | bytes 3145732
  51.2 2.9 %copy-start.4 = (bf16[512,512]{0,1:T(8,128)(2,1)S(1)}, bf16[512,512]{0,1:T(8,128)(2,1)}, u32[]{:S(2)}) copy-start(bf16[512,512]{0,1:T(8,128)(2,1)} %copy.22) | copy-start | bytes 1572868
  52.3 3.0 %copy-start.12 = (bf16[128,512]{0,1:T(8,128)(2,1)S(1)}, bf16[128,512]{0,1:T(8,128)(2,1)}, u32[]{:S(2)}) copy-start(bf16[128,512]{0,1:T(8,128)(2,1)} %copy.21) | copy-start | bytes 393220
  54.1 2.4 %copy-start.11 = (bf16[128,512]{0,1:T(8,128)(2,1)S(1)}, bf16[128,512]{0,1:T(8,128)(2,1)}, u32[]{:S(2)}) copy-start(bf16[128,512]{0,1:T(8,128)(2,1)} %copy.23) | copy-start | bytes 393220
  61.3 1.4 %copy-start.7 = (bf16[512,512]{1,0:T(8,128)(2,1)S(1)}, bf16[512,512]{1,0:T(8,128)(2,1)}, u32[]{:S(2)}) copy-start(bf16[512,512]{1,0:T(8,128)(2,1)} %param.13) | copy-start | bytes 1572868
  61.3 1.4 %copy-start.18 = (bf16[8,64,128]{2,1,0:T(8,128)(2,1)S(1)}, bf16[8,64,128]{2,1,0:T(8,128)(2,1)}, u32[]{:S(2)}) copy-start(bf16[8,64,128]{2,1,0:T(8,128)(2,1)} %convolution_convert_fusion.4) | copy-start | bytes 393220
  61.3 8.0 %copy-start.25 = (f32[4]{0:T(128)S(1)}, f32[4]{0:T(128)}, u32[]{:S(2)}) copy-start(f32[4]{0:T(128)} %compare_convert_fusion) | copy-start | bytes 52
  64.6 27.4 %collective-permute-start.4 = (bf16[128,1024]{1,0:T(8,128)(2,1)}, bf16[128,1024]{1,0:T(8,128)(2,1)}, u32[]{:S(2)}, u32[]{:S(2)}) collective-permute-start(bf16[128,1024]{1,0:T(8,128)(2,1)} %get-tuple-element.139), channel_id=1, source_target_pairs={{0,1},{1,2},{2,3},{3,4},{4,5},{5,6},{6,7},{7,0},{8,9},{9,10},{10,1... | collective-permute-start | bytes 786440 | tf_op jit(solution)/shard_map/ppermute | solution.py:29
  66.0 26.0 %collective-permute-start.3 = (bf16[128,1024]{1,0:T(8,128)(2,1)}, bf16[128,1024]{1,0:T(8,128)(2,1)}, u32[]{:S(2)}, u32[]{:S(2)}) collective-permute-start(bf16[128,1024]{1,0:T(8,128)(2,1)} %get-tuple-element.138), channel_id=1, source_target_pairs={{0,7},{1,0},{2,1},{3,2},{4,3},{5,4},{6,5},{7,6},{8,15},{9,8},{10,9... | collective-permute-start | bytes 786440 | tf_op jit(solution)/shard_map/ppermute | solution.py:29
  69.6 1.3 %copy-start.2 = (f32[4,128,1024]{2,1,0:T(8,128)}, f32[4,128,1024]{2,1,0:T(8,128)S(1)}, u32[]{:S(2)}) copy-start(f32[4,128,1024]{2,1,0:T(8,128)S(1)} %broadcast_multiply_fusion) | copy-start | bytes 6291460
  71.0 5.8 %collective-permute-start = (bf16[128,1024]{1,0:T(8,128)(2,1)S(1)}, bf16[128,1024]{1,0:T(8,128)(2,1)S(1)}, u32[]{:S(2)}, u32[]{:S(2)}) collective-permute-start(bf16[128,1024]{1,0:T(8,128)(2,1)S(1)} %convert_element_type.195), channel_id=1, source_target_pairs={{0,8},{8,16},{16,24},{24,0},{1,9},{9,17},{17,25},{25,1},{2,10},{10... | collective-permute-start | bytes 786440 | tf_op jit(solution)/shard_map/while/body/eval_jaxpr/ppermute | solution.py:29
  78.0 5.8 %collective-permute-start = (bf16[128,1024]{1,0:T(8,128)(2,1)S(1)}, bf16[128,1024]{1,0:T(8,128)(2,1)S(1)}, u32[]{:S(2)}, u32[]{:S(2)}) collective-permute-start(bf16[128,1024]{1,0:T(8,128)(2,1)S(1)} %convert_element_type.195), channel_id=1, source_target_pairs={{0,8},{8,16},{16,24},{24,0},{1,9},{9,17},{17,25},{25,1},{2,10},{10... | collective-permute-start | bytes 786440 | tf_op jit(solution)/shard_map/while/body/eval_jaxpr/ppermute | solution.py:29
  85.0 5.8 %collective-permute-start = (bf16[128,1024]{1,0:T(8,128)(2,1)S(1)}, bf16[128,1024]{1,0:T(8,128)(2,1)S(1)}, u32[]{:S(2)}, u32[]{:S(2)}) collective-permute-start(bf16[128,1024]{1,0:T(8,128)(2,1)S(1)} %convert_element_type.195), channel_id=1, source_target_pairs={{0,8},{8,16},{16,24},{24,0},{1,9},{9,17},{17,25},{25,1},{2,10},{10... | collective-permute-start | bytes 786440 | tf_op jit(solution)/shard_map/while/body/eval_jaxpr/ppermute | solution.py:29
  91.9 1.4 %copy-start.10 = (bf16[512,512]{1,0:T(8,128)(2,1)S(1)}, bf16[512,512]{1,0:T(8,128)(2,1)}, u32[]{:S(2)}) copy-start(bf16[512,512]{1,0:T(8,128)(2,1)} %param.14) | copy-start | bytes 1572868
  92.0 1.4 %copy-start.15 = (f32[128,512]{1,0:T(8,128)S(1)}, f32[128,512]{1,0:T(8,128)}, u32[]{:S(2)}) copy-start(f32[128,512]{1,0:T(8,128)} %fusion.72) | copy-start | bytes 786436
  92.0 1.7 %copy-start.8 = (bf16[512,512]{1,0:T(8,128)(2,1)S(1)}, bf16[512,512]{1,0:T(8,128)(2,1)}, u32[]{:S(2)}) copy-start(bf16[512,512]{1,0:T(8,128)(2,1)} %param.15) | copy-start | bytes 1572868
  (11 other events, 9.1 us)
Sparse Core Ops, SparseCore 0:
  13.2 19.4 all-gather.1
where the time goes:
time: 103 us; the launch traced here: 102 us
  waiting for transfers between devices  28.6 us (28%)
  matrix products  20.4 us (20%)
  between operations  15.2 us (15%)
  local copies, waits for them, and re-layouts  13.6 us (13%)
  other arithmetic  13.2 us (13%)
  starting transfers between devices  11 us (11%)
    ppermute x5, waiting for transfers between devices, shifted(): lax.ppermute(array, axis, [(i, (i + by) % devices) for i in range(devices)])  17.3 us
    all_gather x1, waiting for transfers between devices, on_device(): panels = lax.all_gather(keyvals, 'blk', axis=0, tiled=True)  11.3 us
    ppermute x1, starting transfers between devices, with_halo(): after = lax.ppermute(leading, axis, down)  6.05 us
    unnamed x54, local copies, waits for them, and re-layouts  5.09 us
    ppermute x5, starting transfers between devices, shifted(): lax.ppermute(array, axis, [(i, (i + by) % devices) for i in range(devices)])  4.89 us
    dot_general x1, matrix products, on_device(): grad_norm2 = jnp.dot(grad_pre, w_up.T, preferred_element_type=f32)  3.66 us
    add x3, other arithmetic, carry_step(): return running + lax.dynamic_slice_in_dim(far_parts, target * rows, rows, 0)  3.28 us
    dot_general x1, matrix products, on_device(): jnp.dot(grad_resid.astype(bf16), w_out.T, preferred_element_type=f32)  2.16 us
  transfers between devices with their start and end apart: 8, of which 4 were waited for; matrix products, arithmetic and copies ran while one was open for 6% of the time, Pallas kernels for 0%

commit v1 on v0

v1 whole, which is shorter than its diff:
```python
import functools

import jax
import jax.numpy as jnp
from jax import lax
from jax.experimental import pallas as pl
from jax.experimental.pallas import tpu as pltpu
from jax.sharding import PartitionSpec as P

H = 8
HEAD = 64
EPS = 1e-05
SCALE = HEAD ** (-0.5)
PAIR = 2 * HEAD
GELU_C = 0.7978845608028654
GELU_A = 0.044715
MIB = 1 << 20

f32 = jnp.float32
bf16 = jnp.bfloat16


def dot(a, b):
    return jnp.dot(a, b, preferred_element_type=f32)


def dot_t(a, b):
    return lax.dot_general(a, b, (((1,), (1,)), ((), ())), preferred_element_type=f32)


def t_dot(a, b):
    return lax.dot_general(a, b, (((0,), (0,)), ((), ())), preferred_element_type=f32)


def normalize(values):
    mean_v = jnp.mean(values, axis=-1, keepdims=True)
    centered = values - mean_v
    inv_std = lax.rsqrt(jnp.mean(centered * centered, axis=-1, keepdims=True) + EPS)
    return (centered * inv_std, inv_std)


def normalize_back(unit, inv_std, upstream):
    return inv_std * (
        upstream
        - jnp.mean(upstream, axis=-1, keepdims=True)
        - unit * jnp.mean(upstream * unit, axis=-1, keepdims=True)
    )


def halves(rows):
    left = lax.broadcasted_iota(jnp.int32, rows.shape, 1) < HEAD
    zero = jnp.zeros_like(rows)
    return jnp.concatenate([jnp.where(left, rows, zero), jnp.where(left, zero, rows)], 0)


def unhalve(both):
    n = both.shape[1] // 2
    first, second = both[:, :n], both[:, n:]
    upper = lax.broadcasted_iota(jnp.int32, first.shape, 0) < HEAD
    return jnp.where(upper, first, second).T


def own_kernel(x_ref, cot_ref, wq_ref, wk_ref, wv_ref, wdown_ref, q_ref, k_ref, v_ref, gact_ref):
    unit, _ = normalize(x_ref[...].astype(f32))
    normed = unit.astype(bf16)
    q_ref[...] = (dot(normed, wq_ref[...]) * SCALE).astype(bf16)
    k_ref[...] = dot(normed, wk_ref[...]).astype(bf16)
    v_ref[...] = dot(normed, wv_ref[...]).astype(bf16)
    gact_ref[...] = dot_t(cot_ref[...], wdown_ref[...])


def main_kernel(groups, listed, *refs):
    experts_ref, place_ref = refs[:2]
    slots = refs[2 : 2 + groups]
    (near_a, near_b, q_ref, k_ref, v_ref, gact_ref, cot_ref, wk_ref, wv_ref, wout_ref, wup_ref) = refs[
        2 + groups : 13 + groups
    ]
    outs = refs[13 + groups :]
    far_count = groups.bit_length() - 1
    send_a, send_b, keep = outs[:3]
    sends = outs[3 : 3 + far_count]
    gq_ref, gkv_ref, act_ref, resid_ref, gres_ref = outs[3 + far_count : 8 + far_count]
    chosen_s, k_s, v_s, w_s, inv_s, mixed_s, gk_s, gv_s = outs[8 + far_count :]
    x_ref = slots[0]
    rows, width = x_ref.shape
    picked = [experts_ref[0, e] ^ place_ref[0] for e in range(listed)]
    for e in range(listed):
        for slot in range(groups):

            @pl.when(picked[e] == slot)
            def _(e=e, slot=slot):
                chosen_s[e * rows : (e + 1) * rows, :] = slots[slot][...]

    def project(block, at):
        unit, _ = normalize(block.astype(f32))
        normed = unit.astype(bf16)
        k_s[at : at + block.shape[0], :] = dot(normed, wk_ref[...]).astype(bf16)
        v_s[at : at + block.shape[0], :] = dot(normed, wv_ref[...]).astype(bf16)

    k_s[:rows, :] = k_ref[...]
    v_s[:rows, :] = v_ref[...]
    others = jnp.concatenate([near_a[...], near_b[...], chosen_s[...]], 0)
    project(others, rows)

    for j in range(H // 2):
        cols = slice(j * PAIR, (j + 1) * PAIR)
        q2 = halves(q_ref[:, cols])
        scores = dot_t(k_s[:, cols], q2)
        weights = jnp.exp(scores - jnp.max(scores, axis=0, keepdims=True))
        inv = 1.0 / jnp.sum(weights, axis=0, keepdims=True)
        w_s[j] = weights
        inv_s[j] = inv
        mixed = t_dot(v_s[:, cols], weights.astype(bf16)) * inv
        mixed_s[:, cols] = unhalve(mixed).astype(bf16)

    mixed = mixed_s[...]
    resid = x_ref[...].astype(f32) + dot(mixed, wout_ref[...])
    resid_ref[...] = resid
    unit2, inv2 = normalize(resid)
    pre = dot(unit2.astype(bf16), wup_ref[...])
    square = pre * pre
    tanh = jnp.tanh(GELU_C * pre * (1.0 + GELU_A * square))
    act_ref[...] = (0.5 * pre * (1.0 + tanh)).astype(bf16)
    slope = 0.5 * (1.0 + tanh) + (0.5 * GELU_C) * pre * (1.0 - tanh * tanh) * (
        1.0 + (3.0 * GELU_A) * square
    )
    gpre = (gact_ref[...] * slope).astype(bf16)
    gres = cot_ref[...].astype(f32) + normalize_back(unit2, inv2, dot_t(gpre, wup_ref[...]))
    gres_ref[...] = gres
    gmixed = dot_t(gres.astype(bf16), wout_ref[...]).astype(bf16)
    prod = gmixed.astype(f32) * mixed.astype(f32)
    high = prod.astype(bf16)
    low = (prod - high.astype(f32)).astype(bf16)
    head_of = lax.broadcasted_iota(jnp.int32, (H, width), 1) // HEAD
    ones = (head_of == lax.broadcasted_iota(jnp.int32, (H, width), 0)).astype(bf16)
    delta = dot_t(ones, high) + dot_t(ones, low)

    for j in range(H // 2):
        cols = slice(j * PAIR, (j + 1) * PAIR)
        q2 = halves(q_ref[:, cols])
        g2 = halves(gmixed[:, cols])
        row = jnp.concatenate([delta[2 * j : 2 * j + 1, :], delta[2 * j + 1 : 2 * j + 2, :]], 1)
        probs = w_s[j] * inv_s[j]
        ds = (probs * (dot_t(v_s[:, cols], g2) - row)).astype(bf16)
        gv_s[:, cols] = dot(probs.astype(bf16), g2).astype(bf16)
        gk_s[:, cols] = dot(ds, q2).astype(bf16)
        gq_ref[:, cols] = (unhalve(t_dot(k_s[:, cols], ds)) * SCALE).astype(bf16)

    gkv_ref[:, :width] = gk_s[:rows, :]
    gkv_ref[:, width:] = gv_s[:rows, :]
    parts = dot_t(gk_s[rows:, :], wk_ref[...]) + dot_t(gv_s[rows:, :], wv_ref[...])
    send_a[...] = parts[:rows].astype(bf16)
    send_b[...] = parts[rows : 2 * rows].astype(bf16)

    def far(slot):
        total = jnp.zeros((rows, width), f32)
        for e in range(listed):
            part = parts[(2 + e) * rows : (3 + e) * rows]
            total = total + jnp.where(picked[e] == slot, part, 0.0)
        return total

    keep[...] = far(0)
    for bit in range(far_count):
        for i in range(1 << bit):
            sends[bit][i * rows : (i + 1) * rows, :] = far((1 << bit) + i).astype(bf16)


def rest_kernel(gq_ref, gkv_ref, keep_ref, act_ref, resid_ref, wq_ref, wk_ref, wv_ref, wdown_ref, out_ref, acc_ref):
    width = gq_ref.shape[1]
    acc_ref[...] = (
        keep_ref[...]
        + dot_t(gq_ref[...], wq_ref[...])
        + dot_t(gkv_ref[:, :width], wk_ref[...])
        + dot_t(gkv_ref[:, width:], wv_ref[...])
    )
    out_ref[...] = (resid_ref[...] + dot(act_ref[...], wdown_ref[...])).astype(bf16)


def last_kernel(x_ref, gres_ref, acc_ref, *refs):
    out_ref = refs[-1]
    rows = x_ref.shape[0]
    total = acc_ref[...]
    for part in refs[:-1]:
        total = total + part[:rows, :].astype(f32)
    unit, inv = normalize(x_ref[...].astype(f32))
    out_ref[...] = (gres_ref[...] + normalize_back(unit, inv, total)).astype(bf16)


def call(kernel, outs, args, scratch=(), flops=0, smem=0):
    whole = pl.BlockSpec(memory_space=pltpu.VMEM)
    small = pl.BlockSpec(memory_space=pltpu.SMEM)
    return pl.pallas_call(
        kernel,
        out_shape=[jax.ShapeDtypeStruct(shape, dtype) for shape, dtype in outs],
        in_specs=[small] * smem + [whole] * (len(args) - smem),
        out_specs=[whole] * len(outs),
        scratch_shapes=list(scratch),
        compiler_params=pltpu.CompilerParams(vmem_limit_bytes=40 * MIB),
        cost_estimate=pl.CostEstimate(flops=flops, bytes_accessed=4 * MIB, transcendentals=0),
    )(*args)


def on_device(nodes, experts_list, w_query, w_key, w_value, w_out, w_up, w_down, cotangent):
    rows, width = nodes.shape
    hidden = w_up.shape[1]
    groups = lax.axis_size("blk")
    domains = lax.axis_size("dom")
    listed = experts_list.shape[1]
    bits = groups.bit_length() - 1
    place = lax.axis_index("blk").astype(jnp.int32).reshape(1)

    def across(array, bit):
        return lax.ppermute(array, "blk", [(i, i ^ (1 << bit)) for i in range(groups)])

    pairs_a = [(i, i ^ 1) for i in range(domains)]
    pairs_b = []
    for i in range(1, domains, 2):
        pairs_b += [(i, (i + 1) % domains), ((i + 1) % domains, i)]

    held = {0: nodes}
    top = bits - 1
    held[1 << top] = across(nodes, top)
    near_b = lax.ppermute(nodes, "dom", pairs_b)
    near_a = lax.ppermute(nodes, "dom", pairs_a)
    for bit in range(top - 1, -1, -1):
        for slot in list(held):
            held[slot | (1 << bit)] = across(held[slot], bit)

    q, k, v, gact = call(
        own_kernel,
        [((rows, width), bf16)] * 3 + [((rows, hidden), f32)],
        [nodes, cotangent, w_query, w_key, w_value, w_down],
        flops=2 * rows * width * (3 * width + hidden),
    )
    keys = (3 + listed) * rows
    outs = call(
        functools.partial(main_kernel, groups, listed),
        [((rows, width), bf16)] * 2
        + [((rows, width), f32)]
        + [(((1 << bit) * rows, width), bf16) for bit in range(bits)]
        + [((rows, width), bf16), ((rows, 2 * width), bf16), ((rows, hidden), bf16)]
        + [((rows, width), f32)] * 2,
        [experts_list, place]
        + [held[slot] for slot in range(groups)]
        + [near_a, near_b, q, k, v, gact, cotangent, w_key, w_value, w_out, w_up],
        [
            pltpu.VMEM((listed * rows, width), bf16),
            pltpu.VMEM((keys, width), bf16),
            pltpu.VMEM((keys, width), bf16),
            pltpu.VMEM((H // 2, keys, 2 * rows), f32),
            pltpu.VMEM((H // 2, 1, 2 * rows), f32),
            pltpu.VMEM((rows, width), bf16),
            pltpu.VMEM((keys, width), bf16),
            pltpu.VMEM((keys, width), bf16),
        ],
        flops=2 * rows * width * (8 * keys + 4 * hidden),
        smem=2,
    )
    send_a, send_b, keep = outs[:3]
    sends = list(outs[3 : 3 + bits])
    gq, gkv, act, resid, gres = outs[3 + bits :]

    received = []
    for bit in range(top, -1, -1):
        lo, hi = (1 << bit) * rows, (2 << bit) * rows
        part = sends[bit]
        if received:
            total = part.astype(f32)
            for earlier in received:
                total = total + earlier[lo:hi].astype(f32)
            part = total.astype(bf16)
        received.append(across(part, bit))
        if bit == top:
            from_b = lax.ppermute(send_b, "dom", pairs_b)
            from_a = lax.ppermute(send_a, "dom", pairs_a)

    layer_out, acc = call(
        rest_kernel,
        [((rows, width), bf16), ((rows, width), f32)],
        [gq, gkv, keep, act, resid, w_query, w_key, w_value, w_down],
        flops=2 * rows * width * (3 * width + hidden),
    )
    (grad_nodes,) = call(
        last_kernel,
        [((rows, width), bf16)],
        [nodes, gres, acc, from_a, from_b] + received,
    )
    return (layer_out, grad_nodes)


def solution(mesh):
    split = P(("blk", "dom"), None)
    return jax.shard_map(
        on_device,
        mesh=mesh,
        in_specs=(split, split, P(), P(), P(), P(), P(), P(), split),
        out_specs=(split, split),
        check_vma=False,
    )
```

time: 103 us -> 34.6 us (0.34)
  waiting for transfers between devices: 28.6 us -> 3.21 us
  matrix products: 20.4 us -> 0 us
  between operations: 15.2 us -> 1.38 us
  other arithmetic: 13.2 us -> 0.03 us
  Pallas kernels: 0 us -> 9.08 us
  local copies, waits for them, and re-layouts: 13.6 us -> 6.92 us
  starting transfers between devices: 11 us -> 13.7 us
    dot_general x17 -> x0, matrix products: 20.4 us -> none  [the longest x1 3.66 us: on_device(): grad_norm2 = jnp.dot(grad_pre, w_up.T, preferred_element_type=f32)]
    ppermute x7 -> x9, waiting for transfers between devices: 17.3 us -> 3.21 us  [the longest x5 2.86 us: across(): lax.ppermute(array, 'blk', [(i, i ^ 1 << bit) for i in range(groups)])]
    all_gather x1 -> x0, waiting for transfers between devices: 11.3 us -> none  [on_device(): panels = lax.all_gather(keyvals, 'blk', axis=0, tiled=True)]
    pallas_call x0 -> x4, Pallas kernels: none -> 9.08 us  [call(): pl.pallas_call(kernel, out_shape=[jax.ShapeDtypeStruct(shape, dtype) for...]
    reduce_sum x5 -> x0, other arithmetic: 4.08 us -> none  [the longest x2 1.26 us: normalize(): jnp.mean(centered * centered, axis=-1, keepdims=True) + EPS]
    add x4 -> x0, other arithmetic: 3.29 us -> none  [the longest x3 3.28 us: carry_step(): return running + lax.dynamic_slice_in_dim(far_parts, target * rows, rows, 0)]
    reshape x2 -> x0, local copies, waits for them, and re-layouts: 3.11 us -> none  [the longest x1 1.56 us: attend_back(): grad_v.reshape(count, width)]
    slice x4 -> x0, local copies, waits for them, and re-layouts: 2.91 us -> none  [the longest x2 1.07 us: attend(): kh = heads_of(keyvals[:, :width])]
  transfers between devices with their start and end apart: 8 -> 9, of which waited for: 4 -> 2; matrix products, arithmetic and copies ran while one was open for 6% -> 0% of each run, Pallas kernels for 0% -> 7%
where the time goes in v1:
time: 34.6 us; the launch traced here: 34.3 us
  starting transfers between devices  13.7 us (40%)
  Pallas kernels  9.08 us (26%)
  local copies, waits for them, and re-layouts  6.92 us (20%)
  waiting for transfers between devices  3.21 us (9%)
  between operations  1.38 us (4%)
    pallas_call x4, Pallas kernels, call(): pl.pallas_call(kernel, out_shape=[jax.ShapeDtypeStruct(shape, dtype) for...  9.08 us
    unnamed x22, local copies, waits for them, and re-layouts  6.92 us
    ppermute x1, starting transfers between devices, on_device(): near_b = lax.ppermute(nodes, 'dom', pairs_b)  4.56 us
    ppermute x5, starting transfers between devices, across(): lax.ppermute(array, 'blk', [(i, i ^ 1 << bit) for i in range(groups)])  4.19 us
    ppermute x1, starting transfers between devices, on_device(): from_b = lax.ppermute(send_b, 'dom', pairs_b)  2.88 us
    ppermute x5, waiting for transfers between devices, across(): lax.ppermute(array, 'blk', [(i, i ^ 1 << bit) for i in range(groups)])  2.86 us
    ppermute x1, starting transfers between devices, on_device(): from_a = lax.ppermute(send_a, 'dom', pairs_a)  2.02 us
  transfers between devices with their start and end apart: 9, of which 2 were waited for; matrix products, arithmetic and copies ran while one was open for 0% of the time, Pallas kernels for 7%

profile of v1, /device:TPU:0, one launch (start us, length us, event | category | flops | bytes accessed | tf_op | source)
XLA Modules:
  0.0 34.3 jit_solution(16174261534844977752)
XLA Ops:
  0.6 3.0 %collective-permute-start.1 = (bf16[128,512]{1,0:T(8,128)(2,1)}, bf16[128,512]{1,0:T(8,128)(2,1)S(1)}, u32[]{:S(2)}, u32[]{:S(2)}) collective-permute-start(bf16[128,512]{1,0:T(8,128)(2,1)} %x_ref.3), channel_id=1, source_target_pairs={{0,16},{8,24},{16,0},{24,8},{1,17},{9,25},{17,1},{25,9},{2,18},{10... | collective-permute-start | bytes 393224 | tf_op jit(solution)/shard_map/ppermute | solution.py:213
  3.6 4.6 %collective-permute-start.4 = (bf16[128,512]{1,0:T(8,128)(2,1)}, bf16[128,512]{1,0:T(8,128)(2,1)S(1)}, u32[]{:S(2)}, u32[]{:S(2)}) collective-permute-start(bf16[128,512]{1,0:T(8,128)(2,1)} %x_ref.3), channel_id=1, source_target_pairs={{1,2},{2,1},{3,4},{4,3},{5,6},{6,5},{7,0},{0,7},{9,10},{10,9},{11,... | collective-permute-start | bytes 393224 | tf_op jit(solution)/shard_map/ppermute | solution.py:223
  8.2 0.0 collective-permute-done.1.refs_4_
  8.2 0.5 %collective-permute-start.2 = (bf16[128,512]{1,0:T(8,128)(2,1)S(1)}, bf16[128,512]{1,0:T(8,128)(2,1)S(1)}, u32[]{:S(2)}, u32[]{:S(2)}) collective-permute-start(bf16[128,512]{1,0:T(8,128)(2,1)S(1)} %collective-permute-done.1.refs_4_), channel_id=1, source_target_pairs={{0,8},{8,0},{16,24},{24,16},{1,9},{9,1},{17,25},{25,17},{2,10},{10... | collective-permute-start | bytes 393224 | tf_op jit(solution)/shard_map/ppermute | solution.py:213
  9.4 1.0 %copy-done = bf16[512,512]{1,0:T(8,128)(2,1)S(1)} copy-done((bf16[512,512]{1,0:T(8,128)(2,1)S(1)}, bf16[512,512]{1,0:T(8,128)(2,1)}, u32[]{:S(2)}) %copy-start) | copy-done | bytes 524312
  10.4 1.0 %copy-done.2 = bf16[512,512]{1,0:T(8,128)(2,1)S(1)} copy-done((bf16[512,512]{1,0:T(8,128)(2,1)S(1)}, bf16[512,512]{1,0:T(8,128)(2,1)}, u32[]{:S(2)}) %copy-start.2) | copy-done | bytes 524312
  11.5 1.2 %copy-done.4 = bf16[1024,512]{1,0:T(8,128)(2,1)S(1)} copy-done((bf16[1024,512]{1,0:T(8,128)(2,1)S(1)}, bf16[1024,512]{1,0:T(8,128)(2,1)}, u32[]{:S(2)}) %copy-start.4) | copy-done | bytes 1048600
  12.7 1.0 %copy-done.6 = bf16[512,512]{1,0:T(8,128)(2,1)S(1)} copy-done((bf16[512,512]{1,0:T(8,128)(2,1)S(1)}, bf16[512,512]{1,0:T(8,128)(2,1)}, u32[]{:S(2)}) %copy-start.6) | copy-done | bytes 524312
  13.7 0.9 %copy-done.7 = bf16[128,512]{1,0:T(8,128)(2,1)S(1)} copy-done((bf16[128,512]{1,0:T(8,128)(2,1)S(1)}, bf16[128,512]{1,0:T(8,128)(2,1)}, u32[]{:S(2)}) %copy-start.7) | copy-done | bytes 131096
  14.6 0.9 %copy-done.10 = bf16[128,512]{1,0:T(8,128)(2,1)S(1)} copy-done((bf16[128,512]{1,0:T(8,128)(2,1)S(1)}, bf16[128,512]{1,0:T(8,128)(2,1)}, u32[]{:S(2)}) %copy-start.10) | copy-done | bytes 131096
  15.5 0.9 %shard_map.104 = (bf16[128,512]{1,0:T(8,128)(2,1)S(1)}, bf16[128,512]{1,0:T(8,128)(2,1)S(1)}, bf16[128,512]{1,0:T(8,128)(2,1)S(1)}, f32[128,1024]{1,0:T(8,128)S(1)}) custom-call(bf16[128,512]{1,0:T(8,128)(2,1)S(1)} %copy-done.7, bf16[128,512]{1,0:T(8,128)(2,1)S(1)} %copy-done.10, bf16[512,512]{1,0:T(8,128)(2,1)S(1)} %copy-done.6, ...), custom_call_target="tpu_custom_call" | custom-call | flops 335544320 | bytes 4194304 | tf_op jit(solution)/shard_map/pallas_call | solution.py:192
  16.4 0.1 copy-done.1
  16.6 0.2 copy-done.3
  16.7 0.3 %copy-done.8 = bf16[512,1024]{1,0:T(8,128)(2,1)S(1)} copy-done((bf16[512,1024]{1,0:T(8,128)(2,1)S(1)}, bf16[512,1024]{1,0:T(8,128)(2,1)}, u32[]{:S(2)}) %copy-start.8) | copy-done | bytes 1048600
  17.1 0.1 copy-done.9
  17.2 5.8 %shard_map.105 = (bf16[128,512]{1,0:T(8,128)(2,1)S(1)}, bf16[128,512]{1,0:T(8,128)(2,1)S(1)}, f32[128,512]{1,0:T(8,128)S(1)}, bf16[128,512]{1,0:T(8,128)(2,1)S(1...) custom-call(s32[1,1]{1,0:T(1,128)S(6)} %copy.11.refs_0_, ...), custom_call_target="tpu_custom_call" | custom-call | flops 1073741824 | bytes 4194304 | tf_op jit(solution)/shard_map/pallas_call | solution.py:192
  23.0 0.6 %collective-permute-start.7 = (bf16[256,512]{1,0:T(8,128)(2,1)S(1)}, bf16[256,512]{1,0:T(8,128)(2,1)S(1)}, u32[]{:S(2)}, u32[]{:S(2)}) collective-permute-start(bf16[256,512]{1,0:T(8,128)(2,1)S(1)} %get-tuple-element.32), channel_id=1, source_target_pairs={{0,16},{8,24},{16,0},{24,8},{1,17},{9,25},{17,1},{25,9},{2,18},{10... | collective-permute-start | bytes 786440 | tf_op jit(solution)/shard_map/ppermute | solution.py:213
  23.6 2.0 %collective-permute-start.5 = (bf16[128,512]{1,0:T(8,128)(2,1)S(1)}, bf16[128,512]{1,0:T(8,128)(2,1)S(1)}, u32[]{:S(2)}, u32[]{:S(2)}) collective-permute-start(bf16[128,512]{1,0:T(8,128)(2,1)S(1)} %get-tuple-element.30), channel_id=1, source_target_pairs={{0,1},{1,0},{2,3},{3,2},{4,5},{5,4},{6,7},{7,6},{8,9},{9,8},{10,11... | collective-permute-start | bytes 393224 | tf_op jit(solution)/shard_map/ppermute | solution.py:275
  25.6 2.9 %collective-permute-start.6 = (bf16[128,512]{1,0:T(8,128)(2,1)S(1)}, bf16[128,512]{1,0:T(8,128)(2,1)S(1)}, u32[]{:S(2)}, u32[]{:S(2)}) collective-permute-start(bf16[128,512]{1,0:T(8,128)(2,1)S(1)} %get-tuple-element.31), channel_id=1, source_target_pairs={{1,2},{2,1},{3,4},{4,3},{5,6},{6,5},{7,0},{0,7},{9,10},{10,9},{11,... | collective-permute-start | bytes 393224 | tf_op jit(solution)/shard_map/ppermute | solution.py:274
  28.5 2.8 %collective-permute-done.7.refs_2_ = bf16[256,512]{1,0:T(8,128)(2,1)S(1)} collective-permute-done((bf16[256,512]{1,0:T(8,128)(2,1)S(1)}, bf16[256,512]{1,0:T(8,128)(2,1)S(1)}, u32[]{:S(2)}, u32[]{:S(2)}) %collective-permute-start.7) | collective-permute-done | bytes 262176 | tf_op jit(solution)/shard_map/ppermute | solution.py:213
  31.4 0.1 collective-permute-start.8
  31.5 1.5 %shard_map.106 = (bf16[128,512]{1,0:T(8,128)(2,1)}, f32[128,512]{1,0:T(8,128)S(1)}) custom-call(bf16[128,512]{1,0:T(8,128)(2,1)S(1)} %get-tuple-element.22.gq_ref, bf16[128,1024]{1,0:T(8,128)(2,1)S(1)} %get-tuple-element.23.gkv_ref, f32[128,512]{1,0:T(8,128)S(1)} %get-tuple-element.24.keep_ref, bf16[128,1024]{1,0:T(8,128)(2,1)S(1)} %get-tuple-element.25.act_ref, ...), custom_call_target="tpu_custom_call" | custom-call | flops 335544320 | bytes 4194304 | tf_op jit(solution)/shard_map/pallas_call | solution.py:192
  33.0 0.3 collective-permute-done.6.refs_1_
  33.3 1.0 %shard_map.107 = bf16[128,512]{1,0:T(8,128)(2,1)} custom-call(bf16[128,512]{1,0:T(8,128)(2,1)S(1)} %copy-done.7, f32[128,512]{1,0:T(8,128)S(1)} %get-tuple-element.28.gres_ref, f32[128,512]{1,0:T(8,128)S(1)} %get-tuple-element.29.acc_ref, bf16[128,512]{1,0:T(8,128)(2,1)S(1)} %collective-permute-done.5.refs_0_, ...), custom_call_target="tpu_custom_call" | custom-call | bytes 4194304 | tf_op jit(solution)/shard_map/pallas_call | solution.py:192
  (21 shorter events, 0.1 us)
Async XLA Ops:
  0.6 7.6 %collective-permute-start.1 = (bf16[128,512]{1,0:T(8,128)(2,1)}, bf16[128,512]{1,0:T(8,128)(2,1)S(1)}, u32[]{:S(2)}, u32[]{:S(2)}) collective-permute-start(bf16[128,512]{1,0:T(8,128)(2,1)} %x_ref.3), channel_id=1, source_target_pairs={{0,16},{8,24},{16,0},{24,8},{1,17},{9,25},{17,1},{25,9},{2,18},{10... | collective-permute-start | bytes 393224 | tf_op jit(solution)/shard_map/ppermute | solution.py:213
  3.6 12.8 %collective-permute-start.4 = (bf16[128,512]{1,0:T(8,128)(2,1)}, bf16[128,512]{1,0:T(8,128)(2,1)S(1)}, u32[]{:S(2)}, u32[]{:S(2)}) collective-permute-start(bf16[128,512]{1,0:T(8,128)(2,1)} %x_ref.3), channel_id=1, source_target_pairs={{1,2},{2,1},{3,4},{4,3},{5,6},{6,5},{7,0},{0,7},{9,10},{10,9},{11,... | collective-permute-start | bytes 393224 | tf_op jit(solution)/shard_map/ppermute | solution.py:223
  8.2 8.2 %collective-permute-start.3 = (bf16[128,512]{1,0:T(8,128)(2,1)}, bf16[128,512]{1,0:T(8,128)(2,1)S(1)}, u32[]{:S(2)}, u32[]{:S(2)}) collective-permute-start(bf16[128,512]{1,0:T(8,128)(2,1)} %x_ref.3), channel_id=1, source_target_pairs={{0,1},{1,0},{2,3},{3,2},{4,5},{5,4},{6,7},{7,6},{8,9},{9,8},{10,11... | collective-permute-start | bytes 393224 | tf_op jit(solution)/shard_map/ppermute | solution.py:224
  8.2 8.2 %collective-permute-start = (bf16[128,512]{1,0:T(8,128)(2,1)}, bf16[128,512]{1,0:T(8,128)(2,1)S(1)}, u32[]{:S(2)}, u32[]{:S(2)}) collective-permute-start(bf16[128,512]{1,0:T(8,128)(2,1)} %x_ref.3), channel_id=1, source_target_pairs={{0,8},{8,0},{16,24},{24,16},{1,9},{9,1},{17,25},{25,17},{2,10},{10... | collective-permute-start | bytes 393224 | tf_op jit(solution)/shard_map/ppermute | solution.py:213
  8.2 8.2 %collective-permute-start.2 = (bf16[128,512]{1,0:T(8,128)(2,1)S(1)}, bf16[128,512]{1,0:T(8,128)(2,1)S(1)}, u32[]{:S(2)}, u32[]{:S(2)}) collective-permute-start(bf16[128,512]{1,0:T(8,128)(2,1)S(1)} %collective-permute-done.1.refs_4_), channel_id=1, source_target_pairs={{0,8},{8,0},{16,24},{24,16},{1,9},{9,1},{17,25},{25,17},{2,10},{10... | collective-permute-start | bytes 393224 | tf_op jit(solution)/shard_map/ppermute | solution.py:213
  9.4 1.0 %copy-start = (bf16[512,512]{1,0:T(8,128)(2,1)S(1)}, bf16[512,512]{1,0:T(8,128)(2,1)}, u32[]{:S(2)}) copy-start(bf16[512,512]{1,0:T(8,128)(2,1)} %wk_ref.3) | copy-start | bytes 1572868
  10.4 1.0 %copy-start.2 = (bf16[512,512]{1,0:T(8,128)(2,1)S(1)}, bf16[512,512]{1,0:T(8,128)(2,1)}, u32[]{:S(2)}) copy-start(bf16[512,512]{1,0:T(8,128)(2,1)} %wv_ref.3) | copy-start | bytes 1572868
  11.4 1.2 %copy-start.4 = (bf16[1024,512]{1,0:T(8,128)(2,1)S(1)}, bf16[1024,512]{1,0:T(8,128)(2,1)}, u32[]{:S(2)}) copy-start(bf16[1024,512]{1,0:T(8,128)(2,1)} %wdown_ref.3) | copy-start | bytes 3145732
  12.7 1.0 %copy-start.6 = (bf16[512,512]{1,0:T(8,128)(2,1)S(1)}, bf16[512,512]{1,0:T(8,128)(2,1)}, u32[]{:S(2)}) copy-start(bf16[512,512]{1,0:T(8,128)(2,1)} %wq_ref.3) | copy-start | bytes 1572868
  13.7 0.9 %copy-start.7 = (bf16[128,512]{1,0:T(8,128)(2,1)S(1)}, bf16[128,512]{1,0:T(8,128)(2,1)}, u32[]{:S(2)}) copy-start(bf16[128,512]{1,0:T(8,128)(2,1)} %x_ref.3) | copy-start | bytes 393220
  14.6 0.9 %copy-start.10 = (bf16[128,512]{1,0:T(8,128)(2,1)S(1)}, bf16[128,512]{1,0:T(8,128)(2,1)}, u32[]{:S(2)}) copy-start(bf16[128,512]{1,0:T(8,128)(2,1)} %refs_12_.1) | copy-start | bytes 393220
  15.5 1.0 %copy-start.1 = (bf16[512,512]{1,0:T(8,128)(2,1)S(1)}, bf16[512,512]{1,0:T(8,128)(2,1)}, u32[]{:S(2)}) copy-start(bf16[512,512]{1,0:T(8,128)(2,1)} %wk_ref.3) | copy-start | bytes 1572868
  15.5 1.2 %copy-start.3 = (bf16[512,512]{1,0:T(8,128)(2,1)S(1)}, bf16[512,512]{1,0:T(8,128)(2,1)}, u32[]{:S(2)}) copy-start(bf16[512,512]{1,0:T(8,128)(2,1)} %wv_ref.3) | copy-start | bytes 1572868
  15.5 1.5 %copy-start.8 = (bf16[512,1024]{1,0:T(8,128)(2,1)S(1)}, bf16[512,1024]{1,0:T(8,128)(2,1)}, u32[]{:S(2)}) copy-start(bf16[512,1024]{1,0:T(8,128)(2,1)} %refs_16_.1) | copy-start | bytes 3145732
  15.5 1.7 %copy-start.9 = (bf16[512,512]{1,0:T(8,128)(2,1)S(1)}, bf16[512,512]{1,0:T(8,128)(2,1)}, u32[]{:S(2)}) copy-start(bf16[512,512]{1,0:T(8,128)(2,1)} %refs_15_.1) | copy-start | bytes 1572868
  17.2 14.3 %copy-start.5 = (bf16[1024,512]{1,0:T(8,128)(2,1)S(1)}, bf16[1024,512]{1,0:T(8,128)(2,1)}, u32[]{:S(2)}) copy-start(bf16[1024,512]{1,0:T(8,128)(2,1)} %wdown_ref.3) | copy-start | bytes 3145732
  23.0 8.4 %collective-permute-start.7 = (bf16[256,512]{1,0:T(8,128)(2,1)S(1)}, bf16[256,512]{1,0:T(8,128)(2,1)S(1)}, u32[]{:S(2)}, u32[]{:S(2)}) collective-permute-start(bf16[256,512]{1,0:T(8,128)(2,1)S(1)} %get-tuple-element.32), channel_id=1, source_target_pairs={{0,16},{8,24},{16,0},{24,8},{1,17},{9,25},{17,1},{25,9},{2,18},{10... | collective-permute-start | bytes 786440 | tf_op jit(solution)/shard_map/ppermute | solution.py:213
  23.6 9.3 %collective-permute-start.5 = (bf16[128,512]{1,0:T(8,128)(2,1)S(1)}, bf16[128,512]{1,0:T(8,128)(2,1)S(1)}, u32[]{:S(2)}, u32[]{:S(2)}) collective-permute-start(bf16[128,512]{1,0:T(8,128)(2,1)S(1)} %get-tuple-element.30), channel_id=1, source_target_pairs={{0,1},{1,0},{2,3},{3,2},{4,5},{5,4},{6,7},{7,6},{8,9},{9,8},{10,11... | collective-permute-start | bytes 393224 | tf_op jit(solution)/shard_map/ppermute | solution.py:275
  25.6 7.7 %collective-permute-start.6 = (bf16[128,512]{1,0:T(8,128)(2,1)S(1)}, bf16[128,512]{1,0:T(8,128)(2,1)S(1)}, u32[]{:S(2)}, u32[]{:S(2)}) collective-permute-start(bf16[128,512]{1,0:T(8,128)(2,1)S(1)} %get-tuple-element.31), channel_id=1, source_target_pairs={{1,2},{2,1},{3,4},{4,3},{5,6},{6,5},{7,0},{0,7},{9,10},{10,9},{11,... | collective-permute-start | bytes 393224 | tf_op jit(solution)/shard_map/ppermute | solution.py:274
  31.4 1.9 %collective-permute-start.8 = (bf16[128,512]{1,0:T(8,128)(2,1)S(1)}, bf16[128,512]{1,0:T(8,128)(2,1)S(1)}, u32[]{:S(2)}, u32[]{:S(2)}) collective-permute-start(bf16[128,512]{1,0:T(8,128)(2,1)S(1)} %add_convert_fusion), channel_id=1, source_target_pairs={{0,8},{8,0},{16,24},{24,16},{1,9},{9,1},{17,25},{25,17},{2,10},{10... | collective-permute-start | bytes 393224 | tf_op jit(solution)/shard_map/ppermute | solution.py:213

commit v2 on v1

v2 whole, which is shorter than its diff:
```python
import functools

import jax
import jax.numpy as jnp
from jax import lax
from jax.experimental import pallas as pl
from jax.experimental.pallas import tpu as pltpu
from jax.sharding import PartitionSpec as P

H = 8
HEAD = 64
EPS = 1e-05
SCALE = HEAD ** (-0.5)
PAIR = 2 * HEAD
GELU_C = 0.7978845608028654
GELU_A = 0.044715
MIB = 1 << 20

f32 = jnp.float32
bf16 = jnp.bfloat16


def dot(a, b):
    return jnp.dot(a, b, preferred_element_type=f32)


def dot_t(a, b):
    return lax.dot_general(a, b, (((1,), (1,)), ((), ())), preferred_element_type=f32)


def t_dot(a, b):
    return lax.dot_general(a, b, (((0,), (0,)), ((), ())), preferred_element_type=f32)


def normalize(values):
    mean_v = jnp.mean(values, axis=-1, keepdims=True)
    centered = values - mean_v
    inv_std = lax.rsqrt(jnp.mean(centered * centered, axis=-1, keepdims=True) + EPS)
    return (centered * inv_std, inv_std)


def normalize_back(unit, inv_std, upstream):
    return inv_std * (
        upstream
        - jnp.mean(upstream, axis=-1, keepdims=True)
        - unit * jnp.mean(upstream * unit, axis=-1, keepdims=True)
    )


def halves(rows):
    left = lax.broadcasted_iota(jnp.int32, rows.shape, 1) < HEAD
    zero = jnp.zeros_like(rows)
    return jnp.concatenate([jnp.where(left, rows, zero), jnp.where(left, zero, rows)], 0)


def unhalve(both):
    n = both.shape[1] // 2
    first, second = both[:, :n], both[:, n:]
    upper = lax.broadcasted_iota(jnp.int32, first.shape, 0) < HEAD
    return jnp.where(upper, first, second).T


def sent_slots(groups):
    return [range(1 << bit, groups, 2 << bit) for bit in range(groups.bit_length() - 1)]


def own_kernel(*refs):
    count = 8
    given, held = refs[:count], refs[count : 2 * count]
    q_ref, k_ref, v_ref, gact_ref, unit_ref, inv_ref, sem = refs[2 * count :]
    copies = [pltpu.make_async_copy(given[i], held[i], sem.at[i]) for i in range(count)]
    for copy in copies:
        copy.start()
    x_ref, cot_ref, wdown_ref, wk_ref, wv_ref, wq_ref = held[:6]
    copies[0].wait()
    unit, inv = normalize(x_ref[...].astype(f32))
    unit_ref[...] = unit
    inv_ref[...] = inv
    normed = unit.astype(bf16)
    copies[1].wait()
    copies[2].wait()
    gact_ref[...] = dot_t(cot_ref[...], wdown_ref[...])
    copies[3].wait()
    k_ref[...] = dot(normed, wk_ref[...]).astype(bf16)
    copies[4].wait()
    v_ref[...] = dot(normed, wv_ref[...]).astype(bf16)
    copies[5].wait()
    q_ref[...] = (dot(normed, wq_ref[...]) * SCALE).astype(bf16)
    copies[6].wait()
    copies[7].wait()


def pair_columns():
    return [(j, slice(j * PAIR, (j + 1) * PAIR)) for j in range(H // 2)]


def early_kernel(near_a, q_ref, k_ref, v_ref, wk_ref, wv_ref, ke_ref, ve_ref, se_ref):
    rows = q_ref.shape[0]
    unit, _ = normalize(near_a[...].astype(f32))
    normed = unit.astype(bf16)
    ke_ref[:rows, :] = k_ref[...]
    ve_ref[:rows, :] = v_ref[...]
    ke_ref[rows:, :] = dot(normed, wk_ref[...]).astype(bf16)
    ve_ref[rows:, :] = dot(normed, wv_ref[...]).astype(bf16)
    for j, cols in pair_columns():
        se_ref[j] = dot_t(ke_ref[:, cols], halves(q_ref[:, cols]))


def block_back(v, q2, g2, weights, inv, row):
    probs = weights * inv
    ds = (probs * (dot_t(v, g2) - row)).astype(bf16)
    return ds, dot(ds, q2).astype(bf16), dot(probs.astype(bf16), g2).astype(bf16)


def delta_row(delta, j):
    return jnp.concatenate([delta[2 * j : 2 * j + 1, :], delta[2 * j + 1 : 2 * j + 2, :]], 1)


def main_kernel(groups, listed, *refs):
    experts_ref = refs[0]
    slots = refs[1 : 1 + groups]
    (near_b, x_ref, ke_ref, ve_ref, se_ref, q_ref, gact_ref, cot_ref) = refs[1 + groups : 9 + groups]
    (wk_ref, wv_ref, wout_ref, wup_ref) = refs[9 + groups : 13 + groups]
    outs = refs[13 + groups :]
    bits = groups.bit_length() - 1
    sends = outs[:bits]
    (keep, w_ref, inv_ref, gmixed_ref, delta_ref, kb_ref, vb_ref, ds_ref, act_ref, resid_ref, gres_ref) = outs[
        bits : bits + 11
    ]
    picked_s, mixed_s, gk_s, gv_s = outs[bits + 11 :]
    rows, width = x_ref.shape
    early = 2 * rows
    place = lax.axis_index("blk")
    picked = [experts_ref[0, e] ^ place for e in range(listed)]
    for e in range(listed):
        for i in range(groups):

            @pl.when(picked[e] == i)
            def _(e=e, i=i):
                picked_s[(1 + e) * rows : (2 + e) * rows, :] = slots[i][...]

    picked_s[:rows, :] = near_b[...]
    unit, _ = normalize(picked_s[...].astype(f32))
    normed = unit.astype(bf16)
    kb_ref[...] = dot(normed, wk_ref[...]).astype(bf16)
    vb_ref[...] = dot(normed, wv_ref[...]).astype(bf16)
    for j, cols in pair_columns():
        last = dot_t(kb_ref[:, cols], halves(q_ref[:, cols]))
        first = se_ref[j]
        top = jnp.maximum(jnp.max(first, axis=0, keepdims=True), jnp.max(last, axis=0, keepdims=True))
        first = jnp.exp(first - top)
        last = jnp.exp(last - top)
        inv = 1.0 / (jnp.sum(first, axis=0, keepdims=True) + jnp.sum(last, axis=0, keepdims=True))
        w_ref[j, :early, :] = first
        w_ref[j, early:, :] = last
        inv_ref[j] = inv
        mixed = t_dot(ve_ref[:, cols], first.astype(bf16)) + t_dot(vb_ref[:, cols], last.astype(bf16))
        mixed_s[:, cols] = unhalve(mixed * inv).astype(bf16)

    mixed = mixed_s[...]
    resid = x_ref[...].astype(f32) + dot(mixed, wout_ref[...])
    resid_ref[...] = resid
    unit2, inv2 = normalize(resid)
    pre = dot(unit2.astype(bf16), wup_ref[...])
    square = pre * pre
    tanh = jnp.tanh(GELU_C * pre * (1.0 + GELU_A * square))
    act_ref[...] = (0.5 * pre * (1.0 + tanh)).astype(bf16)
    slope = 0.5 * (1.0 + tanh) + (0.5 * GELU_C) * pre * (1.0 - tanh * tanh) * (
        1.0 + (3.0 * GELU_A) * square
    )
    gpre = (gact_ref[...] * slope).astype(bf16)
    gres = cot_ref[...].astype(f32) + normalize_back(unit2, inv2, dot_t(gpre, wup_ref[...]))
    gres_ref[...] = gres
    gmixed = dot_t(gres.astype(bf16), wout_ref[...]).astype(bf16)
    gmixed_ref[...] = gmixed
    prod = gmixed.astype(f32) * mixed.astype(f32)
    high = prod.astype(bf16)
    low = (prod - high.astype(f32)).astype(bf16)
    head_of = lax.broadcasted_iota(jnp.int32, (H, width), 1) // HEAD
    ones = (head_of == lax.broadcasted_iota(jnp.int32, (H, width), 0)).astype(bf16)
    delta = dot_t(ones, high) + dot_t(ones, low)
    delta_ref[...] = delta

    for j, cols in pair_columns():
        ds_ref[j], gk_s[:, cols], gv_s[:, cols] = block_back(
            vb_ref[rows:, cols],
            halves(q_ref[:, cols]),
            halves(gmixed[:, cols]),
            w_ref[j, early + rows :, :],
            inv_ref[j],
            delta_row(delta, j),
        )
    parts = dot_t(gk_s[...], wk_ref[...]) + dot_t(gv_s[...], wv_ref[...])

    def far(slot):
        total = jnp.zeros((rows, width), f32)
        for e in range(listed):
            total = total + jnp.where(picked[e] == slot, parts[e * rows : (e + 1) * rows], 0.0)
        return total

    keep[...] = far(0)
    for bit, slots_sent in enumerate(sent_slots(groups)):
        for i, slot in enumerate(slots_sent):
            sends[bit][i * rows : (i + 1) * rows, :] = far(slot).astype(bf16)


def near_kernel(
    w_ref, inv_ref, delta_ref, gmixed_ref, q_ref, ve_ref, vb_ref, wk_ref, wv_ref, send_a, send_b, ds_ref, gk_s, gv_s
):
    rows = send_a.shape[0]
    delta = delta_ref[...]
    for j, cols in pair_columns():
        ds_ref[j], gk_s[:, cols], gv_s[:, cols] = block_back(
            jnp.concatenate([ve_ref[rows:, cols], vb_ref[:rows, cols]], 0),
            halves(q_ref[:, cols]),
            halves(gmixed_ref[:, cols]),
            w_ref[j, rows : 3 * rows, :],
            inv_ref[j],
            delta_row(delta, j),
        )
    parts = dot_t(gk_s[...], wk_ref[...]) + dot_t(gv_s[...], wv_ref[...])
    send_a[...] = parts[:rows].astype(bf16)
    send_b[...] = parts[rows:].astype(bf16)


def rest_kernel(*refs):
    (w_ref, inv_ref, delta_ref, gmixed_ref, q_ref, ke_ref, ve_ref, kb_ref, far_ref, near_ref) = refs[:10]
    (keep_ref, act_ref, resid_ref, wq_ref, wk_ref, wv_ref, wdown_ref, out_ref, acc_ref) = refs[10:19]
    gq_s, gk_s, gv_s = refs[19:]
    rows = q_ref.shape[0]
    delta = delta_ref[...]
    for j, cols in pair_columns():
        ds, gk_s[:, cols], gv_s[:, cols] = block_back(
            ve_ref[:rows, cols],
            halves(q_ref[:, cols]),
            halves(gmixed_ref[:, cols]),
            w_ref[j, :rows, :],
            inv_ref[j],
            delta_row(delta, j),
        )
        total = t_dot(ke_ref[:rows, cols], ds) + t_dot(ke_ref[rows:, cols], near_ref[j, :rows])
        total = total + t_dot(kb_ref[:rows, cols], near_ref[j, rows:]) + t_dot(kb_ref[rows:, cols], far_ref[j])
        gq_s[:, cols] = (unhalve(total) * SCALE).astype(bf16)
    acc_ref[...] = (
        keep_ref[...] + dot_t(gq_s[...], wq_ref[...]) + dot_t(gk_s[...], wk_ref[...]) + dot_t(gv_s[...], wv_ref[...])
    )
    out_ref[...] = (resid_ref[...] + dot(act_ref[...], wdown_ref[...])).astype(bf16)


def last_kernel(unit_ref, inv_ref, gres_ref, acc_ref, *refs):
    out_ref = refs[-1]
    rows = unit_ref.shape[0]
    total = acc_ref[...]
    for part in refs[:-1]:
        total = total + part[:rows, :].astype(f32)
    out_ref[...] = (gres_ref[...] + normalize_back(unit_ref[...], inv_ref[...], total)).astype(bf16)


def call(kernel, outs, args, scratch=(), flops=0, smem=0, space=pltpu.VMEM):
    whole = pl.BlockSpec(memory_space=pltpu.VMEM)
    small = pl.BlockSpec(memory_space=pltpu.SMEM)
    return pl.pallas_call(
        kernel,
        out_shape=[jax.ShapeDtypeStruct(shape, dtype) for shape, dtype in outs],
        in_specs=[small] * smem + [pl.BlockSpec(memory_space=space)] * (len(args) - smem),
        out_specs=[whole] * len(outs),
        scratch_shapes=list(scratch),
        compiler_params=pltpu.CompilerParams(vmem_limit_bytes=40 * MIB),
        cost_estimate=pl.CostEstimate(flops=flops, bytes_accessed=4 * MIB, transcendentals=0),
    )(*args)


def on_device(nodes, experts_list, w_query, w_key, w_value, w_out, w_up, w_down, cotangent):
    rows, width = nodes.shape
    hidden = w_up.shape[1]
    groups = lax.axis_size("blk")
    domains = lax.axis_size("dom")
    listed = experts_list.shape[1]
    bits = groups.bit_length() - 1

    def across(array, bit):
        return lax.ppermute(array, "blk", [(i, i ^ (1 << bit)) for i in range(groups)])

    pairs_a = [(i, i ^ 1) for i in range(domains)]
    pairs_b = []
    for i in range(1, domains, 2):
        pairs_b += [(i, (i + 1) % domains), ((i + 1) % domains, i)]

    held = {0: nodes}
    top = bits - 1
    held[1 << top] = across(nodes, top)
    near_a = lax.ppermute(nodes, "dom", pairs_a)
    near_b = lax.ppermute(nodes, "dom", pairs_b)
    for bit in range(top - 1, -1, -1):
        for slot in list(held):
            held[slot | (1 << bit)] = across(held[slot], bit)

    given = [nodes, cotangent, w_down, w_key, w_value, w_query, w_out, w_up]
    *given, q, k, v, gact, unit, inv_std = call(
        own_kernel,
        [(array.shape, bf16) for array in given]
        + [((rows, width), bf16)] * 3
        + [((rows, hidden), f32), ((rows, width), f32), ((rows, 1), f32)],
        [pltpu.with_memory_space_constraint(array, pltpu.HBM) for array in given],
        [pltpu.SemaphoreType.DMA((len(given),))],
        flops=2 * rows * width * (3 * width + hidden),
        space=pltpu.HBM,
    )
    x, cotangent, w_down, w_key, w_value, w_query, w_out, w_up = given
    held[0] = x
    early = 2 * rows
    late = (1 + listed) * rows
    keys = early + late
    ke, ve, se = call(
        early_kernel,
        [((early, width), bf16)] * 2 + [((H // 2, early, 2 * rows), f32)],
        [near_a, q, k, v, w_key, w_value],
        flops=2 * early * width * (2 * width + 2 * rows),
    )
    sent = sent_slots(groups)
    outs = call(
        functools.partial(main_kernel, groups, listed),
        [((len(slots) * rows, width), bf16) for slots in sent]
        + [((rows, width), f32), ((H // 2, keys, 2 * rows), f32), ((H // 2, 1, 2 * rows), f32)]
        + [((rows, width), bf16), ((H, rows), f32), ((late, width), bf16), ((late, width), bf16)]
        + [((H // 2, listed * rows, 2 * rows), bf16), ((rows, hidden), bf16)]
        + [((rows, width), f32)] * 2,
        [experts_list] + [held[slot] for slot in range(groups)] + [near_b, x, ke, ve, se, q, gact, cotangent, w_key, w_value, w_out, w_up],
        [pltpu.VMEM((late, width), bf16), pltpu.VMEM((rows, width), bf16)]
        + [pltpu.VMEM((listed * rows, width), bf16)] * 2,
        flops=2 * rows * width * (6 * keys + 4 * hidden),
        smem=1,
    )
    sends = outs[:bits]
    keep, w, inv, gmixed, delta, kb, vb, ds_far, act, resid, gres = outs[bits:]
    received = [across(sends[0], 0)]
    send_a, send_b, ds_near = call(
        near_kernel,
        [((rows, width), bf16)] * 2 + [((H // 2, 2 * rows, 2 * rows), bf16)],
        [w, inv, delta, gmixed, q, ve, vb, w_key, w_value],
        [pltpu.VMEM((2 * rows, width), bf16)] * 2,
        flops=8 * rows * width * (width + 6 * rows),
    )
    from_b = lax.ppermute(send_b, "dom", pairs_b)
    from_a = lax.ppermute(send_a, "dom", pairs_a)
    for bit in range(1, bits):
        total = sends[bit].astype(f32)
        for lower, array in enumerate(received):
            blocks = array.reshape(-1, rows, width)[(1 << bit) >> (lower + 1) :: (2 << bit) >> (lower + 1)]
            total = total + blocks.reshape(-1, width).astype(f32)
        received.append(across(total.astype(bf16), bit))

    layer_out, acc = call(
        rest_kernel,
        [((rows, width), bf16), ((rows, width), f32)],
        [w, inv, delta, gmixed, q, ke, ve, kb, ds_far, ds_near, keep, act, resid, w_query, w_key, w_value, w_down],
        [pltpu.VMEM((rows, width), bf16)] * 3,
        flops=2 * rows * width * (3 * width + hidden + 8 * rows),
    )
    (grad_nodes,) = call(
        last_kernel,
        [((rows, width), bf16)],
        [unit, inv_std, gres, acc, from_a, from_b] + received,
    )
    return (layer_out, grad_nodes)


def solution(mesh):
    split = P(("blk", "dom"), None)
    return jax.shard_map(
        on_device,
        mesh=mesh,
        in_specs=(split, split, P(), P(), P(), P(), P(), P(), split),
        out_specs=(split, split),
        check_vma=False,
    )
```

time: 34.6 us -> 29.8 us (0.86)
  local copies, waits for them, and re-layouts: 6.92 us -> 0 us
  Pallas kernels: 9.08 us -> 11.8 us
  starting transfers between devices: 13.7 us -> 13.2 us
    unnamed x22 -> x0, local copies, waits for them, and re-layouts: 6.92 us -> none
    pallas_call x4 -> x6, Pallas kernels: 9.08 us -> 11.8 us  [call(): pl.pallas_call(kernel, out_shape=[jax.ShapeDtypeStruct(shape, dtype) for...]
    ppermute x5, waiting for transfers between devices: 2.86 us -> 0.65 us  [across(): lax.ppermute(array, 'blk', [(i, i ^ 1 << bit) for i in range(groups)])]
    ppermute x1, starting transfers between devices: 2.02 us -> 0.07 us  [on_device(): from_a = lax.ppermute(send_a, 'dom', pairs_a)]
    ppermute x1, starting transfers between devices: 0.01 us -> 1.52 us  [on_device(): near_a = lax.ppermute(nodes, 'dom', pairs_a)]
    ppermute x1, waiting for transfers between devices: 0.34 us -> 1.51 us  [on_device(): from_b = lax.ppermute(send_b, 'dom', pairs_b)]
    ppermute x1, waiting for transfers between devices: 0.01 us -> 1.11 us  [on_device(): near_b = lax.ppermute(nodes, 'dom', pairs_b)]
    ppermute x1, starting transfers between devices: 4.56 us -> 3.54 us  [on_device(): near_b = lax.ppermute(nodes, 'dom', pairs_b)]
  transfers between devices with their start and end apart: 9 -> 9, of which waited for: 2 -> 3; matrix products, arithmetic and copies ran while one was open for 0% -> 0% of each run, Pallas kernels for 7% -> 23%
where the time goes in v2:
time: 29.8 us; the launch traced here: 29.6 us
  starting transfers between devices  13.2 us (44%)
  Pallas kernels  11.8 us (40%)
  waiting for transfers between devices  3.27 us (11%)
  between operations  1.35 us (5%)
    pallas_call x6, Pallas kernels, call(): pl.pallas_call(kernel, out_shape=[jax.ShapeDtypeStruct(shape, dtype) for...  11.8 us
    ppermute x5, starting transfers between devices, across(): lax.ppermute(array, 'blk', [(i, i ^ 1 << bit) for i in range(groups)])  4.41 us
    ppermute x1, starting transfers between devices, on_device(): from_b = lax.ppermute(send_b, 'dom', pairs_b)  3.61 us
    ppermute x1, starting transfers between devices, on_device(): near_b = lax.ppermute(nodes, 'dom', pairs_b)  3.54 us
    ppermute x1, starting transfers between devices, on_device(): near_a = lax.ppermute(nodes, 'dom', pairs_a)  1.52 us
    ppermute x1, waiting for transfers between devices, on_device(): from_b = lax.ppermute(send_b, 'dom', pairs_b)  1.51 us
    ppermute x1, waiting for transfers between devices, on_device(): near_b = lax.ppermute(nodes, 'dom', pairs_b)  1.11 us
    ppermute x5, waiting for transfers between devices, across(): lax.ppermute(array, 'blk', [(i, i ^ 1 << bit) for i in range(groups)])  0.65 us
  transfers between devices with their start and end apart: 9, of which 3 were waited for; matrix products, arithmetic and copies ran while one was open for 0% of the time, Pallas kernels for 23%

profile of v2, /device:TPU:0, one launch (start us, length us, event | category | flops | bytes accessed | tf_op | source)
XLA Modules:
  0.0 29.6 jit_solution(13341853404462239069)
XLA Ops:
  0.6 3.0 %collective-permute-start.1 = (bf16[128,512]{1,0:T(8,128)(2,1)}, bf16[128,512]{1,0:T(8,128)(2,1)S(1)}, u32[]{:S(2)}, u32[]{:S(2)}) collective-permute-start(bf16[128,512]{1,0:T(8,128)(2,1)} %refs_0_.2), channel_id=1, source_target_pairs={{0,16},{8,24},{16,0},{24,8},{1,17},{9,25},{17,1},{25,9},{2,18},{10... | collective-permute-start | bytes 393224 | tf_op jit(solution)/shard_map/ppermute | solution.py:282
  3.6 1.5 %collective-permute-start.4 = (bf16[128,512]{1,0:T(8,128)(2,1)}, bf16[128,512]{1,0:T(8,128)(2,1)S(1)}, u32[]{:S(2)}, u32[]{:S(2)}) collective-permute-start(bf16[128,512]{1,0:T(8,128)(2,1)} %refs_0_.2), channel_id=1, source_target_pairs={{0,1},{1,0},{2,3},{3,2},{4,5},{5,4},{6,7},{7,6},{8,9},{9,8},{10,11... | collective-permute-start | bytes 393224 | tf_op jit(solution)/shard_map/ppermute | solution.py:292
  5.2 0.0 collective-permute-start
  5.2 3.5 %collective-permute-start.3 = (bf16[128,512]{1,0:T(8,128)(2,1)}, bf16[128,512]{1,0:T(8,128)(2,1)S(1)}, u32[]{:S(2)}, u32[]{:S(2)}) collective-permute-start(bf16[128,512]{1,0:T(8,128)(2,1)} %refs_0_.2), channel_id=1, source_target_pairs={{1,2},{2,1},{3,4},{4,3},{5,6},{6,5},{7,0},{0,7},{9,10},{10,9},{11,... | collective-permute-start | bytes 393224 | tf_op jit(solution)/shard_map/ppermute | solution.py:293
  8.7 0.0 collective-permute-done.1.refs_3_
  8.7 0.2 collective-permute-start.2
  9.6 2.6 %shard_map.104 = (bf16[128,512]{1,0:T(8,128)(2,1)S(1)}, bf16[128,512]{1,0:T(8,128)(2,1)S(1)}, bf16[1024,512]{1,0:T(8,128)(2,1)S(1)}, bf16[512,512]{1,0:T(8,128)(...) custom-call(bf16[128,512]{1,0:T(8,128)(2,1)} %refs_0_.2, ...), custom_call_target="tpu_custom_call" | custom-call | flops 335544320 | bytes 4194304 | tf_op jit(solution)/shard_map/pallas_call | solution.py:262
  12.2 0.0 collective-permute-done.4.near_a
  12.2 0.6 %shard_map.105 = (bf16[256,512]{1,0:T(8,128)(2,1)S(1)}, bf16[256,512]{1,0:T(8,128)(2,1)S(1)}, f32[4,256,256]{2,1,0:T(8,128)S(1)}) custom-call(bf16[128,512]{1,0:T(8,128)(2,1)S(1)} %collective-permute-done.4.near_a, bf16[128,512]{1,0:T(8,128)(2,1)S(1)} %get-tuple-element.38.q_ref.refs_10_.refs_4_, bf16[128,512]{1,0:T(8,128)(2,1)S(1)} %get-tuple-element.39.k_ref, ...), custom_call_target="tpu_custom_call" | custom-call | flops 335544320 | bytes 4194304 | tf_op jit(solution)/shard_map/pallas_call | solution.py:262
  12.9 0.0 collective-permute-done.refs_2_
  12.9 1.1 %collective-permute-done.3.refs_5_ = bf16[128,512]{1,0:T(8,128)(2,1)S(1)} collective-permute-done((bf16[128,512]{1,0:T(8,128)(2,1)}, bf16[128,512]{1,0:T(8,128)(2,1)S(1)}, u32[]{:S(2)}, u32[]{:S(2)}) %collective-permute-start.3) | collective-permute-done | bytes 131104 | tf_op jit(solution)/shard_map/ppermute | solution.py:293
  14.0 0.0 collective-permute-done.2.refs_4_
  14.0 4.1 %shard_map.106 = (bf16[256,512]{1,0:T(8,128)(2,1)S(1)}, bf16[128,512]{1,0:T(8,128)(2,1)S(1)}, f32[128,512]{1,0:T(8,128)S(1)}, f32[4,512,256]{2,1,0:T(8,128)S(1)}...) custom-call(s32[1,1]{1,0:T(1,128)S(6)} %copy.11.refs_0_, ...), custom_call_target="tpu_custom_call" | custom-call | flops 939524096 | bytes 4194304 | tf_op jit(solution)/shard_map/pallas_call | solution.py:262
  18.0 0.1 collective-permute-start.7
  18.1 1.2 %shard_map.107 = (bf16[128,512]{1,0:T(8,128)(2,1)S(1)}, bf16[128,512]{1,0:T(8,128)(2,1)S(1)}, bf16[4,256,256]{2,1,0:T(8,128)(2,1)S(1)}) custom-call(f32[4,512,256]{2,1,0:T(8,128)S(1)} %get-tuple-element.50.w_ref.refs_0_, f32[4,1,256]{2,1,0:T(1,128)S(1)} %get-tuple-element.51.inv_ref.refs_1_, f32[8,128]{1,0:T(8,128)S(1)} %get-tuple-element.52.delta_ref.refs_2_, ...), custom_call_target="tpu_custom_call" | custom-call | flops 671088640 | bytes 4194304 | tf_op jit(solution)/shard_map/pallas_call | solution.py:262
  19.3 0.1 collective-permute-start.5
  19.4 3.6 %collective-permute-start.6 = (bf16[128,512]{1,0:T(8,128)(2,1)S(1)}, bf16[128,512]{1,0:T(8,128)(2,1)S(1)}, u32[]{:S(2)}, u32[]{:S(2)}) collective-permute-start(bf16[128,512]{1,0:T(8,128)(2,1)S(1)} %get-tuple-element.69), channel_id=1, source_target_pairs={{1,2},{2,1},{3,4},{4,3},{5,6},{6,5},{7,0},{0,7},{9,10},{10,9},{11,... | collective-permute-start | bytes 393224 | tf_op jit(solution)/shard_map/ppermute | solution.py:344
  23.0 0.0 collective-permute-done.7.refs_2_
  23.0 1.1 %collective-permute-start.8 = (bf16[128,512]{1,0:T(8,128)(2,1)S(1)}, bf16[128,512]{1,0:T(8,128)(2,1)S(1)}, u32[]{:S(2)}, u32[]{:S(2)}) collective-permute-start(bf16[128,512]{1,0:T(8,128)(2,1)S(1)} %add_convert_fusion), channel_id=1, source_target_pairs={{0,16},{8,24},{16,0},{24,8},{1,17},{9,25},{17,1},{25,9},{2,18},{10... | collective-permute-start | bytes 393224 | tf_op jit(solution)/shard_map/ppermute | solution.py:282
  24.1 2.4 %shard_map.108 = (bf16[128,512]{1,0:T(8,128)(2,1)}, f32[128,512]{1,0:T(8,128)S(1)}) custom-call(f32[4,512,256]{2,1,0:T(8,128)S(1)} %get-tuple-element.50.w_ref.refs_0_, f32[4,1,256]{2,1,0:T(1,128)S(1)} %get-tuple-element.51.inv_ref.refs_1_, f32[8,128]{1,0:T(8,128)S(1)} %get-tuple-element.52.delta_ref.refs_2_, ...), custom_call_target="tpu_custom_call" | custom-call | flops 469762048 | bytes 4194304 | tf_op jit(solution)/shard_map/pallas_call | solution.py:262
  26.5 0.0 collective-permute-done.5.refs_0_
  26.5 1.5 %collective-permute-done.6.refs_1_ = bf16[128,512]{1,0:T(8,128)(2,1)S(1)} collective-permute-done((bf16[128,512]{1,0:T(8,128)(2,1)S(1)}, bf16[128,512]{1,0:T(8,128)(2,1)S(1)}, u32[]{:S(2)}, u32[]{:S(2)}) %collective-permute-start.6) | collective-permute-done | bytes 131104 | tf_op jit(solution)/shard_map/ppermute | solution.py:344
  28.1 0.6 %collective-permute-done.8.refs_3_ = bf16[128,512]{1,0:T(8,128)(2,1)S(1)} collective-permute-done((bf16[128,512]{1,0:T(8,128)(2,1)S(1)}, bf16[128,512]{1,0:T(8,128)(2,1)S(1)}, u32[]{:S(2)}, u32[]{:S(2)}) %collective-permute-start.8) | collective-permute-done | bytes 131104 | tf_op jit(solution)/shard_map/ppermute | solution.py:282
  28.7 0.9 %shard_map.109 = bf16[128,512]{1,0:T(8,128)(2,1)} custom-call(f32[128,512]{1,0:T(8,128)S(1)} %get-tuple-element.64.unit_ref, f32[128,1]{1,0:T(8,128)S(1)} %get-tuple-element.65.inv_ref, f32[128,512]{1,0:T(8,128)S(1)} %get-tuple-element.66.gres_ref, f32[128,512]{1,0:T(8,128)S(1)} %get-tuple-element.67.acc_ref, ...), custom_call_target="tpu_custom_call" | custom-call | bytes 4194304 | tf_op jit(solution)/shard_map/pallas_call | solution.py:262
  (1 shorter events, 0.0 us)
Async XLA Ops:
  0.6 8.1 %collective-permute-start.1 = (bf16[128,512]{1,0:T(8,128)(2,1)}, bf16[128,512]{1,0:T(8,128)(2,1)S(1)}, u32[]{:S(2)}, u32[]{:S(2)}) collective-permute-start(bf16[128,512]{1,0:T(8,128)(2,1)} %refs_0_.2), channel_id=1, source_target_pairs={{0,16},{8,24},{16,0},{24,8},{1,17},{9,25},{17,1},{25,9},{2,18},{10... | collective-permute-start | bytes 393224 | tf_op jit(solution)/shard_map/ppermute | solution.py:282
  3.6 8.6 %collective-permute-start.4 = (bf16[128,512]{1,0:T(8,128)(2,1)}, bf16[128,512]{1,0:T(8,128)(2,1)S(1)}, u32[]{:S(2)}, u32[]{:S(2)}) collective-permute-start(bf16[128,512]{1,0:T(8,128)(2,1)} %refs_0_.2), channel_id=1, source_target_pairs={{0,1},{1,0},{2,3},{3,2},{4,5},{5,4},{6,7},{7,6},{8,9},{9,8},{10,11... | collective-permute-start | bytes 393224 | tf_op jit(solution)/shard_map/ppermute | solution.py:292
  5.2 7.7 %collective-permute-start = (bf16[128,512]{1,0:T(8,128)(2,1)}, bf16[128,512]{1,0:T(8,128)(2,1)S(1)}, u32[]{:S(2)}, u32[]{:S(2)}) collective-permute-start(bf16[128,512]{1,0:T(8,128)(2,1)} %refs_0_.2), channel_id=1, source_target_pairs={{0,8},{8,0},{16,24},{24,16},{1,9},{9,1},{17,25},{25,17},{2,10},{10... | collective-permute-start | bytes 393224 | tf_op jit(solution)/shard_map/ppermute | solution.py:282
  5.2 8.8 %collective-permute-start.3 = (bf16[128,512]{1,0:T(8,128)(2,1)}, bf16[128,512]{1,0:T(8,128)(2,1)S(1)}, u32[]{:S(2)}, u32[]{:S(2)}) collective-permute-start(bf16[128,512]{1,0:T(8,128)(2,1)} %refs_0_.2), channel_id=1, source_target_pairs={{1,2},{2,1},{3,4},{4,3},{5,6},{6,5},{7,0},{0,7},{9,10},{10,9},{11,... | collective-permute-start | bytes 393224 | tf_op jit(solution)/shard_map/ppermute | solution.py:293
  8.7 5.3 %collective-permute-start.2 = (bf16[128,512]{1,0:T(8,128)(2,1)S(1)}, bf16[128,512]{1,0:T(8,128)(2,1)S(1)}, u32[]{:S(2)}, u32[]{:S(2)}) collective-permute-start(bf16[128,512]{1,0:T(8,128)(2,1)S(1)} %collective-permute-done.1.refs_3_), channel_id=1, source_target_pairs={{0,8},{8,0},{16,24},{24,16},{1,9},{9,1},{17,25},{25,17},{2,10},{10... | collective-permute-start | bytes 393224 | tf_op jit(solution)/shard_map/ppermute | solution.py:282
  18.0 4.9 %collective-permute-start.7 = (bf16[256,512]{1,0:T(8,128)(2,1)S(1)}, bf16[256,512]{1,0:T(8,128)(2,1)S(1)}, u32[]{:S(2)}, u32[]{:S(2)}) collective-permute-start(bf16[256,512]{1,0:T(8,128)(2,1)S(1)} %get-tuple-element.70), channel_id=1, source_target_pairs={{0,8},{8,0},{16,24},{24,16},{1,9},{9,1},{17,25},{25,17},{2,10},{10... | collective-permute-start | bytes 786440 | tf_op jit(solution)/shard_map/ppermute | solution.py:282
  19.3 7.3 %collective-permute-start.5 = (bf16[128,512]{1,0:T(8,128)(2,1)S(1)}, bf16[128,512]{1,0:T(8,128)(2,1)S(1)}, u32[]{:S(2)}, u32[]{:S(2)}) collective-permute-start(bf16[128,512]{1,0:T(8,128)(2,1)S(1)} %get-tuple-element.68), channel_id=1, source_target_pairs={{0,1},{1,0},{2,3},{3,2},{4,5},{5,4},{6,7},{7,6},{8,9},{9,8},{10,11... | collective-permute-start | bytes 393224 | tf_op jit(solution)/shard_map/ppermute | solution.py:345
  19.4 8.7 %collective-permute-start.6 = (bf16[128,512]{1,0:T(8,128)(2,1)S(1)}, bf16[128,512]{1,0:T(8,128)(2,1)S(1)}, u32[]{:S(2)}, u32[]{:S(2)}) collective-permute-start(bf16[128,512]{1,0:T(8,128)(2,1)S(1)} %get-tuple-element.69), channel_id=1, source_target_pairs={{1,2},{2,1},{3,4},{4,3},{5,6},{6,5},{7,0},{0,7},{9,10},{10,9},{11,... | collective-permute-start | bytes 393224 | tf_op jit(solution)/shard_map/ppermute | solution.py:344
  23.0 5.7 %collective-permute-start.8 = (bf16[128,512]{1,0:T(8,128)(2,1)S(1)}, bf16[128,512]{1,0:T(8,128)(2,1)S(1)}, u32[]{:S(2)}, u32[]{:S(2)}) collective-permute-start(bf16[128,512]{1,0:T(8,128)(2,1)S(1)} %add_convert_fusion), channel_id=1, source_target_pairs={{0,16},{8,24},{16,0},{24,8},{1,17},{9,25},{17,1},{25,9},{2,18},{10... | collective-permute-start | bytes 393224 | tf_op jit(solution)/shard_map/ppermute | solution.py:282

commit v3 on v2

v3 whole, which is shorter than its diff:
```python
import functools

import jax
import jax.numpy as jnp
from jax import lax
from jax.experimental import pallas as pl
from jax.experimental.pallas import tpu as pltpu
from jax.sharding import PartitionSpec as P

H = 8
HEAD = 64
EPS = 1e-05
SCALE = HEAD ** (-0.5)
PAIR = 2 * HEAD
GELU_C = 0.7978845608028654
GELU_A = 0.044715
MIB = 1 << 20

f32 = jnp.float32
bf16 = jnp.bfloat16


def dot(a, b):
    return jnp.dot(a, b, preferred_element_type=f32)


def dot_t(a, b):
    return lax.dot_general(a, b, (((1,), (1,)), ((), ())), preferred_element_type=f32)


def t_dot(a, b):
    return lax.dot_general(a, b, (((0,), (0,)), ((), ())), preferred_element_type=f32)


def normalize(values):
    mean_v = jnp.mean(values, axis=-1, keepdims=True)
    centered = values - mean_v
    inv_std = lax.rsqrt(jnp.mean(centered * centered, axis=-1, keepdims=True) + EPS)
    return (centered * inv_std, inv_std)


def normalize_back(unit, inv_std, upstream):
    return inv_std * (
        upstream
        - jnp.mean(upstream, axis=-1, keepdims=True)
        - unit * jnp.mean(upstream * unit, axis=-1, keepdims=True)
    )


def halves(rows):
    left = lax.broadcasted_iota(jnp.int32, rows.shape, 1) < HEAD
    zero = jnp.zeros_like(rows)
    return jnp.concatenate([jnp.where(left, rows, zero), jnp.where(left, zero, rows)], 0)


def unhalve(both):
    n = both.shape[1] // 2
    first, second = both[:, :n], both[:, n:]
    upper = lax.broadcasted_iota(jnp.int32, first.shape, 0) < HEAD
    return jnp.where(upper, first, second).T


def sent_slots(groups):
    return [range(1 << bit, groups, 2 << bit) for bit in range(groups.bit_length() - 1)]


def fetch(given, held, sem):
    copies = [pltpu.make_async_copy(src, dst, sem.at[i]) for i, (src, dst) in enumerate(zip(given, held))]
    for copy in copies:
        copy.start()
    return copies


def own_kernel(*refs):
    given, held = refs[:5], refs[5:10]
    q_ref, k_ref, v_ref, unit_ref, inv_ref, sem = refs[10:]
    copies = fetch(given, held, sem)
    x_ref, wk_ref, wv_ref, wq_ref, _ = held
    copies[0].wait()
    unit, inv = normalize(x_ref[...].astype(f32))
    unit_ref[...] = unit
    inv_ref[...] = inv
    normed = unit.astype(bf16)
    copies[1].wait()
    k_ref[...] = dot(normed, wk_ref[...]).astype(bf16)
    copies[2].wait()
    v_ref[...] = dot(normed, wv_ref[...]).astype(bf16)
    copies[3].wait()
    q_ref[...] = (dot(normed, wq_ref[...]) * SCALE).astype(bf16)
    copies[4].wait()


def pair_columns():
    return [(j, slice(j * PAIR, (j + 1) * PAIR)) for j in range(H // 2)]


def early_kernel(
    near_a, q_ref, k_ref, v_ref, wk_ref, wv_ref, cot_ref, wdown_ref, ke_ref, ve_ref, se_ref, gact_ref
):
    rows = q_ref.shape[0]
    unit, _ = normalize(near_a[...].astype(f32))
    normed = unit.astype(bf16)
    ke_ref[:rows, :] = k_ref[...]
    ve_ref[:rows, :] = v_ref[...]
    ke_ref[rows:, :] = dot(normed, wk_ref[...]).astype(bf16)
    ve_ref[rows:, :] = dot(normed, wv_ref[...]).astype(bf16)
    for j, cols in pair_columns():
        se_ref[j] = dot_t(ke_ref[:, cols], halves(q_ref[:, cols]))
    gact_ref[...] = dot_t(cot_ref[...], wdown_ref[...])


def block_back(v, q2, g2, weights, inv, row):
    probs = weights * inv
    ds = (probs * (dot_t(v, g2) - row)).astype(bf16)
    return ds, dot(ds, q2).astype(bf16), dot(probs.astype(bf16), g2).astype(bf16)


def delta_row(delta, j):
    return jnp.concatenate([delta[2 * j : 2 * j + 1, :], delta[2 * j + 1 : 2 * j + 2, :]], 1)


def main_kernel(groups, listed, *refs):
    experts_ref = refs[0]
    slots = refs[1 : 1 + groups]
    (near_b, x_ref, ke_ref, ve_ref, se_ref, q_ref, wk_ref, wv_ref) = refs[1 + groups : 9 + groups]
    (wout_ref, wup_ref, cot_ref, gact_ref) = refs[9 + groups : 13 + groups]
    outs = refs[13 + groups :]
    (send_a, send_b, keep, w_ref, inv_ref, gmixed_ref, delta_ref, kb_ref, vb_ref, ds_ref) = outs[:10]
    (act_ref, resid_ref, gres_ref), outs = outs[10:13], outs[13:]
    bits = groups.bit_length() - 1
    sends = outs[:bits]
    normed_s, mixed_s, gk_s, gv_s = outs[bits:]
    rows, width = x_ref.shape
    early = 2 * rows
    place = lax.axis_index("blk")
    normed_s[:rows, :] = normalize(near_b[...].astype(f32))[0].astype(bf16)
    for e in range(listed):
        slot = experts_ref[:, e : e + 1] ^ place
        block = jnp.zeros((rows, width), f32)
        for i in range(groups):
            block = jnp.where(slot == i, slots[i][...].astype(f32), block)
        normed_s[(1 + e) * rows : (2 + e) * rows, :] = normalize(block)[0].astype(bf16)
    normed = normed_s[...]
    kb_ref[...] = dot(normed, wk_ref[...]).astype(bf16)
    vb_ref[...] = dot(normed, wv_ref[...]).astype(bf16)
    for j, cols in pair_columns():
        last = dot_t(kb_ref[:, cols], halves(q_ref[:, cols]))
        first = se_ref[j]
        top = jnp.maximum(jnp.max(first, axis=0, keepdims=True), jnp.max(last, axis=0, keepdims=True))
        first = jnp.exp(first - top)
        last = jnp.exp(last - top)
        inv = 1.0 / (jnp.sum(first, axis=0, keepdims=True) + jnp.sum(last, axis=0, keepdims=True))
        w_ref[j, :early, :] = first
        w_ref[j, early:, :] = last
        inv_ref[j] = inv
        mixed = t_dot(ve_ref[:, cols], first.astype(bf16)) + t_dot(vb_ref[:, cols], last.astype(bf16))
        mixed_s[:, cols] = unhalve(mixed * inv).astype(bf16)

    mixed = mixed_s[...]
    resid = x_ref[...].astype(f32) + dot(mixed, wout_ref[...])
    resid_ref[...] = resid
    unit2, inv2 = normalize(resid)
    pre = dot(unit2.astype(bf16), wup_ref[...])
    square = pre * pre
    tanh = jnp.tanh(GELU_C * pre * (1.0 + GELU_A * square))
    act_ref[...] = (0.5 * pre * (1.0 + tanh)).astype(bf16)
    slope = 0.5 * (1.0 + tanh) + (0.5 * GELU_C) * pre * (1.0 - tanh * tanh) * (
        1.0 + (3.0 * GELU_A) * square
    )
    gpre = (gact_ref[...] * slope).astype(bf16)
    gres = cot_ref[...].astype(f32) + normalize_back(unit2, inv2, dot_t(gpre, wup_ref[...]))
    gres_ref[...] = gres
    gmixed = dot_t(gres.astype(bf16), wout_ref[...]).astype(bf16)
    gmixed_ref[...] = gmixed
    prod = gmixed.astype(f32) * mixed.astype(f32)
    high = prod.astype(bf16)
    low = (prod - high.astype(f32)).astype(bf16)
    head_of = lax.broadcasted_iota(jnp.int32, (H, width), 1) // HEAD
    ones = (head_of == lax.broadcasted_iota(jnp.int32, (H, width), 0)).astype(bf16)
    delta = dot_t(ones, high) + dot_t(ones, low)
    delta_ref[...] = delta

    for j, cols in pair_columns():
        ds_ref[j], gk_s[:, cols], gv_s[:, cols] = block_back(
            jnp.concatenate([ve_ref[rows:, cols], vb_ref[:, cols]], 0),
            halves(q_ref[:, cols]),
            halves(gmixed[:, cols]),
            w_ref[j, rows:, :],
            inv_ref[j],
            delta_row(delta, j),
        )
    parts = dot_t(gk_s[...], wk_ref[...]) + dot_t(gv_s[...], wv_ref[...])
    send_a[...] = parts[:rows].astype(bf16)
    send_b[...] = parts[rows : 2 * rows].astype(bf16)
    picked = [experts_ref[:, e : e + 1] ^ place for e in range(listed)]

    def far(slot):
        total = jnp.zeros((rows, width), f32)
        for e in range(listed):
            total = total + jnp.where(picked[e] == slot, parts[(2 + e) * rows : (3 + e) * rows], 0.0)
        return total

    keep[...] = far(0)
    for bit, slots_sent in enumerate(sent_slots(groups)):
        for i, slot in enumerate(slots_sent):
            sends[bit][i * rows : (i + 1) * rows, :] = far(slot).astype(bf16)


def rest_kernel(*refs):
    (w_ref, inv_ref, delta_ref, gmixed_ref, q_ref, ke_ref, ve_ref, kb_ref, ds_ref) = refs[:9]
    (keep_ref, act_ref, resid_ref, wq_ref, wk_ref, wv_ref, wdown_ref, out_ref, acc_ref) = refs[9:18]
    gq_s, gk_s, gv_s = refs[18:]
    rows = q_ref.shape[0]
    delta = delta_ref[...]
    for j, cols in pair_columns():
        ds, gk_s[:, cols], gv_s[:, cols] = block_back(
            ve_ref[:rows, cols],
            halves(q_ref[:, cols]),
            halves(gmixed_ref[:, cols]),
            w_ref[j, :rows, :],
            inv_ref[j],
            delta_row(delta, j),
        )
        total = t_dot(ke_ref[:rows, cols], ds) + t_dot(ke_ref[rows:, cols], ds_ref[j, :rows, :])
        total = total + t_dot(kb_ref[:, cols], ds_ref[j, rows:, :])
        gq_s[:, cols] = (unhalve(total) * SCALE).astype(bf16)
    acc_ref[...] = (
        keep_ref[...] + dot_t(gq_s[...], wq_ref[...]) + dot_t(gk_s[...], wk_ref[...]) + dot_t(gv_s[...], wv_ref[...])
    )
    out_ref[...] = (resid_ref[...] + dot(act_ref[...], wdown_ref[...])).astype(bf16)


def last_kernel(unit_ref, inv_ref, gres_ref, acc_ref, *refs):
    out_ref = refs[-1]
    rows = unit_ref.shape[0]
    total = acc_ref[...]
    for part in refs[:-1]:
        total = total + part[:rows, :].astype(f32)
    out_ref[...] = (gres_ref[...] + normalize_back(unit_ref[...], inv_ref[...], total)).astype(bf16)


def call(kernel, outs, args, scratch=(), flops=0, hbm=0):
    spaces = [pltpu.VMEM] * (len(args) - hbm) + [pltpu.HBM] * hbm
    return pl.pallas_call(
        kernel,
        out_shape=[jax.ShapeDtypeStruct(shape, dtype) for shape, dtype in outs],
        in_specs=[pl.BlockSpec(memory_space=space) for space in spaces],
        out_specs=[pl.BlockSpec(memory_space=pltpu.VMEM)] * len(outs),
        scratch_shapes=list(scratch),
        compiler_params=pltpu.CompilerParams(vmem_limit_bytes=40 * MIB),
        cost_estimate=pl.CostEstimate(flops=flops, bytes_accessed=4 * MIB, transcendentals=0),
    )(*args)


def on_device(nodes, experts_list, w_query, w_key, w_value, w_out, w_up, w_down, cotangent):
    rows, width = nodes.shape
    hidden = w_up.shape[1]
    groups = lax.axis_size("blk")
    domains = lax.axis_size("dom")
    listed = experts_list.shape[1]
    bits = groups.bit_length() - 1

    def across(array, bit):
        return lax.ppermute(array, "blk", [(i, i ^ (1 << bit)) for i in range(groups)])

    pairs_a = [(i, i ^ 1) for i in range(domains)]
    pairs_b = []
    for i in range(1, domains, 2):
        pairs_b += [(i, (i + 1) % domains), ((i + 1) % domains, i)]

    held = {0: nodes}
    top = bits - 1
    held[1 << top] = across(nodes, top)
    near_a = lax.ppermute(nodes, "dom", pairs_a)
    near_b = lax.ppermute(nodes, "dom", pairs_b)
    for bit in range(top - 1, -1, -1):
        held = dict(zip(held, lax.optimization_barrier(tuple(held.values()))))
        for slot in list(held):
            held[slot | (1 << bit)] = across(held[slot], bit)

    def in_hbm(*arrays):
        return [pltpu.with_memory_space_constraint(array, pltpu.HBM) for array in arrays]

    given = [nodes, w_key, w_value, w_query, cotangent]
    x, w_key, w_value, w_query, cotangent, q, k, v, unit, inv_std = call(
        own_kernel,
        [(array.shape, array.dtype) for array in given]
        + [((rows, width), bf16)] * 3
        + [((rows, width), f32), ((rows, 1), f32)],
        in_hbm(*given),
        [pltpu.SemaphoreType.DMA((len(given),))],
        flops=6 * rows * width * width,
        hbm=len(given),
    )
    held[0] = x
    early = 2 * rows
    late = (1 + listed) * rows
    keys = early + late
    ke, ve, se, gact = call(
        early_kernel,
        [((early, width), bf16)] * 2 + [((H // 2, early, 2 * rows), f32), ((rows, hidden), f32)],
        [near_a, q, k, v, w_key, w_value, cotangent, w_down],
        flops=2 * early * width * (2 * width + 2 * rows),
    )
    sent = sent_slots(groups)
    send_a, send_b, keep, w, inv, gmixed, delta, kb, vb, ds, act, resid, gres, *sends = call(
        functools.partial(main_kernel, groups, listed),
        [((rows, width), bf16), ((rows, width), bf16), ((rows, width), f32)]
        + [((H // 2, keys, 2 * rows), f32), ((H // 2, 1, 2 * rows), f32)]
        + [((rows, width), bf16), ((H, rows), f32), ((late, width), bf16), ((late, width), bf16)]
        + [((H // 2, keys - rows, 2 * rows), bf16), ((rows, hidden), bf16)]
        + [((rows, width), f32)] * 2
        + [((len(slots) * rows, width), bf16) for slots in sent],
        [experts_list]
        + [held[slot] for slot in range(groups)]
        + [near_b, x, ke, ve, se, q, w_key, w_value]
        + [w_out, w_up, cotangent, gact],
        [pltpu.VMEM((late, width), bf16), pltpu.VMEM((rows, width), bf16)]
        + [pltpu.VMEM((keys - rows, width), bf16)] * 2,
        flops=2 * rows * width * (8 * keys + 4 * hidden),
    )
    from_a = lax.ppermute(send_a, "dom", pairs_a)
    received = [across(sends[0], 0)]
    from_b = lax.ppermute(send_b, "dom", pairs_b)
    for bit in range(1, bits):
        total = sends[bit].astype(f32)
        for lower, array in enumerate(received):
            blocks = array.reshape(-1, rows, width)[(1 << bit) >> (lower + 1) :: (2 << bit) >> (lower + 1)]
            total = total + blocks.reshape(-1, width).astype(f32)
        received.append(across(total.astype(bf16), bit))

    layer_out, acc = call(
        rest_kernel,
        [((rows, width), bf16), ((rows, width), f32)],
        [w, inv, delta, gmixed, q, ke, ve, kb, ds, keep, act, resid, w_query, w_key, w_value, w_down],
        [pltpu.VMEM((rows, width), bf16)] * 3,
        flops=2 * rows * width * (3 * width + hidden + 8 * rows),
    )
    (grad_nodes,) = call(
        last_kernel,
        [((rows, width), bf16)],
        [unit, inv_std, gres, acc, from_a, from_b] + received,
    )
    return (layer_out, grad_nodes)


def solution(mesh):
    split = P(("blk", "dom"), None)
    return jax.shard_map(
        on_device,
        mesh=mesh,
        in_specs=(split, split, P(), P(), P(), P(), P(), P(), split),
        out_specs=(split, split),
        check_vma=False,
    )
```

time: 29.8 us -> 29.2 us (0.980)
  Pallas kernels: 11.8 us -> 11.1 us
  starting transfers between devices: 13.2 us -> 13.9 us
  waiting for transfers between devices: 3.27 us -> 2.59 us
    ppermute x1, starting transfers between devices: 0.07 us -> 1.02 us  [on_device(): from_a = lax.ppermute(send_a, 'dom', pairs_a)]
    ppermute x1, waiting for transfers between devices: 1.11 us -> 0.24 us  [on_device(): near_b = lax.ppermute(nodes, 'dom', pairs_b)]
    pallas_call x6 -> x5, Pallas kernels: 11.8 us -> 11.1 us  [call(): pl.pallas_call(kernel, out_shape=[jax.ShapeDtypeStruct(shape, dtype) for...]
  transfers between devices with their start and end apart: 9 -> 9, of which waited for: 3 -> 3; matrix products, arithmetic and copies ran while one was open for 0% -> 0% of each run, Pallas kernels for 23% -> 18%
where the time goes in v3:
time: 29.2 us; the launch traced here: 29 us
  starting transfers between devices  13.9 us (48%)
  Pallas kernels  11.1 us (38%)
  waiting for transfers between devices  2.59 us (9%)
  between operations  1.37 us (5%)
    pallas_call x5, Pallas kernels, call(): pl.pallas_call(kernel, out_shape=[jax.ShapeDtypeStruct(shape, dtype) for...  11.1 us
    ppermute x5, starting transfers between devices, across(): lax.ppermute(array, 'blk', [(i, i ^ 1 << bit) for i in range(groups)])  4.24 us
    ppermute x1, starting transfers between devices, on_device(): from_b = lax.ppermute(send_b, 'dom', pairs_b)  3.56 us
    ppermute x1, starting transfers between devices, on_device(): near_b = lax.ppermute(nodes, 'dom', pairs_b)  3.54 us
    ppermute x1, waiting for transfers between devices, on_device(): from_b = lax.ppermute(send_b, 'dom', pairs_b)  1.64 us
    ppermute x1, starting transfers between devices, on_device(): near_a = lax.ppermute(nodes, 'dom', pairs_a)  1.52 us
    ppermute x1, starting transfers between devices, on_device(): from_a = lax.ppermute(send_a, 'dom', pairs_a)  1.02 us
    ppermute x5, waiting for transfers between devices, across(): lax.ppermute(array, 'blk', [(i, i ^ 1 << bit) for i in range(groups)])  0.7 us
  transfers between devices with their start and end apart: 9, of which 3 were waited for; matrix products, arithmetic and copies ran while one was open for 0% of the time, Pallas kernels for 18%

profile of v3, /device:TPU:0, one launch (start us, length us, event | category | flops | bytes accessed | tf_op | source)
XLA Modules:
  0.0 29.0 jit_solution(9098091846227462853)
XLA Ops:
  0.6 3.0 %collective-permute-start = (bf16[128,512]{1,0:T(8,128)(2,1)}, bf16[128,512]{1,0:T(8,128)(2,1)S(1)}, u32[]{:S(2)}, u32[]{:S(2)}) collective-permute-start(bf16[128,512]{1,0:T(8,128)(2,1)} %refs_0_.2), channel_id=1, source_target_pairs={{0,16},{8,24},{16,0},{24,8},{1,17},{9,25},{17,1},{25,9},{2,18},{10... | collective-permute-start | bytes 393224 | tf_op jit(solution)/shard_map/ppermute | solution.py:264
  3.6 1.5 %collective-permute-start.4 = (bf16[128,512]{1,0:T(8,128)(2,1)}, bf16[128,512]{1,0:T(8,128)(2,1)S(1)}, u32[]{:S(2)}, u32[]{:S(2)}) collective-permute-start(bf16[128,512]{1,0:T(8,128)(2,1)} %refs_0_.2), channel_id=1, source_target_pairs={{0,1},{1,0},{2,3},{3,2},{4,5},{5,4},{6,7},{7,6},{8,9},{9,8},{10,11... | collective-permute-start | bytes 393224 | tf_op jit(solution)/shard_map/ppermute | solution.py:274
  5.2 3.5 %collective-permute-start.3 = (bf16[128,512]{1,0:T(8,128)(2,1)}, bf16[128,512]{1,0:T(8,128)(2,1)S(1)}, u32[]{:S(2)}, u32[]{:S(2)}) collective-permute-start(bf16[128,512]{1,0:T(8,128)(2,1)} %refs_0_.2), channel_id=1, source_target_pairs={{1,2},{2,1},{3,4},{4,3},{5,6},{6,5},{7,0},{0,7},{9,10},{10,9},{11,... | collective-permute-start | bytes 393224 | tf_op jit(solution)/shard_map/ppermute | solution.py:275
  8.7 0.0 collective-permute-done.refs_3_
  8.7 0.0 collective-permute-start.1
  8.7 0.5 %collective-permute-start.2 = (bf16[128,512]{1,0:T(8,128)(2,1)S(1)}, bf16[128,512]{1,0:T(8,128)(2,1)S(1)}, u32[]{:S(2)}, u32[]{:S(2)}) collective-permute-start(bf16[128,512]{1,0:T(8,128)(2,1)S(1)} %collective-permute-done.refs_3_), channel_id=1, source_target_pairs={{0,8},{8,0},{16,24},{24,16},{1,9},{9,1},{17,25},{25,17},{2,10},{10... | collective-permute-start | bytes 393224 | tf_op jit(solution)/shard_map/ppermute | solution.py:264
  9.9 2.0 %shard_map.104 = (bf16[128,512]{1,0:T(8,128)(2,1)S(1)}, bf16[512,512]{1,0:T(8,128)(2,1)S(1)}, bf16[512,512]{1,0:T(8,128)(2,1)S(1)}, bf16[512,512]{1,0:T(8,128)(2...) custom-call(bf16[128,512]{1,0:T(8,128)(2,1)} %refs_0_.2, ...), custom_call_target="tpu_custom_call" | custom-call | flops 201326592 | bytes 4194304 | tf_op jit(solution)/shard_map/pallas_call | solution.py:244
  11.9 0.0 collective-permute-done.4.near_a
  11.9 0.9 %shard_map.105 = (bf16[256,512]{1,0:T(8,128)(2,1)S(1)}, bf16[256,512]{1,0:T(8,128)(2,1)S(1)}, f32[4,256,256]{2,1,0:T(8,128)S(1)}, f32[128,1024]{1,0:T(8,128)S(1)}) custom-call(bf16[128,512]{1,0:T(8,128)(2,1)S(1)} %collective-permute-done.4.near_a, bf16[128,512]{1,0:T(8,128)(2,1)S(1)} %get-tuple-element.37.q_ref.refs_10_.refs_4_, ...), custom_call_target="tpu_custom_call" | custom-call | flops 335544320 | bytes 4194304 | tf_op jit(solution)/shard_map/pallas_call | solution.py:244
  12.8 0.2 collective-permute-done.3.refs_5_
  13.0 0.0 collective-permute-done.1.refs_2_
  13.0 0.0 collective-permute-done.2.refs_4_
  13.0 0.0 copy-done.1
  13.1 5.0 %shard_map.106 = (bf16[128,512]{1,0:T(8,128)(2,1)S(1)}, bf16[128,512]{1,0:T(8,128)(2,1)S(1)}, f32[128,512]{1,0:T(8,128)S(1)}, f32[4,512,256]{2,1,0:T(8,128)S(1)}...) custom-call(s32[1,1]{1,0:T(1,128)S(6)} %copy.11.refs_0_, ...), custom_call_target="tpu_custom_call" | custom-call | flops 1073741824 | bytes 4194304 | tf_op jit(solution)/shard_map/pallas_call | solution.py:244
  18.1 0.0 collective-permute-start.7
  18.1 1.0 %collective-permute-start.5 = (bf16[128,512]{1,0:T(8,128)(2,1)S(1)}, bf16[128,512]{1,0:T(8,128)(2,1)S(1)}, u32[]{:S(2)}, u32[]{:S(2)}) collective-permute-start(bf16[128,512]{1,0:T(8,128)(2,1)S(1)} %get-tuple-element.62), channel_id=1, source_target_pairs={{0,1},{1,0},{2,3},{3,2},{4,5},{5,4},{6,7},{7,6},{8,9},{9,8},{10,11... | collective-permute-start | bytes 393224 | tf_op jit(solution)/shard_map/ppermute | solution.py:322
  19.1 3.6 %collective-permute-start.6 = (bf16[128,512]{1,0:T(8,128)(2,1)S(1)}, bf16[128,512]{1,0:T(8,128)(2,1)S(1)}, u32[]{:S(2)}, u32[]{:S(2)}) collective-permute-start(bf16[128,512]{1,0:T(8,128)(2,1)S(1)} %get-tuple-element.63), channel_id=1, source_target_pairs={{1,2},{2,1},{3,4},{4,3},{5,6},{6,5},{7,0},{0,7},{9,10},{10,9},{11,... | collective-permute-start | bytes 393224 | tf_op jit(solution)/shard_map/ppermute | solution.py:324
  22.7 0.0 collective-permute-done.7.refs_2_
  22.7 0.7 %collective-permute-start.8 = (bf16[128,512]{1,0:T(8,128)(2,1)S(1)}, bf16[128,512]{1,0:T(8,128)(2,1)S(1)}, u32[]{:S(2)}, u32[]{:S(2)}) collective-permute-start(bf16[128,512]{1,0:T(8,128)(2,1)S(1)} %add_convert_fusion), channel_id=1, source_target_pairs={{0,16},{8,24},{16,0},{24,8},{1,17},{9,25},{17,1},{25,9},{2,18},{10... | collective-permute-start | bytes 393224 | tf_op jit(solution)/shard_map/ppermute | solution.py:264
  23.4 2.4 %shard_map.107 = (bf16[128,512]{1,0:T(8,128)(2,1)}, f32[128,512]{1,0:T(8,128)S(1)}) custom-call(f32[4,512,256]{2,1,0:T(8,128)S(1)} %get-tuple-element.47.refs_0_, f32[4,1,256]{2,1,0:T(1,128)S(1)} %get-tuple-element.48.refs_1_, f32[8,128]{1,0:T(8,128)S(1)} %get-tuple-element.49.refs_2_, bf16[128,512]{1,0:T(8,128)(2,1)S(1)} %get-tuple-element.50.refs_3_, ...), custom_call_target="tpu_custom_call" | custom-call | flops 469762048 | bytes 4194304 | tf_op jit(solution)/shard_map/pallas_call | solution.py:244
  25.8 0.0 collective-permute-done.5.refs_0_
  25.8 1.6 %collective-permute-done.6.refs_1_ = bf16[128,512]{1,0:T(8,128)(2,1)S(1)} collective-permute-done((bf16[128,512]{1,0:T(8,128)(2,1)S(1)}, bf16[128,512]{1,0:T(8,128)(2,1)S(1)}, u32[]{:S(2)}, u32[]{:S(2)}) %collective-permute-start.6) | collective-permute-done | bytes 131104 | tf_op jit(solution)/shard_map/ppermute | solution.py:324
  27.4 0.7 %collective-permute-done.8.refs_3_ = bf16[128,512]{1,0:T(8,128)(2,1)S(1)} collective-permute-done((bf16[128,512]{1,0:T(8,128)(2,1)S(1)}, bf16[128,512]{1,0:T(8,128)(2,1)S(1)}, u32[]{:S(2)}, u32[]{:S(2)}) %collective-permute-start.8) | collective-permute-done | bytes 131104 | tf_op jit(solution)/shard_map/ppermute | solution.py:264
  28.1 0.9 %shard_map.108 = bf16[128,512]{1,0:T(8,128)(2,1)} custom-call(f32[128,512]{1,0:T(8,128)S(1)} %get-tuple-element.58.unit_ref, f32[128,1]{1,0:T(8,128)S(1)} %get-tuple-element.59.inv_ref, f32[128,512]{1,0:T(8,128)S(1)} %get-tuple-element.60.gres_ref, f32[128,512]{1,0:T(8,128)S(1)} %get-tuple-element.61.acc_ref, ...), custom_call_target="tpu_custom_call" | custom-call | bytes 4194304 | tf_op jit(solution)/shard_map/pallas_call | solution.py:244
  (6 shorter events, 0.0 us)
Async XLA Ops:
  0.6 11.3 %copy-start = (bf16[1024,512]{1,0:T(8,128)(2,1)S(1)}, bf16[1024,512]{1,0:T(8,128)(2,1)}, u32[]{:S(2)}) copy-start(bf16[1024,512]{1,0:T(8,128)(2,1)} %refs_15_.1) | copy-start | bytes 3145732
  0.6 8.1 %collective-permute-start = (bf16[128,512]{1,0:T(8,128)(2,1)}, bf16[128,512]{1,0:T(8,128)(2,1)S(1)}, u32[]{:S(2)}, u32[]{:S(2)}) collective-permute-start(bf16[128,512]{1,0:T(8,128)(2,1)} %refs_0_.2), channel_id=1, source_target_pairs={{0,16},{8,24},{16,0},{24,8},{1,17},{9,25},{17,1},{25,9},{2,18},{10... | collective-permute-start | bytes 393224 | tf_op jit(solution)/shard_map/ppermute | solution.py:264
  3.6 8.2 %collective-permute-start.4 = (bf16[128,512]{1,0:T(8,128)(2,1)}, bf16[128,512]{1,0:T(8,128)(2,1)S(1)}, u32[]{:S(2)}, u32[]{:S(2)}) collective-permute-start(bf16[128,512]{1,0:T(8,128)(2,1)} %refs_0_.2), channel_id=1, source_target_pairs={{0,1},{1,0},{2,3},{3,2},{4,5},{5,4},{6,7},{7,6},{8,9},{9,8},{10,11... | collective-permute-start | bytes 393224 | tf_op jit(solution)/shard_map/ppermute | solution.py:274
  5.2 7.9 %collective-permute-start.3 = (bf16[128,512]{1,0:T(8,128)(2,1)}, bf16[128,512]{1,0:T(8,128)(2,1)S(1)}, u32[]{:S(2)}, u32[]{:S(2)}) collective-permute-start(bf16[128,512]{1,0:T(8,128)(2,1)} %refs_0_.2), channel_id=1, source_target_pairs={{1,2},{2,1},{3,4},{4,3},{5,6},{6,5},{7,0},{0,7},{9,10},{10,9},{11,... | collective-permute-start | bytes 393224 | tf_op jit(solution)/shard_map/ppermute | solution.py:275
  8.7 4.3 %collective-permute-start.1 = (bf16[128,512]{1,0:T(8,128)(2,1)}, bf16[128,512]{1,0:T(8,128)(2,1)S(1)}, u32[]{:S(2)}, u32[]{:S(2)}) collective-permute-start(bf16[128,512]{1,0:T(8,128)(2,1)} %refs_0_.2), channel_id=1, source_target_pairs={{0,8},{8,0},{16,24},{24,16},{1,9},{9,1},{17,25},{25,17},{2,10},{10... | collective-permute-start | bytes 393224 | tf_op jit(solution)/shard_map/ppermute | solution.py:264
  8.7 4.3 %collective-permute-start.2 = (bf16[128,512]{1,0:T(8,128)(2,1)S(1)}, bf16[128,512]{1,0:T(8,128)(2,1)S(1)}, u32[]{:S(2)}, u32[]{:S(2)}) collective-permute-start(bf16[128,512]{1,0:T(8,128)(2,1)S(1)} %collective-permute-done.refs_3_), channel_id=1, source_target_pairs={{0,8},{8,0},{16,24},{24,16},{1,9},{9,1},{17,25},{25,17},{2,10},{10... | collective-permute-start | bytes 393224 | tf_op jit(solution)/shard_map/ppermute | solution.py:264
  9.9 3.2 %copy-start.1 = (bf16[512,1024]{1,0:T(8,128)(2,1)S(1)}, bf16[512,1024]{1,0:T(8,128)(2,1)}, u32[]{:S(2)}) copy-start(bf16[512,1024]{1,0:T(8,128)(2,1)} %refs_14_.1) | copy-start | bytes 3145732
  9.9 3.2 %copy-start.2 = (bf16[512,512]{1,0:T(8,128)(2,1)S(1)}, bf16[512,512]{1,0:T(8,128)(2,1)}, u32[]{:S(2)}) copy-start(bf16[512,512]{1,0:T(8,128)(2,1)} %refs_13_.1) | copy-start | bytes 1572868
  18.1 4.6 %collective-permute-start.7 = (bf16[256,512]{1,0:T(8,128)(2,1)S(1)}, bf16[256,512]{1,0:T(8,128)(2,1)S(1)}, u32[]{:S(2)}, u32[]{:S(2)}) collective-permute-start(bf16[256,512]{1,0:T(8,128)(2,1)S(1)} %get-tuple-element.64), channel_id=1, source_target_pairs={{0,8},{8,0},{16,24},{24,16},{1,9},{9,1},{17,25},{25,17},{2,10},{10... | collective-permute-start | bytes 786440 | tf_op jit(solution)/shard_map/ppermute | solution.py:264
  18.1 7.7 %collective-permute-start.5 = (bf16[128,512]{1,0:T(8,128)(2,1)S(1)}, bf16[128,512]{1,0:T(8,128)(2,1)S(1)}, u32[]{:S(2)}, u32[]{:S(2)}) collective-permute-start(bf16[128,512]{1,0:T(8,128)(2,1)S(1)} %get-tuple-element.62), channel_id=1, source_target_pairs={{0,1},{1,0},{2,3},{3,2},{4,5},{5,4},{6,7},{7,6},{8,9},{9,8},{10,11... | collective-permute-start | bytes 393224 | tf_op jit(solution)/shard_map/ppermute | solution.py:322
  19.1 8.3 %collective-permute-start.6 = (bf16[128,512]{1,0:T(8,128)(2,1)S(1)}, bf16[128,512]{1,0:T(8,128)(2,1)S(1)}, u32[]{:S(2)}, u32[]{:S(2)}) collective-permute-start(bf16[128,512]{1,0:T(8,128)(2,1)S(1)} %get-tuple-element.63), channel_id=1, source_target_pairs={{1,2},{2,1},{3,4},{4,3},{5,6},{6,5},{7,0},{0,7},{9,10},{10,9},{11,... | collective-permute-start | bytes 393224 | tf_op jit(solution)/shard_map/ppermute | solution.py:324
  22.7 5.4 %collective-permute-start.8 = (bf16[128,512]{1,0:T(8,128)(2,1)S(1)}, bf16[128,512]{1,0:T(8,128)(2,1)S(1)}, u32[]{:S(2)}, u32[]{:S(2)}) collective-permute-start(bf16[128,512]{1,0:T(8,128)(2,1)S(1)} %add_convert_fusion), channel_id=1, source_target_pairs={{0,16},{8,24},{16,0},{24,8},{1,17},{9,25},{17,1},{25,9},{2,18},{10... | collective-permute-start | bytes 393224 | tf_op jit(solution)/shard_map/ppermute | solution.py:264

commit v4 on v3

--- a/solution.py
+++ b/solution.py
@@ -121,8 +121,9 @@
 
 def main_kernel(groups, listed, *refs):
     experts_ref = refs[0]
-    slots = refs[1 : 1 + groups]
-    (near_b, x_ref, ke_ref, ve_ref, se_ref, q_ref, wk_ref, wv_ref) = refs[1 + groups : 9 + groups]
+    near_b = refs[3]
+    slots = refs[1:2] + refs[1 + groups : 3 : -1] + refs[2:3]
+    (x_ref, ke_ref, ve_ref, se_ref, q_ref, wk_ref, wv_ref) = refs[2 + groups : 9 + groups]
     (wout_ref, wup_ref, cot_ref, gact_ref) = refs[9 + groups : 13 + groups]
     outs = refs[13 + groups :]
     (send_a, send_b, keep, w_ref, inv_ref, gmixed_ref, delta_ref, kb_ref, vb_ref, ds_ref) = outs[:10]
@@ -260,23 +261,20 @@
     listed = experts_list.shape[1]
     bits = groups.bit_length() - 1
 
+    def exchanged(array, slot):
+        return lax.ppermute(array, "blk", [(i, i ^ slot) for i in range(groups)])
+
     def across(array, bit):
-        return lax.ppermute(array, "blk", [(i, i ^ (1 << bit)) for i in range(groups)])
+        return exchanged(array, 1 << bit)
 
     pairs_a = [(i, i ^ 1) for i in range(domains)]
     pairs_b = []
     for i in range(1, domains, 2):
         pairs_b += [(i, (i + 1) % domains), ((i + 1) % domains, i)]
 
-    held = {0: nodes}
-    top = bits - 1
-    held[1 << top] = across(nodes, top)
     near_a = lax.ppermute(nodes, "dom", pairs_a)
     near_b = lax.ppermute(nodes, "dom", pairs_b)
-    for bit in range(top - 1, -1, -1):
-        held = dict(zip(held, lax.optimization_barrier(tuple(held.values()))))
-        for slot in list(held):
-            held[slot | (1 << bit)] = across(held[slot], bit)
+    held = {slot: exchanged(nodes, slot) for slot in range(1, groups)}
 
     def in_hbm(*arrays):
         return [pltpu.with_memory_space_constraint(array, pltpu.HBM) for array in arrays]
@@ -312,8 +310,9 @@
         + [((rows, width), f32)] * 2
         + [((len(slots) * rows, width), bf16) for slots in sent],
         [experts_list]
-        + [held[slot] for slot in range(groups)]
-        + [near_b, x, ke, ve, se, q, w_key, w_value]
+        + [x, held[groups - 1], near_b]
+        + [held[slot] for slot in range(groups - 2, 0, -1)]
+        + [x, ke, ve, se, q, w_key, w_value]
         + [w_out, w_up, cotangent, gact],
         [pltpu.VMEM((late, width), bf16), pltpu.VMEM((rows, width), bf16)]
         + [pltpu.VMEM((keys - rows, width), bf16)] * 2,

time: 29.2 us -> 28.7 us (0.983)
  starting transfers between devices: 13.9 us -> 13 us
  waiting for transfers between devices: 2.59 us -> 3.02 us
    ppermute x1, waiting for transfers between devices: 0.01 us -> 2.06 us  [on_device(): from_a = lax.ppermute(send_a, 'dom', pairs_a)]
    ppermute x1, waiting for transfers between devices: 1.64 us -> 0.01 us  [on_device(): from_b = lax.ppermute(send_b, 'dom', pairs_b)]
    ppermute x1, starting transfers between devices: 1.52 us -> 3.03 us  [on_device(): near_a = lax.ppermute(nodes, 'dom', pairs_a)]
    ppermute x1, starting transfers between devices: 1.02 us -> 0.01 us  [on_device(): from_a = lax.ppermute(send_a, 'dom', pairs_a)]
    ppermute x5, starting transfers between devices: 4.24 us -> 3.5 us  [exchanged(): return lax.ppermute(array, 'blk', [(i, i ^ slot) for i in range(groups)])]
    ppermute x1, starting transfers between devices: 3.56 us -> 2.88 us  [on_device(): from_b = lax.ppermute(send_b, 'dom', pairs_b)]
where the time goes in v4:
time: 28.7 us; the launch traced here: 28.5 us
  starting transfers between devices  13 us (45%)
  Pallas kernels  11.1 us (39%)
  waiting for transfers between devices  3.02 us (11%)
  between operations  1.37 us (5%)
    pallas_call x5, Pallas kernels, call(): pl.pallas_call(kernel, out_shape=[jax.ShapeDtypeStruct(shape, dtype) for...  11.1 us
    ppermute x1, starting transfers between devices, on_device(): near_b = lax.ppermute(nodes, 'dom', pairs_b)  3.54 us
    ppermute x5, starting transfers between devices, exchanged(): return lax.ppermute(array, 'blk', [(i, i ^ slot) for i in range(groups)])  3.5 us
    ppermute x1, starting transfers between devices, on_device(): near_a = lax.ppermute(nodes, 'dom', pairs_a)  3.03 us
    ppermute x1, starting transfers between devices, on_device(): from_b = lax.ppermute(send_b, 'dom', pairs_b)  2.88 us
    ppermute x1, waiting for transfers between devices, on_device(): from_a = lax.ppermute(send_a, 'dom', pairs_a)  2.06 us
    ppermute x5, waiting for transfers between devices, exchanged(): return lax.ppermute(array, 'blk', [(i, i ^ slot) for i in range(groups)])  0.86 us
  transfers between devices with their start and end apart: 9, of which 3 were waited for; matrix products, arithmetic and copies ran while one was open for 0% of the time, Pallas kernels for 18%

profile of v4, /device:TPU:0, one launch (start us, length us, event | category | flops | bytes accessed | tf_op | source)
XLA Modules:
  0.0 28.5 jit_solution(411385356684163603)
XLA Ops:
  0.6 3.0 %collective-permute-start.4 = (bf16[128,512]{1,0:T(8,128)(2,1)}, bf16[128,512]{1,0:T(8,128)(2,1)S(1)}, u32[]{:S(2)}, u32[]{:S(2)}) collective-permute-start(bf16[128,512]{1,0:T(8,128)(2,1)} %refs_0_.2), channel_id=1, source_target_pairs={{0,1},{1,0},{2,3},{3,2},{4,5},{5,4},{6,7},{7,6},{8,9},{9,8},{10,11... | collective-permute-start | bytes 393224 | tf_op jit(solution)/shard_map/ppermute | solution.py:275
  3.7 1.5 %collective-permute-start.2 = (bf16[128,512]{1,0:T(8,128)(2,1)}, bf16[128,512]{1,0:T(8,128)(2,1)S(1)}, u32[]{:S(2)}, u32[]{:S(2)}) collective-permute-start(bf16[128,512]{1,0:T(8,128)(2,1)} %refs_0_.2), channel_id=1, source_target_pairs={{0,16},{8,24},{16,0},{24,8},{1,17},{9,25},{17,1},{25,9},{2,18},{10... | collective-permute-start | bytes 393224 | tf_op jit(solution)/shard_map/ppermute | solution.py:265
  5.2 3.5 %collective-permute-start.1 = (bf16[128,512]{1,0:T(8,128)(2,1)}, bf16[128,512]{1,0:T(8,128)(2,1)S(1)}, u32[]{:S(2)}, u32[]{:S(2)}) collective-permute-start(bf16[128,512]{1,0:T(8,128)(2,1)} %refs_0_.2), channel_id=1, source_target_pairs={{1,2},{2,1},{3,4},{4,3},{5,6},{6,5},{7,0},{0,7},{9,10},{10,9},{11,... | collective-permute-start | bytes 393224 | tf_op jit(solution)/shard_map/ppermute | solution.py:276
  8.7 0.0 collective-permute-start
  8.7 0.6 %collective-permute-start.3 = (bf16[128,512]{1,0:T(8,128)(2,1)}, bf16[128,512]{1,0:T(8,128)(2,1)S(1)}, u32[]{:S(2)}, u32[]{:S(2)}) collective-permute-start(bf16[128,512]{1,0:T(8,128)(2,1)} %refs_0_.2), channel_id=1, source_target_pairs={{0,8},{8,0},{16,24},{24,16},{1,9},{9,1},{17,25},{25,17},{2,10},{10... | collective-permute-start | bytes 393224 | tf_op jit(solution)/shard_map/ppermute | solution.py:265
  10.0 2.0 %shard_map.104 = (bf16[128,512]{1,0:T(8,128)(2,1)S(1)}, bf16[512,512]{1,0:T(8,128)(2,1)S(1)}, bf16[512,512]{1,0:T(8,128)(2,1)S(1)}, bf16[512,512]{1,0:T(8,128)(2...) custom-call(bf16[128,512]{1,0:T(8,128)(2,1)} %refs_0_.2, ...), custom_call_target="tpu_custom_call" | custom-call | flops 201326592 | bytes 4194304 | tf_op jit(solution)/shard_map/pallas_call | solution.py:245
  12.0 0.0 collective-permute-done.4.near_a
  12.0 0.9 %shard_map.105 = (bf16[256,512]{1,0:T(8,128)(2,1)S(1)}, bf16[256,512]{1,0:T(8,128)(2,1)S(1)}, f32[4,256,256]{2,1,0:T(8,128)S(1)}, f32[128,1024]{1,0:T(8,128)S(1)}) custom-call(bf16[128,512]{1,0:T(8,128)(2,1)S(1)} %collective-permute-done.4.near_a, bf16[128,512]{1,0:T(8,128)(2,1)S(1)} %get-tuple-element.33.q_ref.refs_10_.refs_4_, ...), custom_call_target="tpu_custom_call" | custom-call | flops 335544320 | bytes 4194304 | tf_op jit(solution)/shard_map/pallas_call | solution.py:245
  12.9 0.0 collective-permute-done.2.refs_4_
  13.0 0.1 collective-permute-done.1.refs_3_
  13.0 0.9 %collective-permute-done.refs_2_ = bf16[128,512]{1,0:T(8,128)(2,1)S(1)} collective-permute-done((bf16[128,512]{1,0:T(8,128)(2,1)}, bf16[128,512]{1,0:T(8,128)(2,1)S(1)}, u32[]{:S(2)}, u32[]{:S(2)}) %collective-permute-start) | collective-permute-done | bytes 131104 | tf_op jit(solution)/shard_map/ppermute | solution.py:265
  13.9 0.0 collective-permute-done.3.refs_5_
  13.9 0.0 copy-done.2
  13.9 5.0 %shard_map.106 = (bf16[128,512]{1,0:T(8,128)(2,1)S(1)}, bf16[128,512]{1,0:T(8,128)(2,1)S(1)}, f32[128,512]{1,0:T(8,128)S(1)}, f32[4,512,256]{2,1,0:T(8,128)S(1)}...) custom-call(s32[1,1]{1,0:T(1,128)S(6)} %copy.11.refs_0_, ...), custom_call_target="tpu_custom_call" | custom-call | flops 1073741824 | bytes 4194304 | tf_op jit(solution)/shard_map/pallas_call | solution.py:245
  18.9 0.0 collective-permute-start.7
  18.9 0.0 collective-permute-start.5
  18.9 2.9 %collective-permute-start.6 = (bf16[128,512]{1,0:T(8,128)(2,1)S(1)}, bf16[128,512]{1,0:T(8,128)(2,1)S(1)}, u32[]{:S(2)}, u32[]{:S(2)}) collective-permute-start(bf16[128,512]{1,0:T(8,128)(2,1)S(1)} %get-tuple-element.59), channel_id=1, source_target_pairs={{1,2},{2,1},{3,4},{4,3},{5,6},{6,5},{7,0},{0,7},{9,10},{10,9},{11,... | collective-permute-start | bytes 393224 | tf_op jit(solution)/shard_map/ppermute | solution.py:323
  21.8 0.0 collective-permute-done.7.refs_2_
  21.8 1.4 %collective-permute-start.8 = (bf16[128,512]{1,0:T(8,128)(2,1)S(1)}, bf16[128,512]{1,0:T(8,128)(2,1)S(1)}, u32[]{:S(2)}, u32[]{:S(2)}) collective-permute-start(bf16[128,512]{1,0:T(8,128)(2,1)S(1)} %add_convert_fusion), channel_id=1, source_target_pairs={{0,16},{8,24},{16,0},{24,8},{1,17},{9,25},{17,1},{25,9},{2,18},{10... | collective-permute-start | bytes 393224 | tf_op jit(solution)/shard_map/ppermute | solution.py:265
  23.2 2.4 %shard_map.107 = (bf16[128,512]{1,0:T(8,128)(2,1)}, f32[128,512]{1,0:T(8,128)S(1)}) custom-call(f32[4,512,256]{2,1,0:T(8,128)S(1)} %get-tuple-element.43.refs_0_, f32[4,1,256]{2,1,0:T(1,128)S(1)} %get-tuple-element.44.refs_1_, f32[8,128]{1,0:T(8,128)S(1)} %get-tuple-element.45.refs_2_, bf16[128,512]{1,0:T(8,128)(2,1)S(1)} %get-tuple-element.46.refs_3_, ...), custom_call_target="tpu_custom_call" | custom-call | flops 469762048 | bytes 4194304 | tf_op jit(solution)/shard_map/pallas_call | solution.py:245
  25.6 2.1 %collective-permute-done.5.refs_0_ = bf16[128,512]{1,0:T(8,128)(2,1)S(1)} collective-permute-done((bf16[128,512]{1,0:T(8,128)(2,1)S(1)}, bf16[128,512]{1,0:T(8,128)(2,1)S(1)}, u32[]{:S(2)}, u32[]{:S(2)}) %collective-permute-start.5) | collective-permute-done | bytes 131104 | tf_op jit(solution)/shard_map/ppermute | solution.py:321
  27.6 0.0 collective-permute-done.6.refs_1_
  27.6 0.0 collective-permute-done.8.refs_3_
  27.6 0.9 %shard_map.108 = bf16[128,512]{1,0:T(8,128)(2,1)} custom-call(f32[128,512]{1,0:T(8,128)S(1)} %get-tuple-element.54.unit_ref, f32[128,1]{1,0:T(8,128)S(1)} %get-tuple-element.55.inv_ref, f32[128,512]{1,0:T(8,128)S(1)} %get-tuple-element.56.gres_ref, f32[128,512]{1,0:T(8,128)S(1)} %get-tuple-element.57.acc_ref, ...), custom_call_target="tpu_custom_call" | custom-call | bytes 4194304 | tf_op jit(solution)/shard_map/pallas_call | solution.py:245
  (6 shorter events, 0.0 us)
Async XLA Ops:
  0.6 11.4 %copy-start = (bf16[1024,512]{1,0:T(8,128)(2,1)S(1)}, bf16[1024,512]{1,0:T(8,128)(2,1)}, u32[]{:S(2)}) copy-start(bf16[1024,512]{1,0:T(8,128)(2,1)} %refs_15_.1) | copy-start | bytes 3145732
  0.6 11.4 %collective-permute-start.4 = (bf16[128,512]{1,0:T(8,128)(2,1)}, bf16[128,512]{1,0:T(8,128)(2,1)S(1)}, u32[]{:S(2)}, u32[]{:S(2)}) collective-permute-start(bf16[128,512]{1,0:T(8,128)(2,1)} %refs_0_.2), channel_id=1, source_target_pairs={{0,1},{1,0},{2,3},{3,2},{4,5},{5,4},{6,7},{7,6},{8,9},{9,8},{10,11... | collective-permute-start | bytes 393224 | tf_op jit(solution)/shard_map/ppermute | solution.py:275
  3.7 9.3 %collective-permute-start.2 = (bf16[128,512]{1,0:T(8,128)(2,1)}, bf16[128,512]{1,0:T(8,128)(2,1)S(1)}, u32[]{:S(2)}, u32[]{:S(2)}) collective-permute-start(bf16[128,512]{1,0:T(8,128)(2,1)} %refs_0_.2), channel_id=1, source_target_pairs={{0,16},{8,24},{16,0},{24,8},{1,17},{9,25},{17,1},{25,9},{2,18},{10... | collective-permute-start | bytes 393224 | tf_op jit(solution)/shard_map/ppermute | solution.py:265
  5.2 7.9 %collective-permute-start.1 = (bf16[128,512]{1,0:T(8,128)(2,1)}, bf16[128,512]{1,0:T(8,128)(2,1)S(1)}, u32[]{:S(2)}, u32[]{:S(2)}) collective-permute-start(bf16[128,512]{1,0:T(8,128)(2,1)} %refs_0_.2), channel_id=1, source_target_pairs={{1,2},{2,1},{3,4},{4,3},{5,6},{6,5},{7,0},{0,7},{9,10},{10,9},{11,... | collective-permute-start | bytes 393224 | tf_op jit(solution)/shard_map/ppermute | solution.py:276
  8.7 5.2 %collective-permute-start = (bf16[128,512]{1,0:T(8,128)(2,1)}, bf16[128,512]{1,0:T(8,128)(2,1)S(1)}, u32[]{:S(2)}, u32[]{:S(2)}) collective-permute-start(bf16[128,512]{1,0:T(8,128)(2,1)} %refs_0_.2), channel_id=1, source_target_pairs={{0,24},{8,16},{16,8},{24,0},{1,25},{9,17},{17,9},{25,1},{2,26},{10... | collective-permute-start | bytes 393224 | tf_op jit(solution)/shard_map/ppermute | solution.py:265
  8.7 5.2 %collective-permute-start.3 = (bf16[128,512]{1,0:T(8,128)(2,1)}, bf16[128,512]{1,0:T(8,128)(2,1)S(1)}, u32[]{:S(2)}, u32[]{:S(2)}) collective-permute-start(bf16[128,512]{1,0:T(8,128)(2,1)} %refs_0_.2), channel_id=1, source_target_pairs={{0,8},{8,0},{16,24},{24,16},{1,9},{9,1},{17,25},{25,17},{2,10},{10... | collective-permute-start | bytes 393224 | tf_op jit(solution)/shard_map/ppermute | solution.py:265
  10.0 3.9 %copy-start.1 = (bf16[512,1024]{1,0:T(8,128)(2,1)S(1)}, bf16[512,1024]{1,0:T(8,128)(2,1)}, u32[]{:S(2)}) copy-start(bf16[512,1024]{1,0:T(8,128)(2,1)} %refs_14_.1) | copy-start | bytes 3145732
  10.0 3.9 %copy-start.2 = (bf16[512,512]{1,0:T(8,128)(2,1)S(1)}, bf16[512,512]{1,0:T(8,128)(2,1)}, u32[]{:S(2)}) copy-start(bf16[512,512]{1,0:T(8,128)(2,1)} %refs_13_.1) | copy-start | bytes 1572868
  18.9 2.9 %collective-permute-start.7 = (bf16[256,512]{1,0:T(8,128)(2,1)S(1)}, bf16[256,512]{1,0:T(8,128)(2,1)S(1)}, u32[]{:S(2)}, u32[]{:S(2)}) collective-permute-start(bf16[256,512]{1,0:T(8,128)(2,1)S(1)} %get-tuple-element.60), channel_id=1, source_target_pairs={{0,8},{8,0},{16,24},{24,16},{1,9},{9,1},{17,25},{25,17},{2,10},{10... | collective-permute-start | bytes 786440 | tf_op jit(solution)/shard_map/ppermute | solution.py:265
  18.9 8.7 %collective-permute-start.5 = (bf16[128,512]{1,0:T(8,128)(2,1)S(1)}, bf16[128,512]{1,0:T(8,128)(2,1)S(1)}, u32[]{:S(2)}, u32[]{:S(2)}) collective-permute-start(bf16[128,512]{1,0:T(8,128)(2,1)S(1)} %get-tuple-element.58), channel_id=1, source_target_pairs={{0,1},{1,0},{2,3},{3,2},{4,5},{5,4},{6,7},{7,6},{8,9},{9,8},{10,11... | collective-permute-start | bytes 393224 | tf_op jit(solution)/shard_map/ppermute | solution.py:321
  18.9 8.7 %collective-permute-start.6 = (bf16[128,512]{1,0:T(8,128)(2,1)S(1)}, bf16[128,512]{1,0:T(8,128)(2,1)S(1)}, u32[]{:S(2)}, u32[]{:S(2)}) collective-permute-start(bf16[128,512]{1,0:T(8,128)(2,1)S(1)} %get-tuple-element.59), channel_id=1, source_target_pairs={{1,2},{2,1},{3,4},{4,3},{5,6},{6,5},{7,0},{0,7},{9,10},{10,9},{11,... | collective-permute-start | bytes 393224 | tf_op jit(solution)/shard_map/ppermute | solution.py:323
  21.8 5.8 %collective-permute-start.8 = (bf16[128,512]{1,0:T(8,128)(2,1)S(1)}, bf16[128,512]{1,0:T(8,128)(2,1)S(1)}, u32[]{:S(2)}, u32[]{:S(2)}) collective-permute-start(bf16[128,512]{1,0:T(8,128)(2,1)S(1)} %add_convert_fusion), channel_id=1, source_target_pairs={{0,16},{8,24},{16,0},{24,8},{1,17},{9,25},{17,1},{25,9},{2,18},{10... | collective-permute-start | bytes 393224 | tf_op jit(solution)/shard_map/ppermute | solution.py:265

commit v5 on v4

--- a/solution.py
+++ b/solution.py
@@ -51,6 +51,13 @@
     left = lax.broadcasted_iota(jnp.int32, rows.shape, 1) < HEAD
     zero = jnp.zeros_like(rows)
     return jnp.concatenate([jnp.where(left, rows, zero), jnp.where(left, zero, rows)], 0)
+
+
+def halves_t(rows):
+    turned = rows.T
+    upper = lax.broadcasted_iota(jnp.int32, turned.shape, 0) < HEAD
+    zero = jnp.zeros_like(turned)
+    return jnp.concatenate([jnp.where(upper, turned, zero), jnp.where(upper, zero, turned)], 1)
 
 
 def unhalve(both):
@@ -94,10 +101,11 @@
     return [(j, slice(j * PAIR, (j + 1) * PAIR)) for j in range(H // 2)]
 
 
-def early_kernel(
-    near_a, q_ref, k_ref, v_ref, wk_ref, wv_ref, cot_ref, wdown_ref, ke_ref, ve_ref, se_ref, gact_ref
-):
+def early_kernel(*refs):
+    near_a, q_ref, k_ref, v_ref, wk_ref, wv_ref, cot_ref, wdown_ref, wout_ref, given = refs[:10]
+    wup_ref, ke_ref, ve_ref, se_ref, gact_ref, q2t_ref, *turned, sem = refs[10:]
     rows = q_ref.shape[0]
+    (copy,) = fetch([given], [wup_ref], sem)
     unit, _ = normalize(near_a[...].astype(f32))
     normed = unit.astype(bf16)
     ke_ref[:rows, :] = k_ref[...]
@@ -105,14 +113,20 @@
     ke_ref[rows:, :] = dot(normed, wk_ref[...]).astype(bf16)
     ve_ref[rows:, :] = dot(normed, wv_ref[...]).astype(bf16)
     for j, cols in pair_columns():
-        se_ref[j] = dot_t(ke_ref[:, cols], halves(q_ref[:, cols]))
+        q2t = halves_t(q_ref[:, cols])
+        q2t_ref[j] = q2t
+        se_ref[j] = dot(ke_ref[:, cols], q2t)
     gact_ref[...] = dot_t(cot_ref[...], wdown_ref[...])
-
-
-def block_back(v, q2, g2, weights, inv, row):
+    for weight, out_ref in zip((wk_ref, wv_ref, wout_ref), turned):
+        out_ref[...] = weight[...].T
+    copy.wait()
+    turned[3][...] = wup_ref[...].T
+
+
+def block_back(v, q, g, weights, inv, row):
     probs = weights * inv
-    ds = (probs * (dot_t(v, g2) - row)).astype(bf16)
-    return ds, dot(ds, q2).astype(bf16), dot(probs.astype(bf16), g2).astype(bf16)
+    ds = (probs * (dot(v, halves_t(g)) - row)).astype(bf16)
+    return ds, dot(ds, halves(q)).astype(bf16), dot(probs.astype(bf16), halves(g)).astype(bf16)
 
 
 def delta_row(delta, j):
@@ -123,16 +137,17 @@
     experts_ref = refs[0]
     near_b = refs[3]
     slots = refs[1:2] + refs[1 + groups : 3 : -1] + refs[2:3]
-    (x_ref, ke_ref, ve_ref, se_ref, q_ref, wk_ref, wv_ref) = refs[2 + groups : 9 + groups]
+    (x_ref, ve_ref, se_ref, q_ref, q2t_ref, wk_ref, wv_ref) = refs[2 + groups : 9 + groups]
     (wout_ref, wup_ref, cot_ref, gact_ref) = refs[9 + groups : 13 + groups]
-    outs = refs[13 + groups :]
+    wk_t, wv_t, wout_t, wup_t = refs[13 + groups : 17 + groups]
+    outs = refs[17 + groups :]
     (send_a, send_b, keep, w_ref, inv_ref, gmixed_ref, delta_ref, kb_ref, vb_ref, ds_ref) = outs[:10]
     (act_ref, resid_ref, gres_ref), outs = outs[10:13], outs[13:]
     bits = groups.bit_length() - 1
     sends = outs[:bits]
     normed_s, mixed_s, gk_s, gv_s = outs[bits:]
     rows, width = x_ref.shape
-    early = 2 * rows
+    early = ve_ref.shape[0]
     place = lax.axis_index("blk")
     normed_s[:rows, :] = normalize(near_b[...].astype(f32))[0].astype(bf16)
     for e in range(listed):
@@ -145,7 +160,7 @@
     kb_ref[...] = dot(normed, wk_ref[...]).astype(bf16)
     vb_ref[...] = dot(normed, wv_ref[...]).astype(bf16)
     for j, cols in pair_columns():
-        last = dot_t(kb_ref[:, cols], halves(q_ref[:, cols]))
+        last = dot(kb_ref[:, cols], q2t_ref[j])
         first = se_ref[j]
         top = jnp.maximum(jnp.max(first, axis=0, keepdims=True), jnp.max(last, axis=0, keepdims=True))
         first = jnp.exp(first - top)
@@ -169,9 +184,9 @@
         1.0 + (3.0 * GELU_A) * square
     )
     gpre = (gact_ref[...] * slope).astype(bf16)
-    gres = cot_ref[...].astype(f32) + normalize_back(unit2, inv2, dot_t(gpre, wup_ref[...]))
+    gres = cot_ref[...].astype(f32) + normalize_back(unit2, inv2, dot(gpre, wup_t[...]))
     gres_ref[...] = gres
-    gmixed = dot_t(gres.astype(bf16), wout_ref[...]).astype(bf16)
+    gmixed = dot(gres.astype(bf16), wout_t[...]).astype(bf16)
     gmixed_ref[...] = gmixed
     prod = gmixed.astype(f32) * mixed.astype(f32)
     high = prod.astype(bf16)
@@ -184,13 +199,13 @@
     for j, cols in pair_columns():
         ds_ref[j], gk_s[:, cols], gv_s[:, cols] = block_back(
             jnp.concatenate([ve_ref[rows:, cols], vb_ref[:, cols]], 0),
-            halves(q_ref[:, cols]),
-            halves(gmixed[:, cols]),
+            q_ref[:, cols],
+            gmixed[:, cols],
             w_ref[j, rows:, :],
             inv_ref[j],
             delta_row(delta, j),
         )
-    parts = dot_t(gk_s[...], wk_ref[...]) + dot_t(gv_s[...], wv_ref[...])
+    parts = dot(gk_s[...], wk_t[...]) + dot(gv_s[...], wv_t[...])
     send_a[...] = parts[:rows].astype(bf16)
     send_b[...] = parts[rows : 2 * rows].astype(bf16)
     picked = [experts_ref[:, e : e + 1] ^ place for e in range(listed)]
@@ -216,8 +231,8 @@
     for j, cols in pair_columns():
         ds, gk_s[:, cols], gv_s[:, cols] = block_back(
             ve_ref[:rows, cols],
-            halves(q_ref[:, cols]),
-            halves(gmixed_ref[:, cols]),
+            q_ref[:, cols],
+            gmixed_ref[:, cols],
             w_ref[j, :rows, :],
             inv_ref[j],
             delta_row(delta, j),
@@ -226,7 +241,7 @@
         total = total + t_dot(kb_ref[:, cols], ds_ref[j, rows:, :])
         gq_s[:, cols] = (unhalve(total) * SCALE).astype(bf16)
     acc_ref[...] = (
-        keep_ref[...] + dot_t(gq_s[...], wq_ref[...]) + dot_t(gk_s[...], wk_ref[...]) + dot_t(gv_s[...], wv_ref[...])
+        keep_ref[...] + dot_t(gq_s[...], wq_ref[...]) + dot(gk_s[...], wk_ref[...]) + dot(gv_s[...], wv_ref[...])
     )
     out_ref[...] = (resid_ref[...] + dot(act_ref[...], wdown_ref[...])).astype(bf16)
 
@@ -294,10 +309,16 @@
     early = 2 * rows
     late = (1 + listed) * rows
     keys = early + late
-    ke, ve, se, gact = call(
+    w_up, ke, ve, se, gact, q2t, wk_t, wv_t, wout_t, wup_t = call(
         early_kernel,
-        [((early, width), bf16)] * 2 + [((H // 2, early, 2 * rows), f32), ((rows, hidden), f32)],
-        [near_a, q, k, v, w_key, w_value, cotangent, w_down],
+        [(w_up.shape, bf16)]
+        + [((early, width), bf16)] * 2
+        + [((H // 2, early, 2 * rows), f32), ((rows, hidden), f32), ((H // 2, PAIR, 2 * rows), bf16)]
+        + [((width, width), bf16)] * 3
+        + [((hidden, width), bf16)],
+        [near_a, q, k, v, w_key, w_value, cotangent, w_down, w_out] + in_hbm(w_up),
+        [pltpu.SemaphoreType.DMA((1,))],
+        hbm=1,
         flops=2 * early * width * (2 * width + 2 * rows),
     )
     sent = sent_slots(groups)
@@ -312,8 +333,8 @@
         [experts_list]
         + [x, held[groups - 1], near_b]
         + [held[slot] for slot in range(groups - 2, 0, -1)]
-        + [x, ke, ve, se, q, w_key, w_value]
-        + [w_out, w_up, cotangent, gact],
+        + [x, ve, se, q, q2t, w_key, w_value]
+        + [w_out, w_up, cotangent, gact, wk_t, wv_t, wout_t, wup_t],
         [pltpu.VMEM((late, width), bf16), pltpu.VMEM((rows, width), bf16)]
         + [pltpu.VMEM((keys - rows, width), bf16)] * 2,
         flops=2 * rows * width * (8 * keys + 4 * hidden),
@@ -331,7 +352,7 @@
     layer_out, acc = call(
         rest_kernel,
         [((rows, width), bf16), ((rows, width), f32)],
-        [w, inv, delta, gmixed, q, ke, ve, kb, ds, keep, act, resid, w_query, w_key, w_value, w_down],
+        [w, inv, delta, gmixed, q, ke, ve, kb, ds, keep, act, resid, w_query, wk_t, wv_t, w_down],
         [pltpu.VMEM((rows, width), bf16)] * 3,
         flops=2 * rows * width * (3 * width + hidden + 8 * rows),
     )

time: 28.7 us -> 28.5 us (level)
  waiting for transfers between devices: 3.02 us -> 1.41 us
  starting transfers between devices: 13 us -> 13.9 us
  Pallas kernels: 11.1 us -> 11.6 us
    ppermute x1, waiting for transfers between devices: 2.06 us -> 0.01 us  [on_device(): from_a = lax.ppermute(send_a, 'dom', pairs_a)]
    ppermute x1, waiting for transfers between devices: 0.01 us -> 1.34 us  [on_device(): from_b = lax.ppermute(send_b, 'dom', pairs_b)]
    ppermute x5, starting transfers between devices: 3.5 us -> 4.64 us  [exchanged(): return lax.ppermute(array, 'blk', [(i, i ^ slot) for i in range(groups)])]
    ppermute x5, waiting for transfers between devices: 0.86 us -> 0.06 us  [exchanged(): return lax.ppermute(array, 'blk', [(i, i ^ slot) for i in range(groups)])]
    pallas_call x5, Pallas kernels: 11.1 us -> 11.6 us  [call(): pl.pallas_call(kernel, out_shape=[jax.ShapeDtypeStruct(shape, dtype) for...]
  transfers between devices with their start and end apart: 9 -> 9, of which waited for: 3 -> 2; matrix products, arithmetic and copies ran while one was open for 0% -> 0% of each run, Pallas kernels for 18% -> 22%
where the time goes in v5:
time: 28.5 us; the launch traced here: 28.3 us
  starting transfers between devices  13.9 us (49%)
  Pallas kernels  11.6 us (41%)
  waiting for transfers between devices  1.41 us (5%)
  between operations  1.39 us (5%)
    pallas_call x5, Pallas kernels, call(): pl.pallas_call(kernel, out_shape=[jax.ShapeDtypeStruct(shape, dtype) for...  11.6 us
    ppermute x5, starting transfers between devices, exchanged(): return lax.ppermute(array, 'blk', [(i, i ^ slot) for i in range(groups)])  4.64 us
    ppermute x1, starting transfers between devices, on_device(): near_b = lax.ppermute(nodes, 'dom', pairs_b)  3.54 us
    ppermute x1, starting transfers between devices, on_device(): near_a = lax.ppermute(nodes, 'dom', pairs_a)  3.03 us
    ppermute x1, starting transfers between devices, on_device(): from_b = lax.ppermute(send_b, 'dom', pairs_b)  2.61 us
    ppermute x1, waiting for transfers between devices, on_device(): from_b = lax.ppermute(send_b, 'dom', pairs_b)  1.34 us
  transfers between devices with their start and end apart: 9, of which 2 were waited for; matrix products, arithmetic and copies ran while one was open for 0% of the time, Pallas kernels for 22%

profile of v5, /device:TPU:0, one launch (start us, length us, event | category | flops | bytes accessed | tf_op | source)
XLA Modules:
  0.0 28.3 jit_solution(11199630394510340584)
XLA Ops:
  0.6 0.0 copy-start
  0.7 3.0 %collective-permute-start.4 = (bf16[128,512]{1,0:T(8,128)(2,1)}, bf16[128,512]{1,0:T(8,128)(2,1)S(1)}, u32[]{:S(2)}, u32[]{:S(2)}) collective-permute-start(bf16[128,512]{1,0:T(8,128)(2,1)} %refs_0_.2), channel_id=1, source_target_pairs={{0,1},{1,0},{2,3},{3,2},{4,5},{5,4},{6,7},{7,6},{8,9},{9,8},{10,11... | collective-permute-start | bytes 393224 | tf_op jit(solution)/shard_map/ppermute | solution.py:290
  3.7 1.5 %collective-permute-start.2 = (bf16[128,512]{1,0:T(8,128)(2,1)}, bf16[128,512]{1,0:T(8,128)(2,1)S(1)}, u32[]{:S(2)}, u32[]{:S(2)}) collective-permute-start(bf16[128,512]{1,0:T(8,128)(2,1)} %refs_0_.2), channel_id=1, source_target_pairs={{0,16},{8,24},{16,0},{24,8},{1,17},{9,25},{17,1},{25,9},{2,18},{10... | collective-permute-start | bytes 393224 | tf_op jit(solution)/shard_map/ppermute | solution.py:280
  5.2 3.5 %collective-permute-start.1 = (bf16[128,512]{1,0:T(8,128)(2,1)}, bf16[128,512]{1,0:T(8,128)(2,1)S(1)}, u32[]{:S(2)}, u32[]{:S(2)}) collective-permute-start(bf16[128,512]{1,0:T(8,128)(2,1)} %refs_0_.2), channel_id=1, source_target_pairs={{1,2},{2,1},{3,4},{4,3},{5,6},{6,5},{7,0},{0,7},{9,10},{10,9},{11,... | collective-permute-start | bytes 393224 | tf_op jit(solution)/shard_map/ppermute | solution.py:291
  8.7 0.0 collective-permute-start
  8.7 0.6 %collective-permute-start.3 = (bf16[128,512]{1,0:T(8,128)(2,1)}, bf16[128,512]{1,0:T(8,128)(2,1)S(1)}, u32[]{:S(2)}, u32[]{:S(2)}) collective-permute-start(bf16[128,512]{1,0:T(8,128)(2,1)} %refs_0_.2), channel_id=1, source_target_pairs={{0,8},{8,0},{16,24},{24,16},{1,9},{9,1},{17,25},{25,17},{2,10},{10... | collective-permute-start | bytes 393224 | tf_op jit(solution)/shard_map/ppermute | solution.py:280
  10.0 1.9 %shard_map.104 = (bf16[128,512]{1,0:T(8,128)(2,1)S(1)}, bf16[512,512]{1,0:T(8,128)(2,1)S(1)}, bf16[512,512]{1,0:T(8,128)(2,1)S(1)}, bf16[512,512]{1,0:T(8,128)(2...) custom-call(bf16[128,512]{1,0:T(8,128)(2,1)} %refs_0_.2, ...), custom_call_target="tpu_custom_call" | custom-call | flops 201326592 | bytes 4194304 | tf_op jit(solution)/shard_map/pallas_call | solution.py:260
  11.9 0.0 collective-permute-done.4.refs_0_
  11.9 2.1 %shard_map.105 = (bf16[512,1024]{1,0:T(8,128)(2,1)S(1)}, bf16[256,512]{1,0:T(8,128)(2,1)S(1)}, bf16[256,512]{1,0:T(8,128)(2,1)S(1)}, f32[4,256,256]{2,1,0:T(8,12...) custom-call(bf16[128,512]{1,0:T(8,128)(2,1)S(1)} %collective-permute, ...), custom_call_target="tpu_custom_call" | custom-call | flops 335544320 | bytes 4194304 | tf_op jit(solution)/shard_map/pallas_call | solution.py:260
  14.1 0.0 collective-permute-done.2.refs_4_
  14.1 0.0 collective-permute-done.1.refs_3_
  14.1 0.0 collective-permute-done.refs_2_
  14.1 0.0 collective-permute-done.3.refs_5_
  14.1 4.5 %shard_map.106 = (bf16[128,512]{1,0:T(8,128)(2,1)S(1)}, bf16[128,512]{1,0:T(8,128)(2,1)S(1)}, f32[128,512]{1,0:T(8,128)S(1)}, f32[4,512,256]{2,1,0:T(8,128)S(1)}...) custom-call(s32[1,1]{1,0:T(1,128)S(6)} %copy.11.refs_0_, ...), custom_call_target="tpu_custom_call" | custom-call | flops 1073741824 | bytes 4194304 | tf_op jit(solution)/shard_map/pallas_call | solution.py:260
  18.6 0.0 collective-permute-start.7
  18.6 0.0 collective-permute-start.5
  18.6 2.6 %collective-permute-start.6 = (bf16[128,512]{1,0:T(8,128)(2,1)S(1)}, bf16[128,512]{1,0:T(8,128)(2,1)S(1)}, u32[]{:S(2)}, u32[]{:S(2)}) collective-permute-start(bf16[128,512]{1,0:T(8,128)(2,1)S(1)} %get-tuple-element.71), channel_id=1, source_target_pairs={{1,2},{2,1},{3,4},{4,3},{5,6},{6,5},{7,0},{0,7},{9,10},{10,9},{11,... | collective-permute-start | bytes 393224 | tf_op jit(solution)/shard_map/ppermute | solution.py:344
  21.3 0.0 collective-permute-done.7.refs_2_
  21.3 2.5 %collective-permute-start.8 = (bf16[128,512]{1,0:T(8,128)(2,1)S(1)}, bf16[128,512]{1,0:T(8,128)(2,1)S(1)}, u32[]{:S(2)}, u32[]{:S(2)}) collective-permute-start(bf16[128,512]{1,0:T(8,128)(2,1)S(1)} %add_convert_fusion), channel_id=1, source_target_pairs={{0,16},{8,24},{16,0},{24,8},{1,17},{9,25},{17,1},{25,9},{2,18},{10... | collective-permute-start | bytes 393224 | tf_op jit(solution)/shard_map/ppermute | solution.py:280
  23.8 2.2 %shard_map.107 = (bf16[128,512]{1,0:T(8,128)(2,1)}, f32[128,512]{1,0:T(8,128)S(1)}) custom-call(f32[4,512,256]{2,1,0:T(8,128)S(1)} %get-tuple-element.54.refs_0_, f32[4,1,256]{2,1,0:T(1,128)S(1)} %get-tuple-element.55.refs_1_, f32[8,128]{1,0:T(8,128)S(1)} %get-tuple-element.56.refs_2_, bf16[128,512]{1,0:T(8,128)(2,1)S(1)} %get-tuple-element.57.refs_3_, ...), custom_call_target="tpu_custom_call" | custom-call | flops 469762048 | bytes 4194304 | tf_op jit(solution)/shard_map/pallas_call | solution.py:260
  26.0 0.0 collective-permute-done.5.refs_0_
  26.0 1.3 %collective-permute-done.6.refs_1_ = bf16[128,512]{1,0:T(8,128)(2,1)S(1)} collective-permute-done((bf16[128,512]{1,0:T(8,128)(2,1)S(1)}, bf16[128,512]{1,0:T(8,128)(2,1)S(1)}, u32[]{:S(2)}, u32[]{:S(2)}) %collective-permute-start.6) | collective-permute-done | bytes 131104 | tf_op jit(solution)/shard_map/ppermute | solution.py:344
  27.3 0.1 collective-permute-done.8.refs_3_
  27.4 0.9 %shard_map.108 = bf16[128,512]{1,0:T(8,128)(2,1)} custom-call(f32[128,512]{1,0:T(8,128)S(1)} %get-tuple-element.66.unit_ref, f32[128,1]{1,0:T(8,128)S(1)} %get-tuple-element.67.inv_ref, f32[128,512]{1,0:T(8,128)S(1)} %get-tuple-element.68.gres_ref, f32[128,512]{1,0:T(8,128)S(1)} %get-tuple-element.69.acc_ref, ...), custom_call_target="tpu_custom_call" | custom-call | bytes 4194304 | tf_op jit(solution)/shard_map/pallas_call | solution.py:260
  (4 shorter events, 0.0 us)
Async XLA Ops:
  0.6 11.3 %copy-start = (bf16[1024,512]{1,0:T(8,128)(2,1)S(1)}, bf16[1024,512]{1,0:T(8,128)(2,1)}, u32[]{:S(2)}) copy-start(bf16[1024,512]{1,0:T(8,128)(2,1)} %refs_15_.1) | copy-start | bytes 3145732
  0.6 11.3 %copy-start.1 = (bf16[512,512]{1,0:T(8,128)(2,1)S(1)}, bf16[512,512]{1,0:T(8,128)(2,1)}, u32[]{:S(2)}) copy-start(bf16[512,512]{1,0:T(8,128)(2,1)} %refs_13_.1) | copy-start | bytes 1572868
  0.7 11.3 %collective-permute-start.4 = (bf16[128,512]{1,0:T(8,128)(2,1)}, bf16[128,512]{1,0:T(8,128)(2,1)S(1)}, u32[]{:S(2)}, u32[]{:S(2)}) collective-permute-start(bf16[128,512]{1,0:T(8,128)(2,1)} %refs_0_.2), channel_id=1, source_target_pairs={{0,1},{1,0},{2,3},{3,2},{4,5},{5,4},{6,7},{7,6},{8,9},{9,8},{10,11... | collective-permute-start | bytes 393224 | tf_op jit(solution)/shard_map/ppermute | solution.py:290
  3.7 10.4 %collective-permute-start.2 = (bf16[128,512]{1,0:T(8,128)(2,1)}, bf16[128,512]{1,0:T(8,128)(2,1)S(1)}, u32[]{:S(2)}, u32[]{:S(2)}) collective-permute-start(bf16[128,512]{1,0:T(8,128)(2,1)} %refs_0_.2), channel_id=1, source_target_pairs={{0,16},{8,24},{16,0},{24,8},{1,17},{9,25},{17,1},{25,9},{2,18},{10... | collective-permute-start | bytes 393224 | tf_op jit(solution)/shard_map/ppermute | solution.py:280
  5.2 8.9 %collective-permute-start.1 = (bf16[128,512]{1,0:T(8,128)(2,1)}, bf16[128,512]{1,0:T(8,128)(2,1)S(1)}, u32[]{:S(2)}, u32[]{:S(2)}) collective-permute-start(bf16[128,512]{1,0:T(8,128)(2,1)} %refs_0_.2), channel_id=1, source_target_pairs={{1,2},{2,1},{3,4},{4,3},{5,6},{6,5},{7,0},{0,7},{9,10},{10,9},{11,... | collective-permute-start | bytes 393224 | tf_op jit(solution)/shard_map/ppermute | solution.py:291
  8.7 5.4 %collective-permute-start = (bf16[128,512]{1,0:T(8,128)(2,1)}, bf16[128,512]{1,0:T(8,128)(2,1)S(1)}, u32[]{:S(2)}, u32[]{:S(2)}) collective-permute-start(bf16[128,512]{1,0:T(8,128)(2,1)} %refs_0_.2), channel_id=1, source_target_pairs={{0,24},{8,16},{16,8},{24,0},{1,25},{9,17},{17,9},{25,1},{2,26},{10... | collective-permute-start | bytes 393224 | tf_op jit(solution)/shard_map/ppermute | solution.py:280
  8.7 5.4 %collective-permute-start.3 = (bf16[128,512]{1,0:T(8,128)(2,1)}, bf16[128,512]{1,0:T(8,128)(2,1)S(1)}, u32[]{:S(2)}, u32[]{:S(2)}) collective-permute-start(bf16[128,512]{1,0:T(8,128)(2,1)} %refs_0_.2), channel_id=1, source_target_pairs={{0,8},{8,0},{16,24},{24,16},{1,9},{9,1},{17,25},{25,17},{2,10},{10... | collective-permute-start | bytes 393224 | tf_op jit(solution)/shard_map/ppermute | solution.py:280
  18.6 2.7 %collective-permute-start.7 = (bf16[256,512]{1,0:T(8,128)(2,1)S(1)}, bf16[256,512]{1,0:T(8,128)(2,1)S(1)}, u32[]{:S(2)}, u32[]{:S(2)}) collective-permute-start(bf16[256,512]{1,0:T(8,128)(2,1)S(1)} %get-tuple-element.72), channel_id=1, source_target_pairs={{0,8},{8,0},{16,24},{24,16},{1,9},{9,1},{17,25},{25,17},{2,10},{10... | collective-permute-start | bytes 786440 | tf_op jit(solution)/shard_map/ppermute | solution.py:280
  18.6 7.4 %collective-permute-start.5 = (bf16[128,512]{1,0:T(8,128)(2,1)S(1)}, bf16[128,512]{1,0:T(8,128)(2,1)S(1)}, u32[]{:S(2)}, u32[]{:S(2)}) collective-permute-start(bf16[128,512]{1,0:T(8,128)(2,1)S(1)} %get-tuple-element.70), channel_id=1, source_target_pairs={{0,1},{1,0},{2,3},{3,2},{4,5},{5,4},{6,7},{7,6},{8,9},{9,8},{10,11... | collective-permute-start | bytes 393224 | tf_op jit(solution)/shard_map/ppermute | solution.py:342
  18.6 8.7 %collective-permute-start.6 = (bf16[128,512]{1,0:T(8,128)(2,1)S(1)}, bf16[128,512]{1,0:T(8,128)(2,1)S(1)}, u32[]{:S(2)}, u32[]{:S(2)}) collective-permute-start(bf16[128,512]{1,0:T(8,128)(2,1)S(1)} %get-tuple-element.71), channel_id=1, source_target_pairs={{1,2},{2,1},{3,4},{4,3},{5,6},{6,5},{7,0},{0,7},{9,10},{10,9},{11,... | collective-permute-start | bytes 393224 | tf_op jit(solution)/shard_map/ppermute | solution.py:344
  21.3 6.1 %collective-permute-start.8 = (bf16[128,512]{1,0:T(8,128)(2,1)S(1)}, bf16[128,512]{1,0:T(8,128)(2,1)S(1)}, u32[]{:S(2)}, u32[]{:S(2)}) collective-permute-start(bf16[128,512]{1,0:T(8,128)(2,1)S(1)} %add_convert_fusion), channel_id=1, source_target_pairs={{0,16},{8,24},{16,0},{24,8},{1,17},{9,25},{17,1},{25,9},{2,18},{10... | collective-permute-start | bytes 393224 | tf_op jit(solution)/shard_map/ppermute | solution.py:280

commit v6 on v5

--- a/solution.py
+++ b/solution.py
@@ -79,10 +79,10 @@
 
 
 def own_kernel(*refs):
-    given, held = refs[:5], refs[5:10]
-    q_ref, k_ref, v_ref, unit_ref, inv_ref, sem = refs[10:]
+    given, held = refs[:6], refs[6:12]
+    q_ref, k_ref, v_ref, unit_ref, inv_ref, sem = refs[12:]
     copies = fetch(given, held, sem)
-    x_ref, wk_ref, wv_ref, wq_ref, _ = held
+    x_ref, wk_ref, wv_ref, wq_ref = held[:4]
     copies[0].wait()
     unit, inv = normalize(x_ref[...].astype(f32))
     unit_ref[...] = unit
@@ -95,6 +95,7 @@
     copies[3].wait()
     q_ref[...] = (dot(normed, wq_ref[...]) * SCALE).astype(bf16)
     copies[4].wait()
+    copies[5].wait()
 
 
 def pair_columns():
@@ -102,10 +103,9 @@
 
 
 def early_kernel(*refs):
-    near_a, q_ref, k_ref, v_ref, wk_ref, wv_ref, cot_ref, wdown_ref, wout_ref, given = refs[:10]
-    wup_ref, ke_ref, ve_ref, se_ref, gact_ref, q2t_ref, *turned, sem = refs[10:]
+    near_a, q_ref, k_ref, v_ref, wk_ref, wv_ref, cot_ref, wdown_ref, wout_ref, wup_ref = refs[:10]
+    ke_ref, ve_ref, se_ref, gact_ref, q2t_ref, *turned = refs[10:]
     rows = q_ref.shape[0]
-    (copy,) = fetch([given], [wup_ref], sem)
     unit, _ = normalize(near_a[...].astype(f32))
     normed = unit.astype(bf16)
     ke_ref[:rows, :] = k_ref[...]
@@ -117,10 +117,8 @@
         q2t_ref[j] = q2t
         se_ref[j] = dot(ke_ref[:, cols], q2t)
     gact_ref[...] = dot_t(cot_ref[...], wdown_ref[...])
-    for weight, out_ref in zip((wk_ref, wv_ref, wout_ref), turned):
+    for weight, out_ref in zip((wk_ref, wv_ref, wout_ref, wup_ref), turned):
         out_ref[...] = weight[...].T
-    copy.wait()
-    turned[3][...] = wup_ref[...].T
 
 
 def block_back(v, q, g, weights, inv, row):
@@ -294,8 +292,8 @@
     def in_hbm(*arrays):
         return [pltpu.with_memory_space_constraint(array, pltpu.HBM) for array in arrays]
 
-    given = [nodes, w_key, w_value, w_query, cotangent]
-    x, w_key, w_value, w_query, cotangent, q, k, v, unit, inv_std = call(
+    given = [nodes, w_key, w_value, w_query, cotangent, w_up]
+    x, w_key, w_value, w_query, cotangent, w_up, q, k, v, unit, inv_std = call(
         own_kernel,
         [(array.shape, array.dtype) for array in given]
         + [((rows, width), bf16)] * 3
@@ -309,16 +307,13 @@
     early = 2 * rows
     late = (1 + listed) * rows
     keys = early + late
-    w_up, ke, ve, se, gact, q2t, wk_t, wv_t, wout_t, wup_t = call(
+    ke, ve, se, gact, q2t, wk_t, wv_t, wout_t, wup_t = call(
         early_kernel,
-        [(w_up.shape, bf16)]
-        + [((early, width), bf16)] * 2
+        [((early, width), bf16)] * 2
         + [((H // 2, early, 2 * rows), f32), ((rows, hidden), f32), ((H // 2, PAIR, 2 * rows), bf16)]
         + [((width, width), bf16)] * 3
         + [((hidden, width), bf16)],
-        [near_a, q, k, v, w_key, w_value, cotangent, w_down, w_out] + in_hbm(w_up),
-        [pltpu.SemaphoreType.DMA((1,))],
-        hbm=1,
+        [near_a, q, k, v, w_key, w_value, cotangent, w_down, w_out, w_up],
         flops=2 * early * width * (2 * width + 2 * rows),
     )
     sent = sent_slots(groups)

time: 28.5 us -> 28.2 us (0.989)
  waiting for transfers between devices: 1.41 us -> 3.17 us
  Pallas kernels: 11.6 us -> 10.4 us
  starting transfers between devices: 13.9 us -> 13 us
    pallas_call x5, Pallas kernels: 11.6 us -> 10.4 us  [call(): pl.pallas_call(kernel, out_shape=[jax.ShapeDtypeStruct(shape, dtype) for...]
    ppermute x5, starting transfers between devices: 4.64 us -> 3.5 us  [exchanged(): return lax.ppermute(array, 'blk', [(i, i ^ slot) for i in range(groups)])]
    ppermute x1, waiting for transfers between devices: 1.34 us -> 2.16 us  [on_device(): from_b = lax.ppermute(send_b, 'dom', pairs_b)]
    ppermute x5, waiting for transfers between devices: 0.06 us -> 0.86 us  [exchanged(): return lax.ppermute(array, 'blk', [(i, i ^ slot) for i in range(groups)])]
  transfers between devices with their start and end apart: 9 -> 9, of which waited for: 2 -> 4; matrix products, arithmetic and copies ran while one was open for 0% -> 0% of each run, Pallas kernels for 22% -> 18%
where the time goes in v6:
time: 28.2 us; the launch traced here: 28 us
  starting transfers between devices  13 us (46%)
  Pallas kernels  10.4 us (37%)
  waiting for transfers between devices  3.17 us (11%)
  between operations  1.37 us (5%)
    pallas_call x5, Pallas kernels, call(): pl.pallas_call(kernel, out_shape=[jax.ShapeDtypeStruct(shape, dtype) for...  10.4 us
    ppermute x1, starting transfers between devices, on_device(): near_b = lax.ppermute(nodes, 'dom', pairs_b)  3.54 us
    ppermute x5, starting transfers between devices, exchanged(): return lax.ppermute(array, 'blk', [(i, i ^ slot) for i in range(groups)])  3.5 us
    ppermute x1, starting transfers between devices, on_device(): near_a = lax.ppermute(nodes, 'dom', pairs_a)  3.03 us
    ppermute x1, starting transfers between devices, on_device(): from_b = lax.ppermute(send_b, 'dom', pairs_b)  2.87 us
    ppermute x1, waiting for transfers between devices, on_device(): from_b = lax.ppermute(send_b, 'dom', pairs_b)  2.16 us
    ppermute x5, waiting for transfers between devices, exchanged(): return lax.ppermute(array, 'blk', [(i, i ^ slot) for i in range(groups)])  0.86 us
  transfers between devices with their start and end apart: 9, of which 4 were waited for; matrix products, arithmetic and copies ran while one was open for 0% of the time, Pallas kernels for 18%

profile of v6, /device:TPU:0, one launch (start us, length us, event | category | flops | bytes accessed | tf_op | source)
XLA Modules:
  0.0 28.0 jit_solution(12752150513103386757)
XLA Ops:
  0.7 3.0 %collective-permute-start.4 = (bf16[128,512]{1,0:T(8,128)(2,1)}, bf16[128,512]{1,0:T(8,128)(2,1)S(1)}, u32[]{:S(2)}, u32[]{:S(2)}) collective-permute-start(bf16[128,512]{1,0:T(8,128)(2,1)} %refs_0_.2), channel_id=1, source_target_pairs={{0,1},{1,0},{2,3},{3,2},{4,5},{5,4},{6,7},{7,6},{8,9},{9,8},{10,11... | collective-permute-start | bytes 393224 | tf_op jit(solution)/shard_map/ppermute | solution.py:288
  3.7 1.5 %collective-permute-start.2 = (bf16[128,512]{1,0:T(8,128)(2,1)}, bf16[128,512]{1,0:T(8,128)(2,1)S(1)}, u32[]{:S(2)}, u32[]{:S(2)}) collective-permute-start(bf16[128,512]{1,0:T(8,128)(2,1)} %refs_0_.2), channel_id=1, source_target_pairs={{0,16},{8,24},{16,0},{24,8},{1,17},{9,25},{17,1},{25,9},{2,18},{10... | collective-permute-start | bytes 393224 | tf_op jit(solution)/shard_map/ppermute | solution.py:278
  5.2 3.5 %collective-permute-start.1 = (bf16[128,512]{1,0:T(8,128)(2,1)}, bf16[128,512]{1,0:T(8,128)(2,1)S(1)}, u32[]{:S(2)}, u32[]{:S(2)}) collective-permute-start(bf16[128,512]{1,0:T(8,128)(2,1)} %refs_0_.2), channel_id=1, source_target_pairs={{1,2},{2,1},{3,4},{4,3},{5,6},{6,5},{7,0},{0,7},{9,10},{10,9},{11,... | collective-permute-start | bytes 393224 | tf_op jit(solution)/shard_map/ppermute | solution.py:289
  8.7 0.0 collective-permute-start
  8.7 0.6 %collective-permute-start.3 = (bf16[128,512]{1,0:T(8,128)(2,1)}, bf16[128,512]{1,0:T(8,128)(2,1)S(1)}, u32[]{:S(2)}, u32[]{:S(2)}) collective-permute-start(bf16[128,512]{1,0:T(8,128)(2,1)} %refs_0_.2), channel_id=1, source_target_pairs={{0,8},{8,0},{16,24},{24,16},{1,9},{9,1},{17,25},{25,17},{2,10},{10... | collective-permute-start | bytes 393224 | tf_op jit(solution)/shard_map/ppermute | solution.py:278
  10.0 1.9 %shard_map.104 = (bf16[128,512]{1,0:T(8,128)(2,1)S(1)}, bf16[512,512]{1,0:T(8,128)(2,1)S(1)}, bf16[512,512]{1,0:T(8,128)(2,1)S(1)}, bf16[512,512]{1,0:T(8,128)(2...) custom-call(bf16[128,512]{1,0:T(8,128)(2,1)} %refs_0_.2, ...), custom_call_target="tpu_custom_call" | custom-call | flops 201326592 | bytes 4194304 | tf_op jit(solution)/shard_map/pallas_call | solution.py:258
  11.9 0.0 collective-permute-done.4.refs_0_
  11.9 0.0 copy-done
  11.9 1.0 %shard_map.105 = (bf16[256,512]{1,0:T(8,128)(2,1)S(1)}, bf16[256,512]{1,0:T(8,128)(2,1)S(1)}, f32[4,256,256]{2,1,0:T(8,128)S(1)}, f32[128,1024]{1,0:T(8,128)S(1)...) custom-call(bf16[128,512]{1,0:T(8,128)(2,1)S(1)} %collective-permute, ...), custom_call_target="tpu_custom_call" | custom-call | flops 335544320 | bytes 4194304 | tf_op jit(solution)/shard_map/pallas_call | solution.py:258
  13.0 0.0 collective-permute-done.2.refs_4_
  13.0 0.1 collective-permute-done.1.refs_3_
  13.1 0.9 %collective-permute-done.refs_2_ = bf16[128,512]{1,0:T(8,128)(2,1)S(1)} collective-permute-done((bf16[128,512]{1,0:T(8,128)(2,1)}, bf16[128,512]{1,0:T(8,128)(2,1)S(1)}, u32[]{:S(2)}, u32[]{:S(2)}) %collective-permute-start) | collective-permute-done | bytes 131104 | tf_op jit(solution)/shard_map/ppermute | solution.py:278
  13.9 0.0 collective-permute-done.3.refs_5_
  13.9 4.5 %shard_map.106 = (bf16[128,512]{1,0:T(8,128)(2,1)S(1)}, bf16[128,512]{1,0:T(8,128)(2,1)S(1)}, f32[128,512]{1,0:T(8,128)S(1)}, f32[4,512,256]{2,1,0:T(8,128)S(1)}...) custom-call(s32[1,1]{1,0:T(1,128)S(6)} %copy.11.refs_0_, ...), custom_call_target="tpu_custom_call" | custom-call | flops 1073741824 | bytes 4194304 | tf_op jit(solution)/shard_map/pallas_call | solution.py:258
  18.4 0.0 collective-permute-start.7
  18.4 0.0 collective-permute-start.5
  18.4 2.9 %collective-permute-start.6 = (bf16[128,512]{1,0:T(8,128)(2,1)S(1)}, bf16[128,512]{1,0:T(8,128)(2,1)S(1)}, u32[]{:S(2)}, u32[]{:S(2)}) collective-permute-start(bf16[128,512]{1,0:T(8,128)(2,1)S(1)} %get-tuple-element.71), channel_id=1, source_target_pairs={{1,2},{2,1},{3,4},{4,3},{5,6},{6,5},{7,0},{0,7},{9,10},{10,9},{11,... | collective-permute-start | bytes 393224 | tf_op jit(solution)/shard_map/ppermute | solution.py:339
  21.3 0.0 collective-permute-done.7.refs_2_
  21.3 1.4 %collective-permute-start.8 = (bf16[128,512]{1,0:T(8,128)(2,1)S(1)}, bf16[128,512]{1,0:T(8,128)(2,1)S(1)}, u32[]{:S(2)}, u32[]{:S(2)}) collective-permute-start(bf16[128,512]{1,0:T(8,128)(2,1)S(1)} %add_convert_fusion), channel_id=1, source_target_pairs={{0,16},{8,24},{16,0},{24,8},{1,17},{9,25},{17,1},{25,9},{2,18},{10... | collective-permute-start | bytes 393224 | tf_op jit(solution)/shard_map/ppermute | solution.py:278
  22.7 2.2 %shard_map.107 = (bf16[128,512]{1,0:T(8,128)(2,1)}, f32[128,512]{1,0:T(8,128)S(1)}) custom-call(f32[4,512,256]{2,1,0:T(8,128)S(1)} %get-tuple-element.54.refs_0_, f32[4,1,256]{2,1,0:T(1,128)S(1)} %get-tuple-element.55.refs_1_, f32[8,128]{1,0:T(8,128)S(1)} %get-tuple-element.56.refs_2_, bf16[128,512]{1,0:T(8,128)(2,1)S(1)} %get-tuple-element.57.refs_3_, ...), custom_call_target="tpu_custom_call" | custom-call | flops 469762048 | bytes 4194304 | tf_op jit(solution)/shard_map/pallas_call | solution.py:258
  24.9 0.1 collective-permute-done.5.refs_0_
  24.9 2.2 %collective-permute-done.6.refs_1_ = bf16[128,512]{1,0:T(8,128)(2,1)S(1)} collective-permute-done((bf16[128,512]{1,0:T(8,128)(2,1)S(1)}, bf16[128,512]{1,0:T(8,128)(2,1)S(1)}, u32[]{:S(2)}, u32[]{:S(2)}) %collective-permute-start.6) | collective-permute-done | bytes 131104 | tf_op jit(solution)/shard_map/ppermute | solution.py:339
  27.1 0.0 collective-permute-done.8.refs_3_
  27.1 0.9 %shard_map.108 = bf16[128,512]{1,0:T(8,128)(2,1)} custom-call(f32[128,512]{1,0:T(8,128)S(1)} %get-tuple-element.66.unit_ref, f32[128,1]{1,0:T(8,128)S(1)} %get-tuple-element.67.inv_ref, f32[128,512]{1,0:T(8,128)S(1)} %get-tuple-element.68.gres_ref, f32[128,512]{1,0:T(8,128)S(1)} %get-tuple-element.69.acc_ref, ...), custom_call_target="tpu_custom_call" | custom-call | bytes 4194304 | tf_op jit(solution)/shard_map/pallas_call | solution.py:258
  (4 shorter events, 0.0 us)
Async XLA Ops:
  0.6 11.3 %copy-start = (bf16[1024,512]{1,0:T(8,128)(2,1)S(1)}, bf16[1024,512]{1,0:T(8,128)(2,1)}, u32[]{:S(2)}) copy-start(bf16[1024,512]{1,0:T(8,128)(2,1)} %refs_15_.1) | copy-start | bytes 3145732
  0.6 11.3 %copy-start.1 = (bf16[512,512]{1,0:T(8,128)(2,1)S(1)}, bf16[512,512]{1,0:T(8,128)(2,1)}, u32[]{:S(2)}) copy-start(bf16[512,512]{1,0:T(8,128)(2,1)} %refs_13_.1) | copy-start | bytes 1572868
  0.7 11.3 %collective-permute-start.4 = (bf16[128,512]{1,0:T(8,128)(2,1)}, bf16[128,512]{1,0:T(8,128)(2,1)S(1)}, u32[]{:S(2)}, u32[]{:S(2)}) collective-permute-start(bf16[128,512]{1,0:T(8,128)(2,1)} %refs_0_.2), channel_id=1, source_target_pairs={{0,1},{1,0},{2,3},{3,2},{4,5},{5,4},{6,7},{7,6},{8,9},{9,8},{10,11... | collective-permute-start | bytes 393224 | tf_op jit(solution)/shard_map/ppermute | solution.py:288
  3.7 9.3 %collective-permute-start.2 = (bf16[128,512]{1,0:T(8,128)(2,1)}, bf16[128,512]{1,0:T(8,128)(2,1)S(1)}, u32[]{:S(2)}, u32[]{:S(2)}) collective-permute-start(bf16[128,512]{1,0:T(8,128)(2,1)} %refs_0_.2), channel_id=1, source_target_pairs={{0,16},{8,24},{16,0},{24,8},{1,17},{9,25},{17,1},{25,9},{2,18},{10... | collective-permute-start | bytes 393224 | tf_op jit(solution)/shard_map/ppermute | solution.py:278
  5.2 7.9 %collective-permute-start.1 = (bf16[128,512]{1,0:T(8,128)(2,1)}, bf16[128,512]{1,0:T(8,128)(2,1)S(1)}, u32[]{:S(2)}, u32[]{:S(2)}) collective-permute-start(bf16[128,512]{1,0:T(8,128)(2,1)} %refs_0_.2), channel_id=1, source_target_pairs={{1,2},{2,1},{3,4},{4,3},{5,6},{6,5},{7,0},{0,7},{9,10},{10,9},{11,... | collective-permute-start | bytes 393224 | tf_op jit(solution)/shard_map/ppermute | solution.py:289
  8.7 5.2 %collective-permute-start = (bf16[128,512]{1,0:T(8,128)(2,1)}, bf16[128,512]{1,0:T(8,128)(2,1)S(1)}, u32[]{:S(2)}, u32[]{:S(2)}) collective-permute-start(bf16[128,512]{1,0:T(8,128)(2,1)} %refs_0_.2), channel_id=1, source_target_pairs={{0,24},{8,16},{16,8},{24,0},{1,25},{9,17},{17,9},{25,1},{2,26},{10... | collective-permute-start | bytes 393224 | tf_op jit(solution)/shard_map/ppermute | solution.py:278
  8.7 5.2 %collective-permute-start.3 = (bf16[128,512]{1,0:T(8,128)(2,1)}, bf16[128,512]{1,0:T(8,128)(2,1)S(1)}, u32[]{:S(2)}, u32[]{:S(2)}) collective-permute-start(bf16[128,512]{1,0:T(8,128)(2,1)} %refs_0_.2), channel_id=1, source_target_pairs={{0,8},{8,0},{16,24},{24,16},{1,9},{9,1},{17,25},{25,17},{2,10},{10... | collective-permute-start | bytes 393224 | tf_op jit(solution)/shard_map/ppermute | solution.py:278
  18.4 2.9 %collective-permute-start.7 = (bf16[256,512]{1,0:T(8,128)(2,1)S(1)}, bf16[256,512]{1,0:T(8,128)(2,1)S(1)}, u32[]{:S(2)}, u32[]{:S(2)}) collective-permute-start(bf16[256,512]{1,0:T(8,128)(2,1)S(1)} %get-tuple-element.72), channel_id=1, source_target_pairs={{0,8},{8,0},{16,24},{24,16},{1,9},{9,1},{17,25},{25,17},{2,10},{10... | collective-permute-start | bytes 786440 | tf_op jit(solution)/shard_map/ppermute | solution.py:278
  18.4 6.6 %collective-permute-start.5 = (bf16[128,512]{1,0:T(8,128)(2,1)S(1)}, bf16[128,512]{1,0:T(8,128)(2,1)S(1)}, u32[]{:S(2)}, u32[]{:S(2)}) collective-permute-start(bf16[128,512]{1,0:T(8,128)(2,1)S(1)} %get-tuple-element.70), channel_id=1, source_target_pairs={{0,1},{1,0},{2,3},{3,2},{4,5},{5,4},{6,7},{7,6},{8,9},{9,8},{10,11... | collective-permute-start | bytes 393224 | tf_op jit(solution)/shard_map/ppermute | solution.py:337
  18.4 8.7 %collective-permute-start.6 = (bf16[128,512]{1,0:T(8,128)(2,1)S(1)}, bf16[128,512]{1,0:T(8,128)(2,1)S(1)}, u32[]{:S(2)}, u32[]{:S(2)}) collective-permute-start(bf16[128,512]{1,0:T(8,128)(2,1)S(1)} %get-tuple-element.71), channel_id=1, source_target_pairs={{1,2},{2,1},{3,4},{4,3},{5,6},{6,5},{7,0},{0,7},{9,10},{10,9},{11,... | collective-permute-start | bytes 393224 | tf_op jit(solution)/shard_map/ppermute | solution.py:339
  21.3 5.8 %collective-permute-start.8 = (bf16[128,512]{1,0:T(8,128)(2,1)S(1)}, bf16[128,512]{1,0:T(8,128)(2,1)S(1)}, u32[]{:S(2)}, u32[]{:S(2)}) collective-permute-start(bf16[128,512]{1,0:T(8,128)(2,1)S(1)} %add_convert_fusion), channel_id=1, source_target_pairs={{0,16},{8,24},{16,0},{24,8},{1,17},{9,25},{17,1},{25,9},{2,18},{10... | collective-permute-start | bytes 393224 | tf_op jit(solution)/shard_map/ppermute | solution.py:278

commit v7 on v6

--- a/solution.py
+++ b/solution.py
@@ -133,8 +133,8 @@
 
 def main_kernel(groups, listed, *refs):
     experts_ref = refs[0]
-    near_b = refs[3]
-    slots = refs[1:2] + refs[1 + groups : 3 : -1] + refs[2:3]
+    near_b = refs[2]
+    slots = refs[1:2] + refs[1 + groups : 2 + groups] + refs[3 : 1 + groups]
     (x_ref, ve_ref, se_ref, q_ref, q2t_ref, wk_ref, wv_ref) = refs[2 + groups : 9 + groups]
     (wout_ref, wup_ref, cot_ref, gact_ref) = refs[9 + groups : 13 + groups]
     wk_t, wv_t, wout_t, wup_t = refs[13 + groups : 17 + groups]
@@ -287,7 +287,7 @@
 
     near_a = lax.ppermute(nodes, "dom", pairs_a)
     near_b = lax.ppermute(nodes, "dom", pairs_b)
-    held = {slot: exchanged(nodes, slot) for slot in range(1, groups)}
+    held = {slot: exchanged(nodes, slot) for slot in range(2, groups)}
 
     def in_hbm(*arrays):
         return [pltpu.with_memory_space_constraint(array, pltpu.HBM) for array in arrays]
@@ -304,6 +304,7 @@
         hbm=len(given),
     )
     held[0] = x
+    held[1] = exchanged(x, 1)
     early = 2 * rows
     late = (1 + listed) * rows
     keys = early + late
@@ -326,8 +327,9 @@
         + [((rows, width), f32)] * 2
         + [((len(slots) * rows, width), bf16) for slots in sent],
         [experts_list]
-        + [x, held[groups - 1], near_b]
-        + [held[slot] for slot in range(groups - 2, 0, -1)]
+        + [x, near_b]
+        + [held[slot] for slot in range(2, groups)]
+        + [held[1]]
         + [x, ve, se, q, q2t, w_key, w_value]
         + [w_out, w_up, cotangent, gact, wk_t, wv_t, wout_t, wup_t],
         [pltpu.VMEM((late, width), bf16), pltpu.VMEM((rows, width), bf16)]

time: 28.2 us -> 28.2 us (level)
  transfers between devices with their start and end apart: 9 -> 9, of which waited for: 4 -> 3; matrix products, arithmetic and copies ran while one was open for 0% -> 0% of each run, Pallas kernels for 18% -> 18%
where the time goes in v7:
time: 28.2 us; the launch traced here: 28 us
  starting transfers between devices  13 us (46%)
  Pallas kernels  10.5 us (37%)
  waiting for transfers between devices  3.09 us (11%)
  between operations  1.38 us (5%)
    pallas_call x5, Pallas kernels, call(): pl.pallas_call(kernel, out_shape=[jax.ShapeDtypeStruct(shape, dtype) for...  10.5 us
    ppermute x5, starting transfers between devices, exchanged(): return lax.ppermute(array, 'blk', [(i, i ^ slot) for i in range(groups)])  3.56 us
    ppermute x1, starting transfers between devices, on_device(): near_b = lax.ppermute(nodes, 'dom', pairs_b)  3.54 us
    ppermute x1, starting transfers between devices, on_device(): near_a = lax.ppermute(nodes, 'dom', pairs_a)  3.03 us
    ppermute x1, starting transfers between devices, on_device(): from_b = lax.ppermute(send_b, 'dom', pairs_b)  2.83 us
    ppermute x1, waiting for transfers between devices, on_device(): from_b = lax.ppermute(send_b, 'dom', pairs_b)  2.16 us
    ppermute x5, waiting for transfers between devices, exchanged(): return lax.ppermute(array, 'blk', [(i, i ^ slot) for i in range(groups)])  0.85 us
  transfers between devices with their start and end apart: 9, of which 3 were waited for; matrix products, arithmetic and copies ran while one was open for 0% of the time, Pallas kernels for 18%

profile of v7, /device:TPU:0, one launch (start us, length us, event | category | flops | bytes accessed | tf_op | source)
XLA Modules:
  0.0 28.0 jit_solution(8770461124052840900)
XLA Ops:
  0.7 3.0 %collective-permute-start.4 = (bf16[128,512]{1,0:T(8,128)(2,1)}, bf16[128,512]{1,0:T(8,128)(2,1)S(1)}, u32[]{:S(2)}, u32[]{:S(2)}) collective-permute-start(bf16[128,512]{1,0:T(8,128)(2,1)} %refs_0_.2), channel_id=1, source_target_pairs={{0,1},{1,0},{2,3},{3,2},{4,5},{5,4},{6,7},{7,6},{8,9},{9,8},{10,11... | collective-permute-start | bytes 393224 | tf_op jit(solution)/shard_map/ppermute | solution.py:288
  3.7 1.5 %collective-permute-start.1 = (bf16[128,512]{1,0:T(8,128)(2,1)}, bf16[128,512]{1,0:T(8,128)(2,1)S(1)}, u32[]{:S(2)}, u32[]{:S(2)}) collective-permute-start(bf16[128,512]{1,0:T(8,128)(2,1)} %refs_0_.2), channel_id=1, source_target_pairs={{0,16},{8,24},{16,0},{24,8},{1,17},{9,25},{17,1},{25,9},{2,18},{10... | collective-permute-start | bytes 393224 | tf_op jit(solution)/shard_map/ppermute | solution.py:278
  5.2 3.5 %collective-permute-start = (bf16[128,512]{1,0:T(8,128)(2,1)}, bf16[128,512]{1,0:T(8,128)(2,1)S(1)}, u32[]{:S(2)}, u32[]{:S(2)}) collective-permute-start(bf16[128,512]{1,0:T(8,128)(2,1)} %refs_0_.2), channel_id=1, source_target_pairs={{1,2},{2,1},{3,4},{4,3},{5,6},{6,5},{7,0},{0,7},{9,10},{10,9},{11,... | collective-permute-start | bytes 393224 | tf_op jit(solution)/shard_map/ppermute | solution.py:289
  8.7 0.0 collective-permute-start.2
  8.7 1.9 %shard_map.104 = (bf16[128,512]{1,0:T(8,128)(2,1)S(1)}, bf16[512,512]{1,0:T(8,128)(2,1)S(1)}, bf16[512,512]{1,0:T(8,128)(2,1)S(1)}, bf16[512,512]{1,0:T(8,128)(2...) custom-call(bf16[128,512]{1,0:T(8,128)(2,1)} %refs_0_.2, ...), custom_call_target="tpu_custom_call" | custom-call | flops 201326592 | bytes 4194304 | tf_op jit(solution)/shard_map/pallas_call | solution.py:258
  10.7 0.7 %collective-permute-start.3 = (bf16[128,512]{1,0:T(8,128)(2,1)S(1)}, bf16[128,512]{1,0:T(8,128)(2,1)S(1)}, u32[]{:S(2)}, u32[]{:S(2)}) collective-permute-start(bf16[128,512]{1,0:T(8,128)(2,1)S(1)} %get-tuple-element.38.refs_1_.refs_6_), channel_id=1, source_target_pairs={{0,8},{8,0},{16,24},{24,16},{1,9},{9,1},{17,25},{25,17},{2,10},{10... | collective-permute-start | bytes 393224 | tf_op jit(solution)/shard_map/ppermute | solution.py:278
  12.0 0.0 collective-permute-done.4.refs_0_
  12.0 0.0 copy-done
  12.0 1.0 %shard_map.105 = (bf16[256,512]{1,0:T(8,128)(2,1)S(1)}, bf16[256,512]{1,0:T(8,128)(2,1)S(1)}, f32[4,256,256]{2,1,0:T(8,128)S(1)}, f32[128,1024]{1,0:T(8,128)S(1)...) custom-call(bf16[128,512]{1,0:T(8,128)(2,1)S(1)} %collective-permute, ...), custom_call_target="tpu_custom_call" | custom-call | flops 335544320 | bytes 4194304 | tf_op jit(solution)/shard_map/pallas_call | solution.py:258
  13.0 0.0 collective-permute-done.1.refs_3_
  13.1 0.0 collective-permute-done.refs_2_
  13.1 0.8 %collective-permute-done.2.refs_4_ = bf16[128,512]{1,0:T(8,128)(2,1)S(1)} collective-permute-done((bf16[128,512]{1,0:T(8,128)(2,1)}, bf16[128,512]{1,0:T(8,128)(2,1)S(1)}, u32[]{:S(2)}, u32[]{:S(2)}) %collective-permute-start.2) | collective-permute-done | bytes 131104 | tf_op jit(solution)/shard_map/ppermute | solution.py:278
  13.9 0.0 collective-permute-done.3.refs_5_
  13.9 4.5 %shard_map.106 = (bf16[128,512]{1,0:T(8,128)(2,1)S(1)}, bf16[128,512]{1,0:T(8,128)(2,1)S(1)}, f32[128,512]{1,0:T(8,128)S(1)}, f32[4,512,256]{2,1,0:T(8,128)S(1)}...) custom-call(s32[1,1]{1,0:T(1,128)S(6)} %copy.11.refs_0_, ...), custom_call_target="tpu_custom_call" | custom-call | flops 1073741824 | bytes 4194304 | tf_op jit(solution)/shard_map/pallas_call | solution.py:258
  18.4 0.0 collective-permute-start.7
  18.4 0.0 collective-permute-start.5
  18.4 2.8 %collective-permute-start.6 = (bf16[128,512]{1,0:T(8,128)(2,1)S(1)}, bf16[128,512]{1,0:T(8,128)(2,1)S(1)}, u32[]{:S(2)}, u32[]{:S(2)}) collective-permute-start(bf16[128,512]{1,0:T(8,128)(2,1)S(1)} %get-tuple-element.71), channel_id=1, source_target_pairs={{1,2},{2,1},{3,4},{4,3},{5,6},{6,5},{7,0},{0,7},{9,10},{10,9},{11,... | collective-permute-start | bytes 393224 | tf_op jit(solution)/shard_map/ppermute | solution.py:341
  21.3 0.0 collective-permute-done.7.refs_2_
  21.3 1.4 %collective-permute-start.8 = (bf16[128,512]{1,0:T(8,128)(2,1)S(1)}, bf16[128,512]{1,0:T(8,128)(2,1)S(1)}, u32[]{:S(2)}, u32[]{:S(2)}) collective-permute-start(bf16[128,512]{1,0:T(8,128)(2,1)S(1)} %add_convert_fusion), channel_id=1, source_target_pairs={{0,16},{8,24},{16,0},{24,8},{1,17},{9,25},{17,1},{25,9},{2,18},{10... | collective-permute-start | bytes 393224 | tf_op jit(solution)/shard_map/ppermute | solution.py:278
  22.7 2.2 %shard_map.107 = (bf16[128,512]{1,0:T(8,128)(2,1)}, f32[128,512]{1,0:T(8,128)S(1)}) custom-call(f32[4,512,256]{2,1,0:T(8,128)S(1)} %get-tuple-element.54.refs_0_, f32[4,1,256]{2,1,0:T(1,128)S(1)} %get-tuple-element.55.refs_1_, f32[8,128]{1,0:T(8,128)S(1)} %get-tuple-element.56.refs_2_, bf16[128,512]{1,0:T(8,128)(2,1)S(1)} %get-tuple-element.57.refs_3_, ...), custom_call_target="tpu_custom_call" | custom-call | flops 469762048 | bytes 4194304 | tf_op jit(solution)/shard_map/pallas_call | solution.py:258
  24.9 0.1 collective-permute-done.5.refs_0_
  24.9 2.2 %collective-permute-done.6.refs_1_ = bf16[128,512]{1,0:T(8,128)(2,1)S(1)} collective-permute-done((bf16[128,512]{1,0:T(8,128)(2,1)S(1)}, bf16[128,512]{1,0:T(8,128)(2,1)S(1)}, u32[]{:S(2)}, u32[]{:S(2)}) %collective-permute-start.6) | collective-permute-done | bytes 131104 | tf_op jit(solution)/shard_map/ppermute | solution.py:341
  27.1 0.0 collective-permute-done.8.refs_3_
  27.1 0.9 %shard_map.108 = bf16[128,512]{1,0:T(8,128)(2,1)} custom-call(f32[128,512]{1,0:T(8,128)S(1)} %get-tuple-element.66.unit_ref, f32[128,1]{1,0:T(8,128)S(1)} %get-tuple-element.67.inv_ref, f32[128,512]{1,0:T(8,128)S(1)} %get-tuple-element.68.gres_ref, f32[128,512]{1,0:T(8,128)S(1)} %get-tuple-element.69.acc_ref, ...), custom_call_target="tpu_custom_call" | custom-call | bytes 4194304 | tf_op jit(solution)/shard_map/pallas_call | solution.py:258
  (4 shorter events, 0.0 us)
Async XLA Ops:
  0.6 11.4 %copy-start = (bf16[1024,512]{1,0:T(8,128)(2,1)S(1)}, bf16[1024,512]{1,0:T(8,128)(2,1)}, u32[]{:S(2)}) copy-start(bf16[1024,512]{1,0:T(8,128)(2,1)} %refs_15_.1) | copy-start | bytes 3145732
  0.6 11.4 %copy-start.1 = (bf16[512,512]{1,0:T(8,128)(2,1)S(1)}, bf16[512,512]{1,0:T(8,128)(2,1)}, u32[]{:S(2)}) copy-start(bf16[512,512]{1,0:T(8,128)(2,1)} %refs_13_.1) | copy-start | bytes 1572868
  0.7 11.3 %collective-permute-start.4 = (bf16[128,512]{1,0:T(8,128)(2,1)}, bf16[128,512]{1,0:T(8,128)(2,1)S(1)}, u32[]{:S(2)}, u32[]{:S(2)}) collective-permute-start(bf16[128,512]{1,0:T(8,128)(2,1)} %refs_0_.2), channel_id=1, source_target_pairs={{0,1},{1,0},{2,3},{3,2},{4,5},{5,4},{6,7},{7,6},{8,9},{9,8},{10,11... | collective-permute-start | bytes 393224 | tf_op jit(solution)/shard_map/ppermute | solution.py:288
  3.7 9.4 %collective-permute-start.1 = (bf16[128,512]{1,0:T(8,128)(2,1)}, bf16[128,512]{1,0:T(8,128)(2,1)S(1)}, u32[]{:S(2)}, u32[]{:S(2)}) collective-permute-start(bf16[128,512]{1,0:T(8,128)(2,1)} %refs_0_.2), channel_id=1, source_target_pairs={{0,16},{8,24},{16,0},{24,8},{1,17},{9,25},{17,1},{25,9},{2,18},{10... | collective-permute-start | bytes 393224 | tf_op jit(solution)/shard_map/ppermute | solution.py:278
  5.2 7.9 %collective-permute-start = (bf16[128,512]{1,0:T(8,128)(2,1)}, bf16[128,512]{1,0:T(8,128)(2,1)S(1)}, u32[]{:S(2)}, u32[]{:S(2)}) collective-permute-start(bf16[128,512]{1,0:T(8,128)(2,1)} %refs_0_.2), channel_id=1, source_target_pairs={{1,2},{2,1},{3,4},{4,3},{5,6},{6,5},{7,0},{0,7},{9,10},{10,9},{11,... | collective-permute-start | bytes 393224 | tf_op jit(solution)/shard_map/ppermute | solution.py:289
  8.7 5.2 %collective-permute-start.2 = (bf16[128,512]{1,0:T(8,128)(2,1)}, bf16[128,512]{1,0:T(8,128)(2,1)S(1)}, u32[]{:S(2)}, u32[]{:S(2)}) collective-permute-start(bf16[128,512]{1,0:T(8,128)(2,1)} %refs_0_.2), channel_id=1, source_target_pairs={{0,24},{8,16},{16,8},{24,0},{1,25},{9,17},{17,9},{25,1},{2,26},{10... | collective-permute-start | bytes 393224 | tf_op jit(solution)/shard_map/ppermute | solution.py:278
  10.7 3.2 %collective-permute-start.3 = (bf16[128,512]{1,0:T(8,128)(2,1)S(1)}, bf16[128,512]{1,0:T(8,128)(2,1)S(1)}, u32[]{:S(2)}, u32[]{:S(2)}) collective-permute-start(bf16[128,512]{1,0:T(8,128)(2,1)S(1)} %get-tuple-element.38.refs_1_.refs_6_), channel_id=1, source_target_pairs={{0,8},{8,0},{16,24},{24,16},{1,9},{9,1},{17,25},{25,17},{2,10},{10... | collective-permute-start | bytes 393224 | tf_op jit(solution)/shard_map/ppermute | solution.py:278
  18.4 2.9 %collective-permute-start.7 = (bf16[256,512]{1,0:T(8,128)(2,1)S(1)}, bf16[256,512]{1,0:T(8,128)(2,1)S(1)}, u32[]{:S(2)}, u32[]{:S(2)}) collective-permute-start(bf16[256,512]{1,0:T(8,128)(2,1)S(1)} %get-tuple-element.72), channel_id=1, source_target_pairs={{0,8},{8,0},{16,24},{24,16},{1,9},{9,1},{17,25},{25,17},{2,10},{10... | collective-permute-start | bytes 786440 | tf_op jit(solution)/shard_map/ppermute | solution.py:278
  18.4 6.6 %collective-permute-start.5 = (bf16[128,512]{1,0:T(8,128)(2,1)S(1)}, bf16[128,512]{1,0:T(8,128)(2,1)S(1)}, u32[]{:S(2)}, u32[]{:S(2)}) collective-permute-start(bf16[128,512]{1,0:T(8,128)(2,1)S(1)} %get-tuple-element.70), channel_id=1, source_target_pairs={{0,1},{1,0},{2,3},{3,2},{4,5},{5,4},{6,7},{7,6},{8,9},{9,8},{10,11... | collective-permute-start | bytes 393224 | tf_op jit(solution)/shard_map/ppermute | solution.py:339
  18.4 8.7 %collective-permute-start.6 = (bf16[128,512]{1,0:T(8,128)(2,1)S(1)}, bf16[128,512]{1,0:T(8,128)(2,1)S(1)}, u32[]{:S(2)}, u32[]{:S(2)}) collective-permute-start(bf16[128,512]{1,0:T(8,128)(2,1)S(1)} %get-tuple-element.71), channel_id=1, source_target_pairs={{1,2},{2,1},{3,4},{4,3},{5,6},{6,5},{7,0},{0,7},{9,10},{10,9},{11,... | collective-permute-start | bytes 393224 | tf_op jit(solution)/shard_map/ppermute | solution.py:341
  21.3 5.8 %collective-permute-start.8 = (bf16[128,512]{1,0:T(8,128)(2,1)S(1)}, bf16[128,512]{1,0:T(8,128)(2,1)S(1)}, u32[]{:S(2)}, u32[]{:S(2)}) collective-permute-start(bf16[128,512]{1,0:T(8,128)(2,1)S(1)} %add_convert_fusion), channel_id=1, source_target_pairs={{0,16},{8,24},{16,0},{24,8},{1,17},{9,25},{17,1},{25,9},{2,18},{10... | collective-permute-start | bytes 393224 | tf_op jit(solution)/shard_map/ppermute | solution.py:278

commit v8 on v7

--- a/solution.py
+++ b/solution.py
@@ -191,7 +191,7 @@
     low = (prod - high.astype(f32)).astype(bf16)
     head_of = lax.broadcasted_iota(jnp.int32, (H, width), 1) // HEAD
     ones = (head_of == lax.broadcasted_iota(jnp.int32, (H, width), 0)).astype(bf16)
-    delta = dot_t(ones, high) + dot_t(ones, low)
+    delta = dot_t(jnp.concatenate([ones, ones], 1), jnp.concatenate([high, low], 1))
     delta_ref[...] = delta
 
     for j, cols in pair_columns():
@@ -209,7 +209,7 @@
     picked = [experts_ref[:, e : e + 1] ^ place for e in range(listed)]
 
     def far(slot):
-        total = jnp.zeros((rows, width), f32)
+        total = 0.0
         for e in range(listed):
             total = total + jnp.where(picked[e] == slot, parts[(2 + e) * rows : (3 + e) * rows], 0.0)
         return total

time: 28.2 us -> 28.2 us (level)
  no operation moved by 1% of the time
where the time goes in v8:
time: 28.2 us; the launch traced here: 28 us
  starting transfers between devices  13 us (46%)
  Pallas kernels  10.5 us (37%)
  waiting for transfers between devices  3.09 us (11%)
  between operations  1.38 us (5%)
    pallas_call x5, Pallas kernels, call(): pl.pallas_call(kernel, out_shape=[jax.ShapeDtypeStruct(shape, dtype) for...  10.5 us
    ppermute x5, starting transfers between devices, exchanged(): return lax.ppermute(array, 'blk', [(i, i ^ slot) for i in range(groups)])  3.55 us
    ppermute x1, starting transfers between devices, on_device(): near_b = lax.ppermute(nodes, 'dom', pairs_b)  3.54 us
    ppermute x1, starting transfers between devices, on_device(): near_a = lax.ppermute(nodes, 'dom', pairs_a)  3.03 us
    ppermute x1, starting transfers between devices, on_device(): from_b = lax.ppermute(send_b, 'dom', pairs_b)  2.83 us
    ppermute x1, waiting for transfers between devices, on_device(): from_b = lax.ppermute(send_b, 'dom', pairs_b)  2.16 us
    ppermute x5, waiting for transfers between devices, exchanged(): return lax.ppermute(array, 'blk', [(i, i ^ slot) for i in range(groups)])  0.85 us
  transfers between devices with their start and end apart: 9, of which 3 were waited for; matrix products, arithmetic and copies ran while one was open for 0% of the time, Pallas kernels for 18%

profile of v8, /device:TPU:0, one launch (start us, length us, event | category | flops | bytes accessed | tf_op | source)
XLA Modules:
  0.0 28.0 jit_solution(1567798595802482365)
XLA Ops:
  0.6 0.0 copy-start
  0.7 3.0 %collective-permute-start.4 = (bf16[128,512]{1,0:T(8,128)(2,1)}, bf16[128,512]{1,0:T(8,128)(2,1)S(1)}, u32[]{:S(2)}, u32[]{:S(2)}) collective-permute-start(bf16[128,512]{1,0:T(8,128)(2,1)} %refs_0_.2), channel_id=1, source_target_pairs={{0,1},{1,0},{2,3},{3,2},{4,5},{5,4},{6,7},{7,6},{8,9},{9,8},{10,11... | collective-permute-start | bytes 393224 | tf_op jit(solution)/shard_map/ppermute | solution.py:288
  3.7 1.5 %collective-permute-start.1 = (bf16[128,512]{1,0:T(8,128)(2,1)}, bf16[128,512]{1,0:T(8,128)(2,1)S(1)}, u32[]{:S(2)}, u32[]{:S(2)}) collective-permute-start(bf16[128,512]{1,0:T(8,128)(2,1)} %refs_0_.2), channel_id=1, source_target_pairs={{0,16},{8,24},{16,0},{24,8},{1,17},{9,25},{17,1},{25,9},{2,18},{10... | collective-permute-start | bytes 393224 | tf_op jit(solution)/shard_map/ppermute | solution.py:278
  5.2 3.5 %collective-permute-start = (bf16[128,512]{1,0:T(8,128)(2,1)}, bf16[128,512]{1,0:T(8,128)(2,1)S(1)}, u32[]{:S(2)}, u32[]{:S(2)}) collective-permute-start(bf16[128,512]{1,0:T(8,128)(2,1)} %refs_0_.2), channel_id=1, source_target_pairs={{1,2},{2,1},{3,4},{4,3},{5,6},{6,5},{7,0},{0,7},{9,10},{10,9},{11,... | collective-permute-start | bytes 393224 | tf_op jit(solution)/shard_map/ppermute | solution.py:289
  8.7 0.0 collective-permute-start.2
  8.7 1.9 %shard_map.104 = (bf16[128,512]{1,0:T(8,128)(2,1)S(1)}, bf16[512,512]{1,0:T(8,128)(2,1)S(1)}, bf16[512,512]{1,0:T(8,128)(2,1)S(1)}, bf16[512,512]{1,0:T(8,128)(2...) custom-call(bf16[128,512]{1,0:T(8,128)(2,1)} %refs_0_.2, ...), custom_call_target="tpu_custom_call" | custom-call | flops 201326592 | bytes 4194304 | tf_op jit(solution)/shard_map/pallas_call | solution.py:258
  10.7 0.7 %collective-permute-start.3 = (bf16[128,512]{1,0:T(8,128)(2,1)S(1)}, bf16[128,512]{1,0:T(8,128)(2,1)S(1)}, u32[]{:S(2)}, u32[]{:S(2)}) collective-permute-start(bf16[128,512]{1,0:T(8,128)(2,1)S(1)} %get-tuple-element.38.refs_1_.refs_6_), channel_id=1, source_target_pairs={{0,8},{8,0},{16,24},{24,16},{1,9},{9,1},{17,25},{25,17},{2,10},{10... | collective-permute-start | bytes 393224 | tf_op jit(solution)/shard_map/ppermute | solution.py:278
  12.0 0.0 collective-permute-done.4.refs_0_
  12.0 1.0 %shard_map.105 = (bf16[256,512]{1,0:T(8,128)(2,1)S(1)}, bf16[256,512]{1,0:T(8,128)(2,1)S(1)}, f32[4,256,256]{2,1,0:T(8,128)S(1)}, f32[128,1024]{1,0:T(8,128)S(1)...) custom-call(bf16[128,512]{1,0:T(8,128)(2,1)S(1)} %collective-permute, ...), custom_call_target="tpu_custom_call" | custom-call | flops 335544320 | bytes 4194304 | tf_op jit(solution)/shard_map/pallas_call | solution.py:258
  13.0 0.0 collective-permute-done.1.refs_3_
  13.1 0.0 collective-permute-done.refs_2_
  13.1 0.8 %collective-permute-done.2.refs_4_ = bf16[128,512]{1,0:T(8,128)(2,1)S(1)} collective-permute-done((bf16[128,512]{1,0:T(8,128)(2,1)}, bf16[128,512]{1,0:T(8,128)(2,1)S(1)}, u32[]{:S(2)}, u32[]{:S(2)}) %collective-permute-start.2) | collective-permute-done | bytes 131104 | tf_op jit(solution)/shard_map/ppermute | solution.py:278
  13.9 0.0 collective-permute-done.3.refs_5_
  13.9 4.5 %shard_map.106 = (bf16[128,512]{1,0:T(8,128)(2,1)S(1)}, bf16[128,512]{1,0:T(8,128)(2,1)S(1)}, f32[128,512]{1,0:T(8,128)S(1)}, f32[4,512,256]{2,1,0:T(8,128)S(1)}...) custom-call(s32[1,1]{1,0:T(1,128)S(6)} %copy.11.refs_0_, ...), custom_call_target="tpu_custom_call" | custom-call | flops 1073741824 | bytes 4194304 | tf_op jit(solution)/shard_map/pallas_call | solution.py:258
  18.4 0.0 collective-permute-start.7
  18.4 0.0 collective-permute-start.5
  18.4 2.8 %collective-permute-start.6 = (bf16[128,512]{1,0:T(8,128)(2,1)S(1)}, bf16[128,512]{1,0:T(8,128)(2,1)S(1)}, u32[]{:S(2)}, u32[]{:S(2)}) collective-permute-start(bf16[128,512]{1,0:T(8,128)(2,1)S(1)} %get-tuple-element.71), channel_id=1, source_target_pairs={{1,2},{2,1},{3,4},{4,3},{5,6},{6,5},{7,0},{0,7},{9,10},{10,9},{11,... | collective-permute-start | bytes 393224 | tf_op jit(solution)/shard_map/ppermute | solution.py:341
  21.3 0.0 collective-permute-done.7.refs_2_
  21.3 1.4 %collective-permute-start.8 = (bf16[128,512]{1,0:T(8,128)(2,1)S(1)}, bf16[128,512]{1,0:T(8,128)(2,1)S(1)}, u32[]{:S(2)}, u32[]{:S(2)}) collective-permute-start(bf16[128,512]{1,0:T(8,128)(2,1)S(1)} %add_convert_fusion), channel_id=1, source_target_pairs={{0,16},{8,24},{16,0},{24,8},{1,17},{9,25},{17,1},{25,9},{2,18},{10... | collective-permute-start | bytes 393224 | tf_op jit(solution)/shard_map/ppermute | solution.py:278
  22.7 2.2 %shard_map.107 = (bf16[128,512]{1,0:T(8,128)(2,1)}, f32[128,512]{1,0:T(8,128)S(1)}) custom-call(f32[4,512,256]{2,1,0:T(8,128)S(1)} %get-tuple-element.54.refs_0_, f32[4,1,256]{2,1,0:T(1,128)S(1)} %get-tuple-element.55.refs_1_, f32[8,128]{1,0:T(8,128)S(1)} %get-tuple-element.56.refs_2_, bf16[128,512]{1,0:T(8,128)(2,1)S(1)} %get-tuple-element.57.refs_3_, ...), custom_call_target="tpu_custom_call" | custom-call | flops 469762048 | bytes 4194304 | tf_op jit(solution)/shard_map/pallas_call | solution.py:258
  24.9 0.1 collective-permute-done.5.refs_0_
  24.9 2.2 %collective-permute-done.6.refs_1_ = bf16[128,512]{1,0:T(8,128)(2,1)S(1)} collective-permute-done((bf16[128,512]{1,0:T(8,128)(2,1)S(1)}, bf16[128,512]{1,0:T(8,128)(2,1)S(1)}, u32[]{:S(2)}, u32[]{:S(2)}) %collective-permute-start.6) | collective-permute-done | bytes 131104 | tf_op jit(solution)/shard_map/ppermute | solution.py:341
  27.1 0.0 collective-permute-done.8.refs_3_
  27.1 0.9 %shard_map.108 = bf16[128,512]{1,0:T(8,128)(2,1)} custom-call(f32[128,512]{1,0:T(8,128)S(1)} %get-tuple-element.66.unit_ref, f32[128,1]{1,0:T(8,128)S(1)} %get-tuple-element.67.inv_ref, f32[128,512]{1,0:T(8,128)S(1)} %get-tuple-element.68.gres_ref, f32[128,512]{1,0:T(8,128)S(1)} %get-tuple-element.69.acc_ref, ...), custom_call_target="tpu_custom_call" | custom-call | bytes 4194304 | tf_op jit(solution)/shard_map/pallas_call | solution.py:258
  (4 shorter events, 0.0 us)
Async XLA Ops:
  0.6 11.4 %copy-start = (bf16[1024,512]{1,0:T(8,128)(2,1)S(1)}, bf16[1024,512]{1,0:T(8,128)(2,1)}, u32[]{:S(2)}) copy-start(bf16[1024,512]{1,0:T(8,128)(2,1)} %refs_15_.1) | copy-start | bytes 3145732
  0.6 11.4 %copy-start.1 = (bf16[512,512]{1,0:T(8,128)(2,1)S(1)}, bf16[512,512]{1,0:T(8,128)(2,1)}, u32[]{:S(2)}) copy-start(bf16[512,512]{1,0:T(8,128)(2,1)} %refs_13_.1) | copy-start | bytes 1572868
  0.7 11.3 %collective-permute-start.4 = (bf16[128,512]{1,0:T(8,128)(2,1)}, bf16[128,512]{1,0:T(8,128)(2,1)S(1)}, u32[]{:S(2)}, u32[]{:S(2)}) collective-permute-start(bf16[128,512]{1,0:T(8,128)(2,1)} %refs_0_.2), channel_id=1, source_target_pairs={{0,1},{1,0},{2,3},{3,2},{4,5},{5,4},{6,7},{7,6},{8,9},{9,8},{10,11... | collective-permute-start | bytes 393224 | tf_op jit(solution)/shard_map/ppermute | solution.py:288
  3.7 9.4 %collective-permute-start.1 = (bf16[128,512]{1,0:T(8,128)(2,1)}, bf16[128,512]{1,0:T(8,128)(2,1)S(1)}, u32[]{:S(2)}, u32[]{:S(2)}) collective-permute-start(bf16[128,512]{1,0:T(8,128)(2,1)} %refs_0_.2), channel_id=1, source_target_pairs={{0,16},{8,24},{16,0},{24,8},{1,17},{9,25},{17,1},{25,9},{2,18},{10... | collective-permute-start | bytes 393224 | tf_op jit(solution)/shard_map/ppermute | solution.py:278
  5.2 7.9 %collective-permute-start = (bf16[128,512]{1,0:T(8,128)(2,1)}, bf16[128,512]{1,0:T(8,128)(2,1)S(1)}, u32[]{:S(2)}, u32[]{:S(2)}) collective-permute-start(bf16[128,512]{1,0:T(8,128)(2,1)} %refs_0_.2), channel_id=1, source_target_pairs={{1,2},{2,1},{3,4},{4,3},{5,6},{6,5},{7,0},{0,7},{9,10},{10,9},{11,... | collective-permute-start | bytes 393224 | tf_op jit(solution)/shard_map/ppermute | solution.py:289
  8.7 5.2 %collective-permute-start.2 = (bf16[128,512]{1,0:T(8,128)(2,1)}, bf16[128,512]{1,0:T(8,128)(2,1)S(1)}, u32[]{:S(2)}, u32[]{:S(2)}) collective-permute-start(bf16[128,512]{1,0:T(8,128)(2,1)} %refs_0_.2), channel_id=1, source_target_pairs={{0,24},{8,16},{16,8},{24,0},{1,25},{9,17},{17,9},{25,1},{2,26},{10... | collective-permute-start | bytes 393224 | tf_op jit(solution)/shard_map/ppermute | solution.py:278
  10.7 3.2 %collective-permute-start.3 = (bf16[128,512]{1,0:T(8,128)(2,1)S(1)}, bf16[128,512]{1,0:T(8,128)(2,1)S(1)}, u32[]{:S(2)}, u32[]{:S(2)}) collective-permute-start(bf16[128,512]{1,0:T(8,128)(2,1)S(1)} %get-tuple-element.38.refs_1_.refs_6_), channel_id=1, source_target_pairs={{0,8},{8,0},{16,24},{24,16},{1,9},{9,1},{17,25},{25,17},{2,10},{10... | collective-permute-start | bytes 393224 | tf_op jit(solution)/shard_map/ppermute | solution.py:278
  18.4 2.9 %collective-permute-start.7 = (bf16[256,512]{1,0:T(8,128)(2,1)S(1)}, bf16[256,512]{1,0:T(8,128)(2,1)S(1)}, u32[]{:S(2)}, u32[]{:S(2)}) collective-permute-start(bf16[256,512]{1,0:T(8,128)(2,1)S(1)} %get-tuple-element.72), channel_id=1, source_target_pairs={{0,8},{8,0},{16,24},{24,16},{1,9},{9,1},{17,25},{25,17},{2,10},{10... | collective-permute-start | bytes 786440 | tf_op jit(solution)/shard_map/ppermute | solution.py:278
  18.4 6.6 %collective-permute-start.5 = (bf16[128,512]{1,0:T(8,128)(2,1)S(1)}, bf16[128,512]{1,0:T(8,128)(2,1)S(1)}, u32[]{:S(2)}, u32[]{:S(2)}) collective-permute-start(bf16[128,512]{1,0:T(8,128)(2,1)S(1)} %get-tuple-element.70), channel_id=1, source_target_pairs={{0,1},{1,0},{2,3},{3,2},{4,5},{5,4},{6,7},{7,6},{8,9},{9,8},{10,11... | collective-permute-start | bytes 393224 | tf_op jit(solution)/shard_map/ppermute | solution.py:339
  18.4 8.7 %collective-permute-start.6 = (bf16[128,512]{1,0:T(8,128)(2,1)S(1)}, bf16[128,512]{1,0:T(8,128)(2,1)S(1)}, u32[]{:S(2)}, u32[]{:S(2)}) collective-permute-start(bf16[128,512]{1,0:T(8,128)(2,1)S(1)} %get-tuple-element.71), channel_id=1, source_target_pairs={{1,2},{2,1},{3,4},{4,3},{5,6},{6,5},{7,0},{0,7},{9,10},{10,9},{11,... | collective-permute-start | bytes 393224 | tf_op jit(solution)/shard_map/ppermute | solution.py:341
  21.3 5.8 %collective-permute-start.8 = (bf16[128,512]{1,0:T(8,128)(2,1)S(1)}, bf16[128,512]{1,0:T(8,128)(2,1)S(1)}, u32[]{:S(2)}, u32[]{:S(2)}) collective-permute-start(bf16[128,512]{1,0:T(8,128)(2,1)S(1)} %add_convert_fusion), channel_id=1, source_target_pairs={{0,16},{8,24},{16,0},{24,8},{1,17},{9,25},{17,1},{25,9},{2,18},{10... | collective-permute-start | bytes 393224 | tf_op jit(solution)/shard_map/ppermute | solution.py:278
